TPU v7x, 128 devices: a whole 4x4x4 slice. The times are simulated.
128 devices in a mesh: group: 8 (over y, x_lo), replica: 16 (over x_hi, z, core).
Axes of the slice: x: 4 (x_hi: 2, x_lo: 2; x = x_hi * 2 + x_lo), y: 4, z: 4, core: 2. Of those that a mesh axis runs over, the one named last changes fastest.
Arguments:
- hidden_in: bfloat16 [16, 1024, 896], P('replica', 'group'), may hold values from -6 to 6
- segment_ids: int32 [16, 1024], P('replica'), may hold values from 0 to 2, as said below
- attn_gain: bfloat16 [1, 896], P(None, 'group'), may hold values from 0.5 to 1.5
- w_query: bfloat16 [1, 896, 896], P(None, 'group'), may hold values from -0.1875 to 0.1875
- b_query: bfloat16 [1, 896], P(None, 'group'), may hold values from -3 to 3
- w_key: bfloat16 [1, 896, 128], P(None, 'group'), may hold values from -0.1875 to 0.1875
- b_key: bfloat16 [1, 128], P(None, 'group'), may hold values from -3 to 3
- w_value: bfloat16 [1, 896, 128], P(None, 'group'), may hold values from -0.1875 to 0.1875
- b_value: bfloat16 [1, 128], P(None, 'group'), may hold values from -3 to 3
- w_out: bfloat16 [1, 896, 896], P(None, 'group'), may hold values from -1.5 to 1.5
- ffn_gain: bfloat16 [1, 896], P(None, 'group'), may hold values from 0.5 to 1.5
- w_gate: bfloat16 [1, 896, 4864], P(None, 'group'), may hold values from -0.1875 to 0.1875
- w_up: bfloat16 [1, 896, 4864], P(None, 'group'), may hold values from -0.1875 to 0.1875
- w_down: bfloat16 [1, 4864, 896], P(None, 'group'), may hold values from -0.078125 to 0.078125
- cotangent: bfloat16 [16, 1024, 896], P('replica', 'group'), may hold values from -6 to 6
Outputs:
- hidden_out: bfloat16 [16, 1024, 896], P('replica', 'group')
- grad_in: float32 [16, 1024, 896], P('replica', 'group')
- grad_attn_gain: float32 [1, 896], P(None, 'group')
- grad_w_query: float32 [1, 896, 896], P(None, 'group')
- grad_b_query: float32 [1, 896], P(None, 'group')
- grad_w_key: float32 [1, 896, 128], P(None, 'group')
- grad_b_key: float32 [1, 128], P(None, 'group')
- grad_w_value: float32 [1, 896, 128], P(None, 'group')
- grad_b_value: float32 [1, 128], P(None, 'group')
- grad_w_out: float32 [1, 896, 896], P(None, 'group')
- grad_ffn_gain: float32 [1, 896], P(None, 'group')
- grad_w_gate: float32 [1, 896, 4864], P(None, 'group')
- grad_w_up: float32 [1, 896, 4864], P(None, 'group')
- grad_w_down: float32 [1, 4864, 896], P(None, 'group')
Inputs may be any that keep to these rules, and one draw needn't show every extreme that they name: `segment_ids`: each sequence's ids start at 0, never fall and rise by one at each document boundary; a sequence holds one to three documents, each of 204 tokens or more.
All inputs are finite; a program needn't handle non-finite values.
Results may differ from a plain program's by a relative error of at most 0.035.
Values may be sent and summed in bfloat16 or wider, within the bound.
No kernel may reach another device: no remote copies, remote signals or barrier semaphores. Data moves between devices by JAX's collectives and lax.ppermute only.
A program may use at most 128 MiB of HBM per device.

v0:
```python
import jax
import jax.numpy as jnp
from jax import lax
from jax.sharding import PartitionSpec as P

KV_HEADS = 2
HEAD_DIM = 64


EPS = 1e-06
THETA = 1000000.0
MASKED_SCORE = -1e30


def joined_along(blocks, dim):
    blocks = jnp.moveaxis(blocks, 0, dim)
    dims = blocks.shape
    return blocks.reshape(*dims[:dim], dims[dim] * dims[dim + 1], *dims[dim + 2 :])


def sent_to_all(array, axis):
    copies = jnp.broadcast_to(array, (lax.axis_size(axis), *array.shape))
    return lax.all_to_all(copies, axis, split_axis=0, concat_axis=0, tiled=True)


def gather_directly(array, axis, dim):
    return joined_along(sent_to_all(array, axis), dim)


def split_up(array, dim, devices):
    dims = array.shape
    blocks = array.reshape(*dims[:dim], devices, dims[dim] // devices, *dims[dim + 1 :])
    return jnp.moveaxis(blocks, dim, 0)


def summed_on_arrival(array, axis, dim):
    blocks = split_up(array, dim, lax.axis_size(axis))
    arrived = lax.all_to_all(blocks, axis, split_axis=0, concat_axis=0, tiled=True)
    return arrived.sum(axis=0)


def side_by_side(arrays, axis, dim, along):
    columns = [a.reshape(*a.shape[:along], -1) for a in arrays]
    both = jnp.concatenate(columns, axis=along)
    filled, at, gathered = (lax.all_gather(both, axis, axis=dim, tiled=True), 0, [])
    for a, column in zip(arrays, columns):
        section = filled[..., at : at + column.shape[along]]
        gathered.append(section.reshape(*section.shape[:along], *a.shape[along:]))
        at += column.shape[along]
    return tuple(gathered)


def sent_together(arrays, axis, dim, along):
    widths = [a.shape[along] for a in arrays]
    both = jnp.concatenate(arrays, axis=along)
    filled = lax.all_gather(both, axis, axis=dim, tiled=True)
    return tuple(jnp.split(filled, [sum(widths[:k]) for k in range(1, len(widths))], axis=along))


def sum_at_owner(array, axis, dim):
    devices = lax.axis_size(axis)
    blocks = lax.all_to_all(split_up(array, dim, devices), axis, 0, 0, tiled=True)
    return jnp.sum(blocks.astype(jnp.float32), axis=0)


def side_by_side_2(arrays, axis, dim, along):
    ends, at = ([], 0)
    for a in arrays[:-1]:
        at += a.shape[along]
        ends.append(at)
    both = jnp.concatenate(arrays, axis=along)
    return tuple(jnp.split(sum_at_owner(both, axis, dim), ends, axis=along))


def turn_half(values_in):
    half_size = values_in.shape[-1] // 2
    return jnp.concatenate([-values_in[..., half_size:], values_in[..., :half_size]], axis=-1)


def rotate(values_in, cosine_table, sine_table):
    return values_in * cosine_table + turn_half(values_in) * sine_table


def rotate_back(gradient, cosine_table, sine_table):
    return gradient * cosine_table - turn_half(gradient * sine_table)


def norm_forward(stream, gain_vector):
    scale = lax.rsqrt(jnp.mean(stream * stream, axis=-1, keepdims=True) + EPS)
    return (stream * scale * gain_vector.astype(jnp.float32), scale)


def norm_backward(stream, scale, gain_vector, gradient):
    normalized = stream * scale
    scaled = gradient * gain_vector.astype(jnp.float32)
    gain_grad = jnp.sum(gradient * normalized, axis=0)
    input_grad = scale * (
        scaled - normalized * jnp.mean(scaled * normalized, axis=-1, keepdims=True)
    )
    return (input_grad, gain_grad)


def project(left_side, right_side):
    return jnp.dot(left_side, right_side, preferred_element_type=jnp.float32)


def project_back(gradient, weight):
    return lax.dot_general(
        gradient, weight, (((1,), (1,)), ((), ())), preferred_element_type=jnp.float32
    )


def outer_sum(inputs, gradient):
    return lax.dot_general(
        inputs, gradient, (((0,), (0,)), ((), ())), preferred_element_type=jnp.float32
    )


def own_columns(gradient, width, group_index):
    return lax.dynamic_slice_in_dim(
        jnp.sum(gradient.astype(jnp.float32), axis=0), group_index * width, width, 0
    )


def gather_rows(values_in):
    return gather_directly(values_in, "group", 0)


def sum_rows(terms):
    return summed_on_arrival(terms, "group", 0)


def score_block(queries, keys_in, allowed, key_heads, head_size):
    query_rows = queries.shape[0]
    ratio = queries.shape[1] // (key_heads * head_size)
    query_split = queries.reshape(query_rows, key_heads, ratio, head_size)
    key_split = keys_in.reshape(keys_in.shape[0], key_heads, head_size)
    raw_scores = jnp.einsum(
        "qcgd,kcd->cgqk", query_split, key_split, preferred_element_type=jnp.float32
    )
    scores = jnp.where(allowed[None, None], raw_scores * head_size ** (-0.5), MASKED_SCORE)
    return (scores, query_split, key_split)


def local(
    hidden_in,
    segment_ids,
    attn_gain,
    w_query,
    b_query,
    w_key,
    b_key,
    w_value,
    b_value,
    w_out,
    ffn_gain,
    w_gate,
    w_up,
    w_down,
    cotangent,
):
    seq_count, span_rows, model_width = hidden_in.shape
    layer_count = w_query.shape[0]
    head_size = HEAD_DIM
    key_heads = KV_HEADS
    token_rows = seq_count * span_rows
    group_index = lax.axis_index("group")
    own_segments = lax.dynamic_slice_in_dim(segment_ids, group_index * span_rows, span_rows, 1)
    seq_length = segment_ids.shape[1]
    query_index = group_index * span_rows + jnp.arange(span_rows, dtype=jnp.int32)
    key_index = jnp.arange(seq_length, dtype=jnp.int32)
    earlier = jnp.sum(
        (segment_ids[:, None, :] < own_segments[:, :, None]).astype(jnp.int32), axis=-1
    )
    positions = query_index[None, :] - earlier
    allowed = (key_index[None, None, :] <= query_index[None, :, None]) & (
        segment_ids[:, None, :] == own_segments[:, :, None]
    )
    half_size = head_size // 2
    frequency = THETA ** (-(2.0 * jnp.arange(half_size, dtype=jnp.float32)) / head_size)
    angles = positions.reshape(token_rows).astype(jnp.float32)[:, None] * frequency
    cosine_table = jnp.concatenate([jnp.cos(angles), jnp.cos(angles)], axis=-1)[:, None, :]
    sine_table = jnp.concatenate([jnp.sin(angles), jnp.sin(angles)], axis=-1)[:, None, :]

    def fetch_weights(layer_index):
        attention = (
            *side_by_side(
                (
                    attn_gain[layer_index],
                    w_query[layer_index],
                    b_query[layer_index],
                    w_key[layer_index],
                ),
                "group",
                0,
                1,
            ),
            lax.all_gather(b_key[layer_index], "group", axis=0, tiled=True),
            lax.all_gather(w_value[layer_index], "group", axis=0, tiled=True),
            lax.all_gather(b_value[layer_index], "group", axis=0, tiled=True),
            *side_by_side((w_out[layer_index], ffn_gain[layer_index]), "group", 0, 1),
        )
        gate_part, up_part = (
            lax.all_to_all(w_gate[layer_index], "group", split_axis=1, concat_axis=0, tiled=True),
            lax.all_to_all(w_up[layer_index], "group", split_axis=1, concat_axis=0, tiled=True),
        )
        return tuple(attention) + (gate_part, up_part, w_down[layer_index])

    def attend_forward(packed):
        block_queries, block_keys, block_values, block_allowed = packed
        scores, query_split, key_split = score_block(
            block_queries, block_keys, block_allowed, key_heads, head_size
        )
        maximum = jnp.max(scores, axis=-1, keepdims=True)
        weights = jnp.exp(scores - maximum)
        totals = jnp.sum(weights, axis=-1, keepdims=True)
        probs = (weights / totals).astype(jnp.bfloat16)
        value_split = block_values.reshape(block_values.shape[0], key_heads, head_size)
        mixed = jnp.einsum("cgqk,kcd->qcgd", probs, value_split, preferred_element_type=jnp.float32)
        return (
            mixed.reshape(block_queries.shape[0], -1).astype(jnp.bfloat16),
            (maximum + jnp.log(totals))[..., 0],
        )

    def attend_backward(packed):
        block_queries, block_keys, block_values, block_allowed, block_logsum, block_grad = packed
        scores, query_split, key_split = score_block(
            block_queries, block_keys, block_allowed, key_heads, head_size
        )
        probs = jnp.exp(scores - block_logsum[..., None])
        value_split = block_values.reshape(block_values.shape[0], key_heads, head_size)
        grad_split = block_grad.reshape(query_split.shape)
        grad_probs = jnp.einsum(
            "qcgd,kcd->cgqk", grad_split, value_split, preferred_element_type=jnp.float32
        )
        inner = jnp.sum(probs * grad_probs, axis=-1, keepdims=True)
        grad_scores = (probs * (grad_probs - inner) * head_size ** (-0.5)).astype(jnp.bfloat16)
        grad_queries = jnp.einsum(
            "cgqk,kcd->qcgd", grad_scores, key_split, preferred_element_type=jnp.float32
        )
        grad_keys = jnp.einsum(
            "cgqk,qcgd->kcd", grad_scores, query_split, preferred_element_type=jnp.float32
        )
        grad_values = jnp.einsum(
            "cgqk,qcgd->kcd",
            probs.astype(jnp.bfloat16),
            grad_split,
            preferred_element_type=jnp.float32,
        )
        return (
            grad_queries.reshape(block_queries.shape[0], -1),
            grad_keys.reshape(block_keys.shape[0], -1),
            grad_values.reshape(block_keys.shape[0], -1),
        )

    stream = hidden_in.astype(jnp.float32).reshape(token_rows, model_width)
    layer_index = 0
    gathered = fetch_weights(layer_index)
    (
        first_gain,
        query_weight,
        query_bias,
        key_weight,
        key_bias,
        value_weight,
        value_bias,
        out_weight,
        second_gain,
        gate_weight,
        up_weight,
        down_weight,
    ) = gathered
    normed, first_scale = norm_forward(stream, first_gain)
    normed = normed.astype(jnp.bfloat16)
    raw_query = project(normed, query_weight) + query_bias.astype(jnp.float32)
    raw_key = project(normed, key_weight) + key_bias.astype(jnp.float32)
    raw_value = project(normed, value_weight) + value_bias.astype(jnp.float32)
    queries = (
        rotate(raw_query.reshape(token_rows, -1, head_size), cosine_table, sine_table)
        .reshape(seq_count, span_rows, -1)
        .astype(jnp.bfloat16)
    )
    local_keys = (
        rotate(raw_key.reshape(token_rows, key_heads, head_size), cosine_table, sine_table)
        .reshape(seq_count, span_rows, -1)
        .astype(jnp.bfloat16)
    )
    local_values = raw_value.reshape(seq_count, span_rows, -1).astype(jnp.bfloat16)
    all_keys, all_values = sent_together((local_keys, local_values), "group", 1, 0)
    attended, logsum = lax.map(attend_forward, (queries, all_keys, all_values, allowed))
    attended = attended.reshape(token_rows, -1)
    middle = stream + project(attended, out_weight)
    second_normed, second_scale = norm_forward(middle, second_gain)
    second_normed = second_normed.astype(jnp.bfloat16)
    group_second = gather_rows(second_normed)
    gate_value = project(group_second, gate_weight)
    up_value = project(group_second, up_weight)
    hidden = (jax.nn.silu(gate_value) * up_value).astype(jnp.bfloat16)
    layer_out = middle + sum_rows(project(hidden, down_weight))
    stored = [
        (
            stream,
            first_scale,
            normed,
            queries,
            all_keys,
            all_values,
            logsum,
            attended,
            middle,
            second_scale,
            second_normed,
            group_second,
            gate_value,
            up_value,
            hidden,
        )
    ]
    hidden_out = layer_out.reshape(seq_count, span_rows, model_width).astype(jnp.bfloat16)
    stream_grad = cotangent.astype(jnp.float32).reshape(token_rows, model_width)
    collected = [None] * layer_count
    layer_index = 0
    (
        layer_in,
        first_scale,
        normed,
        queries,
        all_keys,
        all_values,
        logsum,
        attended,
        middle,
        second_scale,
        second_normed,
        group_second,
        gate_value,
        up_value,
        hidden,
    ) = stored[layer_index]
    gathered = fetch_weights(layer_index)
    (
        first_gain,
        query_weight,
        query_bias,
        key_weight,
        key_bias,
        value_weight,
        value_bias,
        out_weight,
        second_gain,
        gate_weight,
        up_weight,
        down_weight,
    ) = gathered
    down_grad = stream_grad.astype(jnp.bfloat16)
    group_down = gather_rows(down_grad)
    grad_hidden = project_back(group_down, down_weight)
    sigmoid_gate = jax.nn.sigmoid(gate_value)
    grad_gate = (
        grad_hidden * up_value * sigmoid_gate * (1.0 + gate_value * (1.0 - sigmoid_gate))
    ).astype(jnp.bfloat16)
    grad_up = (grad_hidden * gate_value * sigmoid_gate).astype(jnp.bfloat16)
    second_terms = project_back(grad_gate, gate_weight) + project_back(grad_up, up_weight)
    grad_second = sum_rows(second_terms)
    norm_term, grad_second_gain = norm_backward(middle, second_scale, second_gain, grad_second)
    grad_middle = stream_grad + norm_term
    attn_grad = grad_middle.astype(jnp.bfloat16)
    grad_attended = project_back(attn_grad, out_weight).astype(jnp.bfloat16)
    grad_queries, grad_keys, grad_values = lax.map(
        attend_backward,
        (
            queries,
            all_keys,
            all_values,
            allowed,
            logsum,
            grad_attended.reshape(seq_count, span_rows, -1),
        ),
    )
    own_keys, own_values = side_by_side_2(
        (grad_keys.astype(jnp.bfloat16), grad_values.astype(jnp.bfloat16)), "group", 1, 0
    )
    grad_query = (
        rotate_back(grad_queries.reshape(token_rows, -1, head_size), cosine_table, sine_table)
        .reshape(token_rows, -1)
        .astype(jnp.bfloat16)
    )
    grad_key = (
        rotate_back(own_keys.reshape(token_rows, key_heads, head_size), cosine_table, sine_table)
        .reshape(token_rows, -1)
        .astype(jnp.bfloat16)
    )
    grad_value = own_values.reshape(token_rows, -1).astype(jnp.bfloat16)
    grad_first = (
        project_back(grad_query, query_weight)
        + project_back(grad_key, key_weight)
        + project_back(grad_value, value_weight)
    )
    norm_term, grad_first_gain = norm_backward(layer_in, first_scale, first_gain, grad_first)
    stream_grad = grad_middle + norm_term
    own_normed = lax.all_to_all(normed, "group", split_axis=1, concat_axis=0, tiled=True)
    own_attended = lax.all_to_all(attended, "group", split_axis=1, concat_axis=0, tiled=True)
    group_query, group_key, group_value, group_attn = sent_together(
        (grad_query, grad_key, grad_value, attn_grad), "group", 0, 1
    )
    grad_gate_weight = lax.all_to_all(
        outer_sum(group_second, grad_gate).astype(jnp.bfloat16),
        "group",
        split_axis=0,
        concat_axis=1,
        tiled=True,
    )
    grad_up_weight = lax.all_to_all(
        outer_sum(group_second, grad_up).astype(jnp.bfloat16),
        "group",
        split_axis=0,
        concat_axis=1,
        tiled=True,
    )
    grad_down_weight = outer_sum(hidden, group_down)
    gain_first = summed_on_arrival(grad_first_gain, "group", 0)
    gain_second = summed_on_arrival(grad_second_gain, "group", 0)
    grad_query_weight = outer_sum(own_normed, group_query)
    grad_key_weight = outer_sum(own_normed, group_key)
    grad_value_weight = outer_sum(own_normed, group_value)
    grad_out_weight = outer_sum(own_attended, group_attn)
    grad_query_bias = own_columns(group_query, b_query.shape[1], group_index)
    grad_key_bias = own_columns(group_key, b_key.shape[1], group_index)
    grad_value_bias = own_columns(group_value, b_value.shape[1], group_index)
    shares = (
        lax.psum(gain_first.astype(jnp.bfloat16), "replica").astype(jnp.float32),
        lax.psum(grad_query_weight.astype(jnp.bfloat16), "replica").astype(jnp.float32),
        lax.psum(grad_query_bias.astype(jnp.bfloat16), "replica").astype(jnp.float32),
        lax.psum(grad_key_weight.astype(jnp.bfloat16), "replica").astype(jnp.float32),
        lax.psum(grad_key_bias.astype(jnp.bfloat16), "replica").astype(jnp.float32),
        lax.psum(grad_value_weight.astype(jnp.bfloat16), "replica").astype(jnp.float32),
        lax.psum(grad_value_bias.astype(jnp.bfloat16), "replica").astype(jnp.float32),
        lax.psum(grad_out_weight.astype(jnp.bfloat16), "replica").astype(jnp.float32),
        lax.psum(gain_second.astype(jnp.bfloat16), "replica").astype(jnp.float32),
        lax.psum(grad_gate_weight, "replica").astype(jnp.float32),
        lax.psum(grad_up_weight, "replica").astype(jnp.float32),
        lax.psum(grad_down_weight.astype(jnp.bfloat16), "replica").astype(jnp.float32),
    )
    collected[layer_index] = shares
    stacked = [jnp.stack([collected[0][member]]) for member in range(12)]
    return (
        hidden_out,
        stream_grad.reshape(seq_count, span_rows, model_width),
        stacked[0],
        stacked[1],
        stacked[2],
        stacked[3],
        stacked[4],
        stacked[5],
        stacked[6],
        stacked[7],
        stacked[8],
        stacked[9],
        stacked[10],
        stacked[11],
    )


def solution(mesh):
    placed = (
        P("replica", "group", None),
        P("replica", None),
        P(None, "group"),
        P(None, "group", None),
        P(None, "group"),
        P(None, "group", None),
        P(None, "group"),
        P(None, "group", None),
        P(None, "group"),
        P(None, "group", None),
        P(None, "group"),
        P(None, "group", None),
        P(None, "group", None),
        P(None, "group", None),
        P("replica", "group", None),
    )
    return jax.shard_map(
        local,
        mesh=mesh,
        in_specs=placed,
        out_specs=(
            P("replica", "group", None),
            P("replica", "group", None),
            P(None, "group"),
            P(None, "group", None),
            P(None, "group"),
            P(None, "group", None),
            P(None, "group"),
            P(None, "group", None),
            P(None, "group"),
            P(None, "group", None),
            P(None, "group"),
            P(None, "group", None),
            P(None, "group", None),
            P(None, "group", None),
        ),
        check_vma=False,
    )
```

profile of v0, /device:TPU:1, one launch (start us, length us, event | category | flops | bytes accessed | tf_op | source)
XLA Modules:
  0.0 656.4 jit_solution(17888126146509066957)
XLA Ops:
  8.2 1.6 pad_maximum_fusion.2
  11.4 1.9 concatenate.40
  13.3 2.1 all_to_all.118
  16.6 5.9 all-to-all-start.1
  24.3 35.2 %all-reduce.4 = (bf16[128]{0:T(256)(128)(2,1)S(1)}, bf16[128]{0:T(256)(128)(2,1)S(1)}) all-reduce(bf16[128]{0:T(256)(128)(2,1)S(1)} %dynamic-update-slice.1, bf16[128]{0:T(256)(128)(2,1)S(1)} %dynamic-update-slice), channel_id=4, replica_groups=mesh['group'=8,'replica'=16] {'group'}, use_global_device_ids=true, to_apply=%add.1 | all-reduce | flops 256 | bytes 1024
  60.7 3.3 all_to_all.122
  65.2 23.1 %all-gather.1 = bf16[1,896,128]{2,1,0:T(8,128)(2,1)S(1)} all-gather(bf16[1,112,128]{2,1,0:T(8,128)(2,1)S(1)} %copy-done.34), channel_id=3, replica_groups=mesh['group'=8,'replica'=16] {'group'}, dimensions={1}, use_global_device_ids=true | all-gather | bytes 258048 | tf_op jit(solution)/shard_map/all_gather | solution.py:199
  89.8 38.3 %all-gather.7.cloned.1.call-done = bf16[896,1026]{1,0:T(8,128)(2,1)} async-done(((bf16[112,1026]{1,0:T(8,128)(2,1)}), bf16[896,1026]{1,0:T(8,128)(2,1)}) %all-gather.7.cloned.1.call-update) | async-done | bytes 1838608 | tf_op jit(solution)/shard_map/all_gather | solution.py:45
  131.5 22.1 %all_gather.28 = bf16[2,1024,128]{1,2,0:T(8,128)(2,1)S(1)} all-gather(bf16[2,128,128]{1,2,0:T(8,128)(2,1)S(1)} %pad_maximum_fusion.3), channel_id=1, replica_groups=mesh['group'=8,'replica'=16] {'group'}, dimensions={1}, use_global_device_ids=true | all-gather | bytes 589824 | tf_op jit(solution)/shard_map/all_gather | solution.py:56
  158.3 2.9 copy-done.1
  162.2 3.6 all-to-all-start.2
  165.8 4.6 fusion.52
  171.1 6.2 all-to-all-done.2
  177.5 22.7 %all_to_all.161 = bf16[8,128,896]{2,1,0:T(8,128)(2,1)} all-to-all(bf16[8,128,896]{2,1,0:T(8,128)(2,1)S(1)} %broadcast_in_dim.83), channel_id=1, replica_groups=mesh['group'=8,'replica'=16] {'group'}, dimensions={0} | all-to-all | bytes 3670016 | tf_op jit(solution)/shard_map/all_to_all | solution.py:23
  201.7 4.5 all-to-all-start.4
  206.2 5.0 fusion.104
  211.1 3.0 fusion.105
  214.1 9.8 %all-to-all-done.4 = bf16[8,128,896]{2,1,0:T(8,128)(2,1)} async-done(((bf16[8,128,896]{2,1,0:T(8,128)(2,1)}), bf16[8,128,896]{2,1,0:T(8,128)(2,1)}, u32[]{:S(2)}, u32[]{:S(2)}) %all-to-all-start.4) | async-done | bytes 1835040 | tf_op jit(solution)/shard_map/all_to_all | solution.py:23
  224.0 6.4 multiply_convert_fusion
  230.3 3.9 fusion.106
  234.3 3.7 convolution_add_fusion
  238.0 4.7 all-to-all-start.5
  242.7 36.4 %all-to-all-done.5 = f32[8,128,896]{2,1,0:T(8,128)} async-done(((f32[8,128,896]{2,1,0:T(8,128)}), f32[8,128,896]{2,1,0:T(8,128)}, u32[]{:S(2)}, u32[]{:S(2)}) %all-to-all-start.5) | async-done | bytes 3670048 | tf_op jit(solution)/shard_map/all_to_all | solution.py:38
  279.2 2.3 reduce_sum.160
  283.9 4.2 fusion.107
  288.1 12.6 %fusion.12 = f32[2,64,7,128]{3,1,2,0:T(8,128)S(1)} fusion(bf16[1024,2,64,1]{0,2,3,1:T(8,128)(2,1)S(1)} %bitcast.279, f32[2,1024,128,7]{2,1,3,0:T(8,128)} %fusion.107, f32[2,7,128,1024]{2,3,1,0:T(8,128)} %copy-done.1, f32[2,7,128]{2,1,0:T(8,128)S(1)} %log_add_fusion), kind=kOutput, calls=%fused_computation.22 | convolution fusion | flops 247728896 | bytes 15408128 | tf_op jit(solution)/shard_map/while/body/eval_jaxpr/cgqk,kcd->qcgd/dot_general | solution.py:238
  300.7 12.6 %fusion.48 = bf16[2,64,1024]{2,1,0:T(8,128)(2,1)S(1)} fusion(bf16[128,2,7,64]{0,3,2,1:T(8,128)(2,1)S(1)} %bitcast.287, f32[2,1024,128,7]{2,1,3,0:T(8,128)} %fusion.107, f32[2,7,128,1024]{2,3,1,0:T(8,128)} %copy-done.1, f32[2,7,128]{2,1,0:T(8,128)S(1)} %log_add_fusion), kind=kOutput, calls=%fused_computation.50 | convolution fusion | flops 247859968 | bytes 15178752 | tf_op jit(solution)/shard_map/while/body/eval_jaxpr/cgqk,qcgd->kcd/dot_general | solution.py:241
  313.3 4.4 fusion.45
  319.5 7.2 %all-to-all-start.6 = ((bf16[8,2,128,128]{2,3,1,0:T(8,128)(2,1)}), bf16[8,2,128,128]{2,3,1,0:T(8,128)(2,1)S(1)}, u32[]{:S(2)}, u32[]{:S(2)}) async-start(bf16[8,2,128,128]{2,3,1,0:T(8,128)(2,1)} %maximum_bitcast_fusion), calls=%async_computation.6 | async-start | bytes 1048576 | tf_op jit(solution)/shard_map/all_to_all | solution.py:62
  328.8 2.0 copy.180
  330.7 2.0 copy.178
  334.7 1.8 pad_maximum_fusion
  336.8 4.8 all-to-all-start.9
  341.6 1.5 multiply_convert_fusion.3
  343.2 4.4 all-to-all-done.9
  348.3 4.0 all-to-all-start.8
  352.3 3.3 convolution_convert_fusion.1
  357.1 3.6 all-to-all-done.8
  360.7 3.8 all-to-all-start.11
  364.6 4.4 convolution_convert_fusion
  368.9 2.4 copy.194
  371.3 19.9 %all-to-all-done.11 = bf16[8,112,608]{2,1,0:T(8,128)(2,1)S(1)} async-done(((bf16[8,112,608]{2,1,0:T(8,128)(2,1)}), bf16[8,112,608]{2,1,0:T(8,128)(2,1)S(1)}, u32[]{:S(2)}, u32[]{:S(2)}) %all-to-all-start.11) | async-done | bytes 1089568 | tf_op jit(solution)/shard_map/all_to_all | solution.py:406
  391.1 4.2 all-to-all-start.12
  395.4 4.9 fusion.26
  400.3 21.6 %all-to-all-done.12 = bf16[8,112,608]{2,1,0:T(8,128)(2,1)} async-done(((bf16[8,112,608]{2,1,0:T(8,128)(2,1)}), bf16[8,112,608]{2,1,0:T(8,128)(2,1)}, u32[]{:S(2)}, u32[]{:S(2)}) %all-to-all-start.12) | async-done | bytes 1089568 | tf_op jit(solution)/shard_map/all_to_all | solution.py:413
  421.9 4.5 all-to-all-start.3
  426.5 4.3 fusion.25
  432.0 2.9 stack.90
  436.4 1.7 stack.92
  438.1 44.3 %all-gather.11.cloned.1.call-done = bf16[1024,2048]{1,0:T(8,128)(2,1)} async-done(((bf16[128,2048]{1,0:T(8,128)(2,1)}), bf16[1024,2048]{1,0:T(8,128)(2,1)}) %all-gather.11.cloned.1.call-update) | async-done | bytes 4194320 | tf_op jit(solution)/shard_map/all_gather | solution.py:56
  482.4 2.8 fusion.59
  485.2 2.8 fusion.62
  489.3 6.4 all-to-all-done.3
  495.8 3.3 all-to-all-start.10
  499.1 2.4 reduce_sum.159
  501.5 2.4 all-to-all-done.10
  506.1 3.2 multiply_reduce_fusion.1
  510.0 3.3 all-to-all-start.7
  513.4 2.1 add_bitcast_fusion
  515.5 3.1 all-to-all-done.7
  518.6 1.9 convert_reduce_fusion
  524.4 64.8 %all-reduce.2 = (bf16[1,112]{1,0:T(2,128)(2,1)S(1)}, bf16[1,112]{1,0:T(2,128)(2,1)S(1)}, bf16[1,112,128]{2,1,0:T(8,128)(2,1)S(1)}, bf16[1,16]{1,0:T(2,128)(2,1)S...) all-reduce(bf16[1,112]{1,0:T(2,128)(2,1)S(1)} %bitcast.300, ...), channel_id=1, replica_groups=mesh['group'=8,'replica'=16] {'replica'}, use_global_device_ids=true, to_apply=%region_13.14 | all-reduce | flops 29040 | bytes 116160 | tf_op jit(solution)/shard_map/psum | solution.py:431
  593.0 48.9 %all-reduce.7.cloned.1.call-done = (bf16[1,112,896]{2,1,0:T(8,128)(2,1)}, bf16[1,112,896]{2,1,0:T(8,128)(2,1)}, bf16[1,112,4864]{2,1,0:T(8,128)(2,1)}, bf16[1,112,4864]{2,1,0:T(8,128)(2,1)}, bf16[1,608,896]{2,1,0:T(8,128)(2,1)}) async-done(((bf16[1,112,896]{2,1,0:T(8,128)(2,1)}, bf16[1,112,896]{2,1,0:T(8,128)(2,1)}, bf16[1,112,4864]{2,1,0:T(8,128)(2,1)}, bf16[1,112,4864]{2,1,0:T(8,128)(2,1)}, ...) | async-done | bytes 3670032 | tf_op jit(solution)/shard_map/psum | solution.py:432
  641.9 2.8 stack.91
  (208 shorter events, 49.8 us)
Async XLA Ops:
  7.2 216.8 %copy-start = (bf16[1,608,896]{2,1,0:T(8,128)(2,1)S(1)}, bf16[1,608,896]{2,1,0:T(8,128)(2,1)}, u32[]{:S(2)}) copy-start(bf16[1,608,896]{2,1,0:T(8,128)(2,1)} %param.28) | copy-start | bytes 3268612
  7.2 6.1 copy-start.18
  7.2 81.5 %all-gather.9.cloned.1.call-start = ((), (), s32[]{:S(2)}) async-start(), calls=%async_computation.14 | async-start | bytes 2064384 | tf_op jit(solution)/shard_map/all_gather | solution.py:45
  9.8 118.3 %all-gather.7.cloned.1.call-start = ((), (), s32[]{:S(2)}) async-start(), calls=%async_computation.13 | async-start | bytes 2322432 | tf_op jit(solution)/shard_map/all_gather | solution.py:45
  15.4 7.1 %copy-start.46 = (u32[128]{0:T(128)S(1)}, u32[128]{0:T(128)}, u32[]{:S(2)}) copy-start(u32[128]{0:T(128)} %constant.96) | copy-start | bytes 1540
  15.4 8.4 %copy-start.44 = (bf16[1,16]{1,0:T(2,128)(2,1)S(1)}, bf16[1,16]{1,0:T(2,128)(2,1)}, u32[]{:S(2)}) copy-start(bf16[1,16]{1,0:T(2,128)(2,1)} %param.21) | copy-start | bytes 100
  15.4 8.6 %copy-start.45 = (bf16[1,16]{1,0:T(2,128)(2,1)S(1)}, bf16[1,16]{1,0:T(2,128)(2,1)}, u32[]{:S(2)}) copy-start(bf16[1,16]{1,0:T(2,128)(2,1)} %param.23) | copy-start | bytes 100
  15.4 44.6 %copy-start.36 = (s32[1,1024]{1,0:T(1,128)S(1)}, s32[1,1024]{1,0:T(1,128)}, u32[]{:S(2)}) copy-start(s32[1,1024]{1,0:T(1,128)} %param.16) | copy-start | bytes 12292
  16.6 145.6 %all-to-all-start.1 = ((bf16[112,8,608]{2,0,1:T(8,128)(2,1)}), bf16[112,8,608]{2,0,1:T(8,128)(2,1)}, u32[]{:S(2)}, u32[]{:S(2)}) async-start(bf16[112,8,608]{2,0,1:T(8,128)(2,1)} %copy.173), calls=%async_computation.1 | async-start | bytes 2293760 | tf_op jit(solution)/shard_map/all_to_all | solution.py:204
  60.7 94.9 %copy-start.3 = (f32[128,896]{1,0:T(8,128)}, f32[128,896]{1,0:T(8,128)S(1)}, u32[]{:S(2)}) copy-start(f32[128,896]{1,0:T(8,128)S(1)} %copy.167) | copy-start | bytes 1376260
  60.7 4.5 copy-start.34
  60.7 27.6 %copy-start.2 = (bf16[1,128,896]{2,1,0:T(8,128)(2,1)S(1)}, bf16[1,128,896]{2,1,0:T(8,128)(2,1)}, u32[]{:S(2)}) copy-start(bf16[1,128,896]{2,1,0:T(8,128)(2,1)} %param.15) | copy-start | bytes 688132
  64.0 67.1 %copy-start.47 = (f32[128]{0:T(128)S(1)}, f32[128]{0:T(128)}, u32[]{:S(2)}) copy-start(f32[128]{0:T(128)} %convert_element_type.313) | copy-start | bytes 1540
  88.3 65.3 %copy-start.25 = (bf16[1,896,128]{2,1,0:T(8,128)(2,1)}, bf16[1,896,128]{2,1,0:T(8,128)(2,1)S(1)}, u32[]{:S(2)}) copy-start(bf16[1,896,128]{2,1,0:T(8,128)(2,1)S(1)} %all-gather.1) | copy-start | bytes 688132
  88.5 65.1 %copy-start.39 = (f32[128]{0:T(128)}, f32[128]{0:T(128)S(1)}, u32[]{:S(2)}) copy-start(f32[128]{0:T(128)S(1)} %add_rsqrt_fusion.1) | copy-start | bytes 1540
  128.1 25.5 %copy-start.6 = (bf16[896,1026]{1,0:T(8,128)(2,1)S(1)}, bf16[896,1026]{1,0:T(8,128)(2,1)}, u32[]{:S(2)}) copy-start(bf16[896,1026]{1,0:T(8,128)(2,1)} %all-gather.7.cloned.1.call-done) | copy-start | bytes 5515780
  156.8 1.4 copy-start.19
  156.8 9.0 %copy-start.21 = (bf16[1,1024,128]{1,2,0:T(8,128)(2,1)}, bf16[1,1024,128]{1,2,0:T(8,128)(2,1)S(1)}, u32[]{:S(2)}) copy-start(bf16[1,1024,128]{1,2,0:T(8,128)(2,1)S(1)} %get-tuple-element.91) | copy-start | bytes 786436
  157.0 1.2 copy-start.29
  158.2 2.9 copy-start.1
  162.2 15.1 %all-to-all-start.2 = ((bf16[112,8,608]{2,0,1:T(8,128)(2,1)}), bf16[112,8,608]{2,0,1:T(8,128)(2,1)S(1)}, u32[]{:S(2)}, u32[]{:S(2)}) async-start(bf16[112,8,608]{2,0,1:T(8,128)(2,1)} %copy.174), calls=%async_computation.2 | async-start | bytes 2293760 | tf_op jit(solution)/shard_map/all_to_all | solution.py:205
  165.8 4.6 copy-start.13
  170.4 6.9 %copy-start.28 = (bf16[2,64,7,128]{3,1,2,0:T(8,128)(2,1)}, bf16[2,64,7,128]{3,1,2,0:T(8,128)(2,1)S(1)}, u32[]{:S(2)}) copy-start(bf16[2,64,7,128]{3,1,2,0:T(8,128)(2,1)S(1)} %fusion.52) | copy-start | bytes 688132
  171.0 111.3 %copy-start.37 = (f32[128]{0:T(128)}, f32[128]{0:T(128)S(1)}, u32[]{:S(2)}) copy-start(f32[128]{0:T(128)S(1)} %add_rsqrt_fusion) | copy-start | bytes 1540
  177.5 22.7 %copy-start.7 = (bf16[1,128,896]{2,1,0:T(8,128)(2,1)S(1)}, bf16[1,128,896]{2,1,0:T(8,128)(2,1)}, u32[]{:S(2)}) copy-start(bf16[1,128,896]{2,1,0:T(8,128)(2,1)} %param.29) | copy-start | bytes 688132
  201.7 22.3 %all-to-all-start.4 = ((bf16[8,128,896]{2,1,0:T(8,128)(2,1)}), bf16[8,128,896]{2,1,0:T(8,128)(2,1)}, u32[]{:S(2)}, u32[]{:S(2)}) async-start(bf16[8,128,896]{2,1,0:T(8,128)(2,1)} %broadcast_in_dim.84), calls=%async_computation.4 | async-start | bytes 3670016 | tf_op jit(solution)/shard_map/all_to_all | solution.py:23
  206.2 5.0 copy-start.12
  230.3 3.9 copy-start.48
  230.3 3.9 copy-start.5
  238.0 41.2 %all-to-all-start.5 = ((f32[8,128,896]{2,1,0:T(8,128)}), f32[8,128,896]{2,1,0:T(8,128)}, u32[]{:S(2)}, u32[]{:S(2)}) async-start(f32[8,128,896]{2,1,0:T(8,128)} %bitcast.258), calls=%async_computation.5 | async-start | bytes 7340032 | tf_op jit(solution)/shard_map/all_to_all | solution.py:38
  242.7 39.5 %copy-start.8 = (bf16[1,128,896]{2,1,0:T(8,128)(2,1)S(1)}, bf16[1,128,896]{2,1,0:T(8,128)(2,1)}, u32[]{:S(2)}) copy-start(bf16[1,128,896]{2,1,0:T(8,128)(2,1)} %param.29) | copy-start | bytes 688132
  281.4 1.7 copy-start.14
  282.2 1.7 copy-start.41
  282.2 1.7 copy-start.22
  282.4 0.7 copy-start.27
  283.9 4.2 copy-start.20
  288.1 12.6 %copy-start.30 = (bf16[128,896]{0,1:T(8,128)(2,1)S(1)}, bf16[128,896]{0,1:T(8,128)(2,1)}, u32[]{:S(2)}) copy-start(bf16[128,896]{0,1:T(8,128)(2,1)} %copy-done.29) | copy-start | bytes 688132
  300.7 17.0 %copy-start.15 = (f32[2,64,7,128]{3,1,2,0:T(8,128)}, f32[2,64,7,128]{3,1,2,0:T(8,128)S(1)}, u32[]{:S(2)}) copy-start(f32[2,64,7,128]{3,1,2,0:T(8,128)S(1)} %fusion.12) | copy-start | bytes 1376260
  319.5 14.8 %all-to-all-start.6 = ((bf16[8,2,128,128]{2,3,1,0:T(8,128)(2,1)}), bf16[8,2,128,128]{2,3,1,0:T(8,128)(2,1)S(1)}, u32[]{:S(2)}, u32[]{:S(2)}) async-start(bf16[8,2,128,128]{2,3,1,0:T(8,128)(2,1)} %maximum_bitcast_fusion), calls=%async_computation.6 | async-start | bytes 1048576 | tf_op jit(solution)/shard_map/all_to_all | solution.py:62
  326.8 6.0 copy-start.4
  326.8 155.7 %all-gather.11.cloned.1.call-start = ((), (), s32[]{:S(2)}) async-start(), calls=%async_computation.15 | async-start | bytes 4718592 | tf_op jit(solution)/shard_map/all_gather | solution.py:56
  334.0 2.8 copy-start.10
  334.4 2.2 copy-start.23
  336.8 10.8 %all-to-all-start.9 = ((bf16[128,8,112]{0,2,1:T(8,128)(2,1)}), bf16[128,8,112]{0,2,1:T(8,128)(2,1)S(1)}, u32[]{:S(2)}, u32[]{:S(2)}) async-start(bf16[128,8,112]{0,2,1:T(8,128)(2,1)} %bitcast.285), calls=%async_computation.9 | async-start | bytes 458752 | tf_op jit(solution)/shard_map/all_to_all | solution.py:402
  347.6 0.7 copy-start.31
  348.3 12.4 %all-to-all-start.8 = ((bf16[128,8,112]{0,2,1:T(8,128)(2,1)}), bf16[128,8,112]{0,2,1:T(8,128)(2,1)}, u32[]{:S(2)}, u32[]{:S(2)}) async-start(bf16[128,8,112]{0,2,1:T(8,128)(2,1)} %multiply_convert_fusion.3), calls=%async_computation.8 | async-start | bytes 458752 | tf_op jit(solution)/shard_map/all_to_all | solution.py:401
  360.7 30.4 %all-to-all-start.11 = ((bf16[8,112,608]{2,1,0:T(8,128)(2,1)}), bf16[8,112,608]{2,1,0:T(8,128)(2,1)S(1)}, u32[]{:S(2)}, u32[]{:S(2)}) async-start(bf16[8,112,608]{2,1,0:T(8,128)(2,1)} %bitcast.262), calls=%async_computation.11 | async-start | bytes 2293760 | tf_op jit(solution)/shard_map/all_to_all | solution.py:406
  391.1 30.8 %all-to-all-start.12 = ((bf16[8,112,608]{2,1,0:T(8,128)(2,1)}), bf16[8,112,608]{2,1,0:T(8,128)(2,1)}, u32[]{:S(2)}, u32[]{:S(2)}) async-start(bf16[8,112,608]{2,1,0:T(8,128)(2,1)} %bitcast.263), calls=%async_computation.12 | async-start | bytes 2293760 | tf_op jit(solution)/shard_map/all_to_all | solution.py:413
  421.9 73.8 %all-to-all-start.3 = ((f32[8,128,896]{2,1,0:T(8,128)}), f32[8,128,896]{2,1,0:T(8,128)}, u32[]{:S(2)}, u32[]{:S(2)}) async-start(f32[8,128,896]{2,1,0:T(8,128)} %fusion.26), calls=%async_computation.3 | async-start | bytes 7340032 | tf_op jit(solution)/shard_map/all_to_all | solution.py:38
  426.5 215.5 %all-reduce.7.cloned.1.call-start = ((), (), s32[]{:S(2)}) async-start(), calls=%async_computation.16 | async-start | bytes 7340032 | tf_op jit(solution)/shard_map/psum | solution.py:432
  495.8 8.2 %all-to-all-start.10 = ((f32[8,1,112]{2,1,0:T(1,128)}), f32[8,1,112]{2,1,0:T(1,128)S(1)}, u32[]{:S(2)}, u32[]{:S(2)}) async-start(f32[8,1,112]{2,1,0:T(1,128)} %all_to_all.138), calls=%async_computation.10 | async-start | bytes 8192 | tf_op jit(solution)/shard_map/all_to_all | solution.py:38
  499.1 6.7 %copy-start.24 = (f32[2,128,128]{1,2,0:T(8,128)S(1)}, f32[2,128,128]{1,2,0:T(8,128)}, u32[]{:S(2)}) copy-start(f32[2,128,128]{1,2,0:T(8,128)} %copy-done.23) | copy-start | bytes 393220
  499.1 6.7 %copy-start.26 = (bf16[1,896,128]{2,1,0:T(8,128)(2,1)S(1)}, bf16[1,896,128]{2,1,0:T(8,128)(2,1)}, u32[]{:S(2)}) copy-start(bf16[1,896,128]{2,1,0:T(8,128)(2,1)} %copy-done.25) | copy-start | bytes 688132
  499.1 7.0 %copy-start.11 = (bf16[128,896]{1,0:T(8,128)(2,1)S(1)}, bf16[128,896]{1,0:T(8,128)(2,1)}, u32[]{:S(2)}) copy-start(bf16[128,896]{1,0:T(8,128)(2,1)} %copy-done.10) | copy-start | bytes 688132
  505.8 7.5 %copy-start.9 = (bf16[1,128,896]{2,1,0:T(8,128)(2,1)S(1)}, bf16[1,128,896]{2,1,0:T(8,128)(2,1)}, u32[]{:S(2)}) copy-start(bf16[1,128,896]{2,1,0:T(8,128)(2,1)} %param.29) | copy-start | bytes 688132
  505.8 7.5 %copy-start.38 = (f32[128]{0:T(128)S(1)}, f32[128]{0:T(128)}, u32[]{:S(2)}) copy-start(f32[128]{0:T(128)} %copy-done.37) | copy-start | bytes 1540
  505.9 7.5 %copy-start.40 = (f32[128]{0:T(128)S(1)}, f32[128]{0:T(128)}, u32[]{:S(2)}) copy-start(f32[128]{0:T(128)} %copy-done.39) | copy-start | bytes 1540
  505.9 7.5 %copy-start.42 = (f32[128]{0:T(128)S(1)}, f32[128]{0:T(128)}, u32[]{:S(2)}) copy-start(f32[128]{0:T(128)} %copy-done.41) | copy-start | bytes 1540
  510.0 8.6 %all-to-all-start.7 = ((f32[8,1,112]{2,1,0:T(1,128)}), f32[8,1,112]{2,1,0:T(1,128)S(1)}, u32[]{:S(2)}, u32[]{:S(2)}) async-start(f32[8,1,112]{2,1,0:T(1,128)} %all_to_all.130), calls=%async_computation.7 | async-start | bytes 8192 | tf_op jit(solution)/shard_map/all_to_all | solution.py:38
  515.5 8.9 %copy-start.43 = (bf16[112]{0:T(256)(128)(2,1)S(1)}, bf16[112]{0:T(256)(128)(2,1)}, u32[]{:S(2)}) copy-start(bf16[112]{0:T(256)(128)(2,1)} %reduce_sum.171) | copy-start | bytes 676
  641.9 2.8 copy-start.17
  644.7 1.6 copy-start.16
  646.2 1.7 copy-start.33
  646.2 2.4 copy-start.32
  (1 other events, 0.7 us)
Sparse Core Ops, SparseCore 0:
  10.3 63.4 all-gather.8
  76.0 52.0 all-gather.6
  336.7 145.6 all-gather.10
  488.1 153.7 all-reduce.6
where the time goes:
time: 667 us; the launch traced here: 656 us
  waiting for transfers between devices  246 us (37%)
  blocking collectives  168 us (25%)
  matrix products  94.9 us (14%)
  starting transfers between devices  54.1 us (8%)
  local copies, waits for them, and re-layouts  39.1 us (6%)
  other arithmetic  38.6 us (6%)
  between operations  15.9 us (2%)
    psum x1, blocking collectives, local(): lax.psum(gain_first.astype(jnp.bfloat16), 'replica').astype(jnp.float32)  64.8 us
    psum x1, waiting for transfers between devices, local(): lax.psum(grad_query_weight.astype(jnp.bfloat16), 'replica')  48.9 us
    all_to_all x4, waiting for transfers between devices, summed_on_arrival(): lax.all_to_all(blocks, axis, split_axis=0, concat_axis=0, tiled=True)  48.4 us
    all_gather x1, waiting for transfers between devices, sent_together(): filled = lax.all_gather(both, axis, axis=dim, tiled=True)  44.3 us
    all_gather x2, waiting for transfers between devices, side_by_side(): lax.all_gather(both, axis, axis=dim, tiled=True)  38.3 us
    unnamed x1, blocking collectives  35.2 us
    all_gather x1, blocking collectives, fetch_weights(): lax.all_gather(w_value[layer_index], 'group', axis=0, tiled=True)  23.1 us
    all_to_all x1, blocking collectives, sent_to_all(): return lax.all_to_all(copies, axis, split_axis=0, concat_axis=0, tiled=True)  22.7 us
  transfers between devices with their start and end apart: 16, of which 14 were waited for; matrix products, arithmetic and copies ran while one was open for 14% of the time, Pallas kernels for 0%

commit v1 on v0

v1 whole, which is shorter than its diff:
```python
import jax
import jax.numpy as jnp
from jax import lax
from jax.sharding import Mesh
from jax.sharding import PartitionSpec as P

KV_HEADS = 2
HEAD_DIM = 64
EPS = 1e-06
THETA = 1000000.0
MASKED_SCORE = -1e30
GROUP = ("y", "xl")
REPLICA = ("xh", "z", "c")
SIZES = (4, 2, 2, 4, 2)
AXES = ("y", "xl", "xh", "z", "c")
N = 8
PAD = 640
BF = jnp.bfloat16
F32 = jnp.float32


def shift(array, axis, by, size):
    return lax.ppermute(array, axis, [(i, (i + by) % size) for i in range(size)])


def gather_slots(array):
    return [array] + [shift(array, GROUP, -k, N) for k in range(1, N)]


def return_slots(slots):
    total = slots[0].astype(F32)
    for k in range(1, N):
        total = total + shift(slots[k], GROUP, k, N).astype(F32)
    return total


def at(blocks, index):
    return lax.dynamic_index_in_dim(blocks, index, 0, keepdims=False)


def to_all(array):
    return lax.all_to_all(jnp.broadcast_to(array, (N, *array.shape)), GROUP, 0, 0, tiled=True)


def turn_half(values_in):
    half_size = values_in.shape[-1] // 2
    return jnp.concatenate([-values_in[..., half_size:], values_in[..., :half_size]], axis=-1)


def rotate(values_in, cosine_table, sine_table):
    return values_in * cosine_table + turn_half(values_in) * sine_table


def rotate_back(gradient, cosine_table, sine_table):
    return gradient * cosine_table - turn_half(gradient * sine_table)


def norm_forward(stream, gain):
    scale = lax.rsqrt(jnp.mean(stream * stream, axis=-1, keepdims=True) + EPS)
    return stream * scale * gain, scale


def norm_backward(stream, scale, gain, gradient):
    normalized = stream * scale
    scaled = gradient * gain
    gain_grad = jnp.sum(gradient * normalized, axis=0)
    grad = scale * (scaled - normalized * jnp.mean(scaled * normalized, axis=-1, keepdims=True))
    return grad, gain_grad


def mm(a, b):
    return jnp.dot(a, b, preferred_element_type=F32)


def mm_t(a, b):
    return lax.dot_general(a, b, (((1,), (1,)), ((), ())), preferred_element_type=F32)


def outer(a, b):
    return lax.dot_general(a, b, (((0,), (0,)), ((), ())), preferred_element_type=F32)


def core_sum(first, second, c):
    low = c == 0
    keep = jnp.where(low, first, second)
    send = jnp.where(low, second, first).astype(BF)
    return (keep + shift(send, "c", 1, 2).astype(F32)).astype(BF)


def core_pair(own, c):
    other = shift(own, "c", 1, 2)
    low = c == 0
    return jnp.where(low, own, other), jnp.where(low, other, own)


def spread_sum(blocks, z, xh):
    total = at(blocks, z).astype(F32)
    for k in (1, 3, 2):
        total = total + shift(at(blocks, (z + k) % 4), "z", k, 4).astype(F32)
    send = at(total, 1 - xh).astype(BF)
    return (at(total, xh) + shift(send, "xh", 1, 2).astype(F32)).astype(BF)


def spread_gather(piece, z, xh):
    other = shift(piece, "xh", 1, 2)
    low = xh == 0
    pair = jnp.stack([jnp.where(low, piece, other), jnp.where(low, other, piece)])
    slots = jnp.stack([pair] + [shift(pair, "z", -k, 4) for k in (1, 2, 3)])
    return [at(slots, (j // 2 - z) % 4)[j % 2] for j in range(8)]


def swap_pairs():
    pairs = []
    for y in range(4):
        for xl in range(2):
            for xh in range(2):
                for z in range(4):
                    for c in range(2):
                        source = (((y * 2 + xl) * 2 + xh) * 4 + z) * 2 + c
                        target = (((z * 2 + xh) * 2 + xl) * 4 + y) * 2 + c
                        pairs.append((source, target))
    return pairs


def local(
    hidden_in,
    segment_ids,
    attn_gain,
    w_query,
    b_query,
    w_key,
    b_key,
    w_value,
    b_value,
    w_out,
    ffn_gain,
    w_gate,
    w_up,
    w_down,
    cotangent,
):
    g = lax.axis_index(GROUP)
    c = lax.axis_index("c")
    z = lax.axis_index("z")
    xh = lax.axis_index("xh")
    rows, width = hidden_in.shape[1:]
    part = w_query.shape[1]
    units = w_down.shape[1]
    kv = w_key.shape[2]
    heads = width // HEAD_DIM
    ratio = heads // KV_HEADS

    segments = segment_ids[0]
    length = segments.shape[0]
    own_segments = lax.dynamic_slice_in_dim(segments, g * rows, rows, 0)
    query_index = g * rows + jnp.arange(rows, dtype=jnp.int32)
    earlier = jnp.sum((segments[None, :] < own_segments[:, None]).astype(jnp.int32), axis=-1)
    positions = query_index - earlier
    blocks = (g - jnp.arange(N, dtype=jnp.int32)) % N
    key_index = (blocks[:, None] * rows + jnp.arange(rows, dtype=jnp.int32)[None]).reshape(-1)
    doubled = jnp.concatenate([segments.reshape(N, rows)] * 2, axis=0)
    key_segments = lax.dynamic_slice_in_dim(doubled, g + 1, N, 0)[::-1].reshape(-1)
    allowed = (key_index[None, :] <= query_index[:, None]) & (
        key_segments[None, :] == own_segments[:, None]
    )
    half = HEAD_DIM // 2
    frequency = THETA ** (-(2.0 * jnp.arange(half, dtype=F32)) / HEAD_DIM)
    angles = positions.astype(F32)[:, None] * frequency
    cosine = jnp.concatenate([jnp.cos(angles)] * 2, axis=-1)[:, None, :]
    sine = jnp.concatenate([jnp.sin(angles)] * 2, axis=-1)[:, None, :]

    small = jnp.concatenate([attn_gain[0], b_query[0], b_key[0], b_value[0], ffn_gain[0]])
    small = jnp.pad(small[None], ((0, 15), (0, width + 2 * kv - small.shape[0])))
    packed = jnp.concatenate(
        [jnp.concatenate([w_query[0], w_key[0], w_value[0]], axis=1), small], axis=0
    )
    fetched = to_all(packed)
    w_qkv = fetched[:, :part].reshape(width, width + 2 * kv)
    vec = fetched[:, part].astype(F32)
    k16 = kv // N
    first_gain = vec[:, :part].reshape(-1)
    bias = jnp.concatenate(
        [
            vec[:, part : 2 * part].reshape(-1),
            vec[:, 2 * part : 2 * part + k16].reshape(-1),
            vec[:, 2 * part + k16 : 2 * part + 2 * k16].reshape(-1),
        ]
    )
    second_gain = vec[:, 2 * part + 2 * k16 : 3 * part + 2 * k16].reshape(-1)
    out_weight = to_all(w_out[0]).reshape(width, width)

    def pad_units(w):
        return jnp.pad(w.reshape(part, N, units), ((0, 0), (0, 0), (0, PAD - units)))

    gate_up = jnp.moveaxis(jnp.concatenate([pad_units(w_gate[0]), pad_units(w_up[0])], -1), 1, 0)
    w_gu = lax.all_to_all(gate_up, GROUP, 0, 0, tiled=True).reshape(width, 2 * PAD)
    w_dn = jnp.pad(w_down[0], ((0, PAD - units), (0, 0)))
    group_down = jnp.concatenate(gather_slots(cotangent[0]))

    stream = hidden_in[0].astype(F32)
    normed, first_scale = norm_forward(stream, first_gain)
    normed = normed.astype(BF)
    raw = mm(normed, w_qkv) + bias
    turned = rotate(raw[:, : width + kv].reshape(rows, -1, HEAD_DIM), cosine, sine)
    turned = turned.reshape(rows, -1).astype(BF)
    queries = turned[:, :width].reshape(rows, KV_HEADS, ratio, HEAD_DIM)
    own_kv = jnp.concatenate([turned[:, width:], raw[:, width + kv :].astype(BF)], axis=1)
    slots = [own_kv]
    for k in range(1, N):
        slots.append(lax.ppermute(own_kv, GROUP, [(i, i + k) for i in range(N - k)]))
    all_kv = jnp.concatenate(slots)
    keys = all_kv[:, :kv].reshape(length, KV_HEADS, HEAD_DIM)
    values = all_kv[:, kv:].reshape(length, KV_HEADS, HEAD_DIM)
    scores = jnp.einsum("qcgd,kcd->cgqk", queries, keys, preferred_element_type=F32)
    scores = jnp.where(allowed[None, None], scores * HEAD_DIM ** (-0.5), MASKED_SCORE)
    maximum = jnp.max(scores, axis=-1, keepdims=True)
    weights = jnp.exp(scores - maximum)
    totals = jnp.sum(weights, axis=-1, keepdims=True)
    probs = (weights / totals).astype(BF)
    mixed = jnp.einsum("cgqk,kcd->qcgd", probs, values, preferred_element_type=F32)
    attended = mixed.reshape(rows, -1).astype(BF)
    logsum = maximum + jnp.log(totals)
    middle = stream + mm(attended, out_weight)

    second_normed, second_scale = norm_forward(middle, second_gain)
    group_second = jnp.concatenate(gather_slots(second_normed.astype(BF)))
    both = mm(group_second, w_gu)
    gate, up = both[:, :PAD], both[:, PAD:]
    sigmoid = jax.nn.sigmoid(gate)
    hidden = (gate * sigmoid * up).astype(BF)
    grad_hidden = mm_t(group_down, w_dn)
    grad_gate = (grad_hidden * up * sigmoid * (1.0 + gate * (1.0 - sigmoid))).astype(BF)
    grad_up = (grad_hidden * gate * sigmoid).astype(BF)
    grad_both = jnp.concatenate([grad_gate, grad_up], axis=1)
    second_terms = mm_t(grad_both, w_gu).astype(BF)
    grad_second = return_slots([second_terms[k * rows : (k + 1) * rows] for k in range(N)])
    down_terms = mm(hidden, w_dn).astype(BF)
    layer_out = middle + return_slots([down_terms[k * rows : (k + 1) * rows] for k in range(N)])
    hidden_out = layer_out.astype(BF)[None]

    shares = core_sum(outer(group_second, grad_gate), outer(group_second, grad_up), c)
    share = spread_sum(shares.reshape(4, 2, part, PAD), z, xh)
    share = lax.ppermute(share, AXES, swap_pairs())
    columns = jnp.stack(spread_gather(share, z, xh))
    columns = core_pair(columns, c)

    def unpad(array):
        return jnp.moveaxis(array[:, :, :units], 0, 1).reshape(1, part, N * units).astype(F32)

    grad_w_gate, grad_w_up = unpad(columns[0]), unpad(columns[1])
    down_share = outer(hidden, group_down)
    half_rows = PAD // 2
    down_share = core_sum(down_share[:half_rows], down_share[half_rows:], c)
    down_share = spread_sum(down_share.reshape(4, 2, PAD // 16, width), z, xh)
    down_share = jnp.concatenate(spread_gather(down_share, z, xh))
    grad_w_down = jnp.concatenate(core_pair(down_share, c))[None, :units].astype(F32)

    stream_grad = cotangent[0].astype(F32)
    term, gain_second = norm_backward(middle, second_scale, second_gain, grad_second)
    grad_middle = stream_grad + term
    attn_grad = grad_middle.astype(BF)
    grad_attended = mm_t(attn_grad, out_weight).astype(BF)
    grad_out = outer(attended, attn_grad)
    grad_split = grad_attended.reshape(queries.shape)
    probs = jnp.exp(scores - logsum)
    grad_probs = jnp.einsum("qcgd,kcd->cgqk", grad_split, values, preferred_element_type=F32)
    inner = jnp.sum(probs * grad_probs, axis=-1, keepdims=True)
    grad_scores = (probs * (grad_probs - inner) * HEAD_DIM ** (-0.5)).astype(BF)
    grad_queries = jnp.einsum("cgqk,kcd->qcgd", grad_scores, keys, preferred_element_type=F32)
    grad_keys = jnp.einsum("cgqk,qcgd->kcd", grad_scores, queries, preferred_element_type=F32)
    grad_values = jnp.einsum(
        "cgqk,qcgd->kcd", probs.astype(BF), grad_split, preferred_element_type=F32
    )
    grad_kv = jnp.concatenate([grad_keys.reshape(length, kv), grad_values.reshape(length, kv)], 1)
    own = grad_kv[:rows]
    grad_kv = grad_kv.astype(BF)
    for k in range(1, N):
        block = grad_kv[k * rows : (k + 1) * rows]
        own = own + lax.ppermute(block, GROUP, [(i, i - k) for i in range(k, N)]).astype(F32)
    grad_qk = jnp.concatenate([grad_queries.reshape(rows, width), own[:, :kv]], axis=1)
    grad_qk = rotate_back(grad_qk.reshape(rows, -1, HEAD_DIM), cosine, sine).reshape(rows, -1)
    grad_qkv = jnp.concatenate([grad_qk, own[:, kv:]], axis=1).astype(BF)
    grad_first = mm_t(grad_qkv, w_qkv)
    term, gain_first = norm_backward(stream, first_scale, first_gain, grad_first)
    grad_in = (grad_middle + term)[None]

    outer_qkv = outer(normed, grad_qkv)
    bias_grad = jnp.sum(grad_qkv.astype(F32), axis=0)
    lanes = width + kv
    row_a = jnp.concatenate(
        [
            bias_grad[:width].reshape(N, part),
            bias_grad[width : width + kv].reshape(N, k16),
            bias_grad[width + kv :].reshape(N, k16),
        ],
        axis=1,
    )
    row_b = jnp.concatenate([gain_first.reshape(N, part), gain_second.reshape(N, part)], axis=1)

    def with_row(array, row):
        row = jnp.pad(row[:, None], ((0, 0), (0, 15), (0, lanes - row.shape[1])))
        return jnp.concatenate([array.reshape(N, part, lanes), row], axis=1)

    side_a = with_row(outer_qkv[:, :lanes], row_a)
    side_b = with_row(jnp.concatenate([grad_out, outer_qkv[:, lanes:]], axis=1), row_b)
    shares = core_sum(side_a, side_b, c)
    total = at(shares, g).astype(F32)
    for k in range(1, N):
        total = total + shift(at(shares, (g + k) % N), GROUP, k, N).astype(F32)
    pieces = jnp.moveaxis(total.astype(BF).reshape(part + 16, 4, 2, lanes // 8), 0, 2)
    piece = spread_sum(pieces, z, xh)
    whole = jnp.concatenate(spread_gather(piece, z, xh), axis=1)
    whole_a, whole_b = [half_side.astype(F32) for half_side in core_pair(whole, c)]
    last_a, last_b = whole_a[part], whole_b[part]
    return (
        hidden_out,
        grad_in,
        last_b[None, :part],
        whole_a[None, :part, :width],
        last_a[None, :part],
        whole_a[None, :part, width:],
        last_a[None, part : part + k16],
        whole_b[None, :part, width:],
        last_a[None, part + k16 : part + 2 * k16],
        whole_b[None, :part, :width],
        last_b[None, part : 2 * part],
        grad_w_gate,
        grad_w_up,
        grad_w_down,
    )


def solution(mesh):
    split = Mesh(mesh.devices.reshape(SIZES), AXES)
    tokens = P(REPLICA, GROUP, None)
    vector = P(None, GROUP)
    matrix = P(None, GROUP, None)
    weights = (vector, matrix, vector, matrix, vector, matrix, vector, matrix, vector)
    return jax.shard_map(
        local,
        mesh=split,
        in_specs=(tokens, P(REPLICA, None)) + weights + (matrix,) * 3 + (tokens,),
        out_specs=(tokens, tokens) + weights + (matrix,) * 3,
        check_vma=False,
    )
```

time: 667 us -> 469 us (0.70)
  waiting for transfers between devices: 246 us -> 74 us
  blocking collectives: 168 us -> 0 us
  starting transfers between devices: 54.1 us -> 195 us
  local copies, waits for them, and re-layouts: 39.1 us -> 83.4 us
  matrix products: 94.9 us -> 74 us
  between operations: 15.9 us -> 2.35 us
  other arithmetic: 38.6 us -> 31.1 us
    ppermute x0 -> x80, starting transfers between devices: none -> 178 us  [the longest x65 151 us: shift(): lax.ppermute(array, axis, [(i, (i + by) % size) for i in range(size)])]
    all_to_all x12 -> x3, waiting for transfers between devices: 114 us -> 1.17 us  [the longest x2 1.16 us: to_all(): lax.all_to_all(jnp.broadcast_to(array, (N, *array.shape)), GROUP, 0, 0, t...]
    all_gather x3 -> x0, waiting for transfers between devices: 82.6 us -> none  [the longest x1 44.3 us: sent_together(): filled = lax.all_gather(both, axis, axis=dim, tiled=True)]
    ppermute x0 -> x80, waiting for transfers between devices: none -> 72.8 us  [the longest x65 72.8 us: shift(): lax.ppermute(array, axis, [(i, (i + by) % size) for i in range(size)])]
    psum x1 -> x0, blocking collectives: 64.8 us -> none  [local(): lax.psum(gain_first.astype(jnp.bfloat16), 'replica').astype(jnp.float32)]
    psum x1 -> x0, waiting for transfers between devices: 48.9 us -> none  [local(): lax.psum(grad_query_weight.astype(jnp.bfloat16), 'replica')]
    all_gather x2 -> x0, blocking collectives: 45.2 us -> none  [the longest x1 23.1 us: fetch_weights(): lax.all_gather(w_value[layer_index], 'group', axis=0, tiled=True)]
    all_to_all x12 -> x3, starting transfers between devices: 54 us -> 17.6 us  [the longest x2 13.2 us: to_all(): lax.all_to_all(jnp.broadcast_to(array, (N, *array.shape)), GROUP, 0, 0, t...]
  transfers between devices with their start and end apart: 16 -> 83, of which waited for: 14 -> 25; matrix products, arithmetic and copies ran while one was open for 14% -> 26% of each run, Pallas kernels for 0% -> 0%
where the time goes in v1:
time: 469 us; the launch traced here: 460 us
  starting transfers between devices  195 us (42%)
  local copies, waits for them, and re-layouts  83.4 us (18%)
  waiting for transfers between devices  74 us (16%)
  matrix products  74 us (16%)
  other arithmetic  31.1 us (7%)
    ppermute x65, starting transfers between devices, shift(): lax.ppermute(array, axis, [(i, (i + by) % size) for i in range(size)])  151 us
    ppermute x65, waiting for transfers between devices, shift(): lax.ppermute(array, axis, [(i, (i + by) % size) for i in range(size)])  72.8 us
    unnamed x130, local copies, waits for them, and re-layouts  33.3 us
    ppermute x7, starting transfers between devices, local(): lax.ppermute(own_kv, GROUP, [(i, i + k) for i in range(N - k)])  16.8 us
    dot_general x5, matrix products, outer(): lax.dot_general(a, b, (((0,), (0,)), ((), ())), preferred_element_type=F32)  15 us
    all_to_all x2, starting transfers between devices, to_all(): lax.all_to_all(jnp.broadcast_to(array, (N, *array.shape)), GROUP, 0, 0, t...  13.2 us
    dot_general x4, matrix products, mm_t(): lax.dot_general(a, b, (((1,), (1,)), ((), ())), preferred_element_type=F32)  13 us
    dot_general x1, matrix products, local(): jnp.einsum('cgqk,kcd->qcgd', grad_scores, keys, preferred_element_type=F32)  12.6 us
  transfers between devices with their start and end apart: 83, of which 25 were waited for; matrix products, arithmetic and copies ran while one was open for 26% of the time, Pallas kernels for 0%

profile of v1, /device:TPU:1, one launch (start us, length us, event | category | flops | bytes accessed | tf_op | source)
XLA Modules:
  0.0 460.3 jit_solution(7537270949931217713)
XLA Ops:
  0.6 4.6 collective-permute-start.21
  5.8 2.6 collective-permute-start.24
  8.4 3.4 concatenate.82
  14.6 5.3 %all-to-all-start = ((bf16[8,128,1152]{2,1,0:T(8,128)(2,1)}), bf16[8,128,1152]{2,1,0:T(8,128)(2,1)S(1)}, u32[]{:S(2)}, u32[]{:S(2)}) async-start(bf16[8,128,1152]{2,1,0:T(8,128)(2,1)} %broadcast_in_dim.35), calls=%async_computation | async-start | bytes 4718592 | tf_op jit(solution)/shard_map/all_to_all | solution.py:42
  22.7 3.1 reshape_squeeze.11
  25.7 3.9 reshape_squeeze.10
  49.2 8.0 %all-to-all-start.1 = ((bf16[8,112,896]{2,1,0:T(8,128)(2,1)}), bf16[8,112,896]{2,1,0:T(8,128)(2,1)S(1)}, u32[]{:S(2)}, u32[]{:S(2)}) async-start(bf16[8,112,896]{2,1,0:T(8,128)(2,1)} %broadcast_in_dim.38), calls=%async_computation.1 | async-start | bytes 3211264 | tf_op jit(solution)/shard_map/all_to_all | solution.py:42
  70.9 3.4 collective-permute-start
  75.9 3.1 collective-permute-start.1
  79.0 3.7 collective-permute-start.2
  82.7 2.5 collective-permute-start.3
  96.8 3.0 copy-done
  100.8 4.4 all-to-all-start.2
  105.2 4.4 fusion.24
  111.1 3.5 collective-permute-start.7
  117.0 2.4 collective-permute-start.10
  119.4 11.2 %collective-permute-done.7 = bf16[128,896]{1,0:T(8,128)(2,1)S(1)} collective-permute-done((bf16[128,896]{1,0:T(8,128)(2,1)S(1)}, bf16[128,896]{1,0:T(8,128)(2,1)S(1)}, u32[]{:S(2)}, u32[]{:S(2)}) %collective-permute-start.7) | collective-permute-done | bytes 229408 | tf_op jit(solution)/shard_map/ppermute | solution.py:23
  131.8 4.1 collective-permute-done.8
  135.9 5.2 %collective-permute-start.13 = (bf16[128,896]{1,0:T(8,128)(2,1)S(1)}, bf16[128,896]{1,0:T(8,128)(2,1)S(1)}, u32[]{:S(2)}, u32[]{:S(2)}) collective-permute-start(bf16[128,896]{1,0:T(8,128)(2,1)S(1)} %get-tuple-element.62), channel_id=1, source_target_pairs={{0,16},{16,32},{32,48},{48,64},{64,80},{80,96},{96,112},{112,0},{1... | collective-permute-start | bytes 688136 | tf_op jit(solution)/shard_map/ppermute | solution.py:23
  148.4 5.2 %fusion.124 = f32[1024,1280]{1,0:T(8,128)S(1)} fusion(bf16[1024,896]{1,0:T(8,128)(2,1)} %constant_dynamic-update-slice_fusion.8, bf16[896,1280]{1,0:T(8,128)(2,1)} %bitcast.32), kind=kOutput, calls=%fused_computation.310 | convolution fusion | flops 2348810240 | bytes 9371648 | tf_op jit(solution)/shard_map/dot_general | solution.py:72
  153.6 3.9 multiply_convert_fusion.1
  159.2 3.0 fusion.127
  162.2 4.0 fusion.126
  166.2 5.4 %fusion.21 = bf16[1024,896]{1,0:T(8,128)(2,1)S(1)} fusion(bf16[896,1280]{1,0:T(8,128)(2,1)} %bitcast.32, bf16[1024,640]{1,0:T(8,128)(2,1)S(1)} %get-tuple-element.64, bf16[1024,640]{1,0:T(8,128)(2,1)S(1)} %get-tuple-element.63), kind=kOutput, calls=%fused_computation.43 | convolution fusion | flops 2354970624 | bytes 6750208 | tf_op jit(solution)/shard_map/dot_general | solution.py:76
  171.7 6.8 %collective-permute-start.34 = (bf16[128,896]{1,0:T(8,128)(2,1)S(1)}, bf16[128,896]{1,0:T(8,128)(2,1)S(1)}, u32[]{:S(2)}, u32[]{:S(2)}) collective-permute-start(bf16[128,896]{1,0:T(8,128)(2,1)S(1)} %get-tuple-element.76), channel_id=1, source_target_pairs={{0,112},{16,0},{32,16},{48,32},{64,48},{80,64},{96,80},{112,96},{1... | collective-permute-start | bytes 688136 | tf_op jit(solution)/shard_map/ppermute | solution.py:23
  181.7 4.9 %select_convert_fusion.1 = (bf16[896,640]{1,0:T(8,128)(2,1)}, f32[896,640]{1,0:T(8,128)}) fusion(f32[896,640]{1,0:T(8,128)S(1)} %fusion.126, pred[]{:T(512)S(6)} %eq.76, bf16[1024,896]{1,0:T(8,128)(2,1)} %constant_dynamic-update-slice_fusion.8, bf16[1024,640]{1,0:T(8,128)(2,1)S(1)} %get-tuple-element.64), kind=kOutput, calls=%fused_computation.42 | convolution fusion | flops 1174978560 | bytes 8880129 | tf_op jit(solution)/shard_map/dot_general | solution.py:80
  188.7 6.7 %collective-permute-start.28 = (bf16[128,896]{1,0:T(8,128)(2,1)S(1)}, bf16[128,896]{1,0:T(8,128)(2,1)S(1)}, u32[]{:S(2)}, u32[]{:S(2)}) collective-permute-start(bf16[128,896]{1,0:T(8,128)(2,1)S(1)} %get-tuple-element.75), channel_id=1, source_target_pairs={{0,16},{16,32},{32,48},{48,64},{64,80},{80,96},{96,112},{112,0},{1... | collective-permute-start | bytes 688136 | tf_op jit(solution)/shard_map/ppermute | solution.py:23
  195.4 3.3 collective-permute-start.20
  205.0 4.0 collective-permute-start.15
  210.4 3.2 collective-permute-done.18
  214.6 10.5 %collective-permute-done.15 = bf16[128,896]{1,0:T(8,128)(2,1)S(1)} collective-permute-done((bf16[128,896]{1,0:T(8,128)(2,1)S(1)}, bf16[128,896]{1,0:T(8,128)(2,1)S(1)}, u32[]{:S(2)}, u32[]{:S(2)}) %collective-permute-start.15) | collective-permute-done | bytes 229408 | tf_op jit(solution)/shard_map/ppermute | solution.py:23
  231.2 5.2 %fusion.125 = f32[2,1024,128,7]{2,1,3,0:T(8,128)} fusion(bf16[1024,2,64,1]{0,2,3,1:T(8,128)(2,1)} %bitcast.401, bf16[128,2,7,64]{0,3,2,1:T(8,128)(2,1)} %bitcast.394), kind=kOutput, calls=%fused_computation.311 | convolution fusion | flops 234881024 | bytes 7831552 | tf_op jit(solution)/shard_map/qcgd,kcd->cgqk/dot_general | solution.py:266
  238.5 12.5 %fusion.17 = f32[2,64,1024,1]{2,1,3,0:T(8,128)S(1)} fusion(bf16[128,2,7,64]{0,3,2,1:T(8,128)(2,1)} %bitcast.405, f32[2,1024,128,7]{2,1,3,0:T(8,128)} %fusion.125, f32[2,7,128,1024]{2,3,1,0:T(8,128)} %copy-done, f32[2,7,128]{2,1,0:T(8,128)S(1)} %log_add_fusion), kind=kOutput, calls=%fused_computation.35 | convolution fusion | flops 247728896 | bytes 15440896 | tf_op jit(solution)/shard_map/cgqk,qcgd->kcd/dot_general | solution.py:270
  263.0 12.6 %fusion.18 = f32[2,64,7,128]{3,1,2,0:T(8,128)S(1)} fusion(bf16[1024,2,64,1]{0,2,3,1:T(8,128)(2,1)S(1)} %bitcast.399, f32[2,1024,128,7]{2,1,3,0:T(8,128)} %fusion.125, f32[2,7,128,1024]{2,3,1,0:T(8,128)} %copy-done, f32[2,7,128]{2,1,0:T(8,128)S(1)} %log_add_fusion), kind=kOutput, calls=%fused_computation.36 | convolution fusion | flops 247728896 | bytes 15408128 | tf_op jit(solution)/shard_map/cgqk,kcd->qcgd/dot_general | solution.py:269
  275.7 3.7 collective-permute-start.59
  285.1 2.5 fusion.54
  287.9 4.1 pad_maximum_fusion
  292.0 5.2 %copy.120 = f32[896,1024]{1,0:T(8,128)} copy(f32[896,1024]{0,1:T(8,128)} %pad_maximum_fusion) | data formatting | bytes 7340032 | tf_op jit(solution)/shard_map/concatenate | solution.py:305
  298.5 3.7 collective-permute-start.73
  303.7 2.8 select_convert_fusion
  306.5 3.0 collective-permute-done.72
  309.6 2.9 collective-permute-start.74
  314.4 2.9 collective-permute-start.75
  320.3 3.3 collective-permute-start.77
  326.7 2.6 collective-permute-start.61
  329.5 4.5 collective-permute-done.62
  334.0 7.0 %collective-permute-done.61 = bf16[2,112,640]{2,1,0:T(8,128)(2,1)S(1)} collective-permute-done((bf16[2,112,640]{2,1,0:T(8,128)(2,1)S(1)}, bf16[2,112,640]{2,1,0:T(8,128)(2,1)S(1)}, u32[]{:S(2)}, u32[]{:S(2)}) %collective-permute-start.61) | collective-permute-done | bytes 286752 | tf_op jit(solution)/shard_map/ppermute | solution.py:23
  341.5 3.3 collective-permute-start.63
  344.8 2.6 collective-permute-done.63
  348.2 7.9 %collective-permute-start.65 = (bf16[112,640]{1,0:T(8,128)(2,1)S(1)}, bf16[112,640]{1,0:T(8,128)(2,1)S(1)}, u32[]{:S(2)}, u32[]{:S(2)}) collective-permute-start(bf16[112,640]{1,0:T(8,128)(2,1)S(1)} %collective-permute-done.64), channel_id=1, source_target_pairs={{0,8},{8,0},{1,9},{9,1},{2,10},{10,2},{3,11},{11,3},{4,12},{12,4},... | collective-permute-start | bytes 430088 | tf_op jit(solution)/shard_map/ppermute | solution.py:23
  356.1 6.7 %collective-permute-start.79 = (bf16[320,896]{1,0:T(8,128)(2,1)S(1)}, bf16[320,896]{1,0:T(8,128)(2,1)S(1)}, u32[]{:S(2)}, u32[]{:S(2)}) collective-permute-start(bf16[320,896]{1,0:T(8,128)(2,1)S(1)} %constant_dynamic-update-slice_fusion.32), channel_id=1, source_target_pairs={{0,1},{1,0},{2,3},{3,2},{4,5},{5,4},{6,7},{7,6},{8,9},{9,8},{10,11... | collective-permute-start | bytes 1720328 | tf_op jit(solution)/shard_map/ppermute | solution.py:23
  363.0 2.5 collective-permute-start.68
  365.4 5.6 %collective-permute-start.67 = (bf16[2,112,640]{2,1,0:T(8,128)(2,1)S(1)}, bf16[2,112,640]{2,1,0:T(8,128)(2,1)S(1)}, u32[]{:S(2)}, u32[]{:S(2)}) collective-permute-start(bf16[2,112,640]{2,1,0:T(8,128)(2,1)S(1)} %get-tuple-element.119), channel_id=1, source_target_pairs={{0,4},{2,6},{4,0},{6,2},{1,5},{3,7},{5,1},{7,3},{8,12},{10,14},{12... | collective-permute-start | bytes 860168 | tf_op jit(solution)/shard_map/ppermute | solution.py:23
  373.2 5.6 %collective-permute-start.49 = (bf16[128,1024]{1,0:T(8,128)(2,1)S(1)}, bf16[128,1024]{1,0:T(8,128)(2,1)S(1)}, u32[]{:S(2)}, u32[]{:S(2)}) collective-permute-start(bf16[128,1024]{1,0:T(8,128)(2,1)S(1)} %get-tuple-element.69), channel_id=1, source_target_pairs={{0,112},{16,0},{32,16},{48,32},{64,48},{80,64},{96,80},{112,96},{1... | collective-permute-start | bytes 786440 | tf_op jit(solution)/shard_map/ppermute | solution.py:23
  379.8 3.6 collective-permute-start.47
  383.4 5.3 %collective-permute-start.46 = (bf16[128,1024]{1,0:T(8,128)(2,1)S(1)}, bf16[128,1024]{1,0:T(8,128)(2,1)S(1)}, u32[]{:S(2)}, u32[]{:S(2)}) collective-permute-start(bf16[128,1024]{1,0:T(8,128)(2,1)S(1)} %get-tuple-element.72), channel_id=1, source_target_pairs={{0,64},{16,80},{32,96},{48,112},{64,0},{80,16},{96,32},{112,48},{1... | collective-permute-start | bytes 786440 | tf_op jit(solution)/shard_map/ppermute | solution.py:23
  392.4 9.4 %collective-permute-start.43 = (bf16[128,1024]{1,0:T(8,128)(2,1)S(1)}, bf16[128,1024]{1,0:T(8,128)(2,1)S(1)}, u32[]{:S(2)}, u32[]{:S(2)}) collective-permute-start(bf16[128,1024]{1,0:T(8,128)(2,1)S(1)} %get-tuple-element.68), channel_id=1, source_target_pairs={{0,16},{16,32},{32,48},{48,64},{64,80},{80,96},{96,112},{112,0},{1... | collective-permute-start | bytes 786440 | tf_op jit(solution)/shard_map/ppermute | solution.py:23
  405.7 5.0 %collective-permute-done.43 = bf16[128,1024]{1,0:T(8,128)(2,1)S(1)} collective-permute-done((bf16[128,1024]{1,0:T(8,128)(2,1)S(1)}, bf16[128,1024]{1,0:T(8,128)(2,1)S(1)}, u32[]{:S(2)}, u32[]{:S(2)}) %collective-permute-start.43) | collective-permute-done | bytes 262176 | tf_op jit(solution)/shard_map/ppermute | solution.py:23
  413.2 2.8 collective-permute-done.52
  417.9 3.5 collective-permute-done.53
  422.6 3.2 collective-permute-done.54
  432.0 8.7 %collective-permute-start.58 = (bf16[128,1024]{0,1:T(8,128)(2,1)S(1)}, bf16[128,1024]{0,1:T(8,128)(2,1)S(1)}, u32[]{:S(2)}, u32[]{:S(2)}) collective-permute-start(bf16[128,1024]{0,1:T(8,128)(2,1)S(1)} %constant_dynamic-update-slice_fusion.24), channel_id=1, source_target_pairs={{0,1},{1,0},{2,3},{3,2},{4,5},{5,4},{6,7},{7,6},{8,9},{9,8},{10,11... | collective-permute-start | bytes 786440 | tf_op jit(solution)/shard_map/ppermute | solution.py:23
  452.1 2.9 reshape.421
  457.1 2.9 reshape.422
  (391 shorter events, 155.8 us)
Async XLA Ops:
  0.6 34.5 %collective-permute-start.21 = (bf16[128,896]{1,0:T(8,128)(2,1)}, bf16[128,896]{1,0:T(8,128)(2,1)}, u32[]{:S(2)}, u32[]{:S(2)}) collective-permute-start(bf16[128,896]{1,0:T(8,128)(2,1)} %bitcast.35), channel_id=1, source_target_pairs={{0,112},{16,0},{32,16},{48,32},{64,48},{80,64},{96,80},{112,96},{1... | collective-permute-start | bytes 688136 | tf_op jit(solution)/shard_map/ppermute | solution.py:23
  5.2 33.2 %collective-permute-start.22 = (bf16[128,896]{1,0:T(8,128)(2,1)}, bf16[128,896]{1,0:T(8,128)(2,1)}, u32[]{:S(2)}, u32[]{:S(2)}) collective-permute-start(bf16[128,896]{1,0:T(8,128)(2,1)} %bitcast.35), channel_id=1, source_target_pairs={{0,96},{16,112},{32,0},{48,16},{64,32},{80,48},{96,64},{112,80},{1... | collective-permute-start | bytes 688136 | tf_op jit(solution)/shard_map/ppermute | solution.py:23
  5.7 35.5 %collective-permute-start.23 = (bf16[128,896]{1,0:T(8,128)(2,1)}, bf16[128,896]{1,0:T(8,128)(2,1)}, u32[]{:S(2)}, u32[]{:S(2)}) collective-permute-start(bf16[128,896]{1,0:T(8,128)(2,1)} %bitcast.35), channel_id=1, source_target_pairs={{0,80},{16,96},{32,112},{48,0},{64,16},{80,32},{96,48},{112,64},{1... | collective-permute-start | bytes 688136 | tf_op jit(solution)/shard_map/ppermute | solution.py:23
  5.8 37.0 %collective-permute-start.24 = (bf16[128,896]{1,0:T(8,128)(2,1)}, bf16[128,896]{1,0:T(8,128)(2,1)}, u32[]{:S(2)}, u32[]{:S(2)}) collective-permute-start(bf16[128,896]{1,0:T(8,128)(2,1)} %bitcast.35), channel_id=1, source_target_pairs={{0,64},{16,80},{32,96},{48,112},{64,0},{80,16},{96,32},{112,48},{1... | collective-permute-start | bytes 688136 | tf_op jit(solution)/shard_map/ppermute | solution.py:23
  8.4 36.1 %collective-permute-start.25 = (bf16[128,896]{1,0:T(8,128)(2,1)}, bf16[128,896]{1,0:T(8,128)(2,1)}, u32[]{:S(2)}, u32[]{:S(2)}) collective-permute-start(bf16[128,896]{1,0:T(8,128)(2,1)} %bitcast.35), channel_id=1, source_target_pairs={{0,48},{16,64},{32,80},{48,96},{64,112},{80,0},{96,16},{112,32},{1... | collective-permute-start | bytes 688136 | tf_op jit(solution)/shard_map/ppermute | solution.py:23
  14.6 32.7 %all-to-all-start = ((bf16[8,128,1152]{2,1,0:T(8,128)(2,1)}), bf16[8,128,1152]{2,1,0:T(8,128)(2,1)S(1)}, u32[]{:S(2)}, u32[]{:S(2)}) async-start(bf16[8,128,1152]{2,1,0:T(8,128)(2,1)} %broadcast_in_dim.35), calls=%async_computation | async-start | bytes 4718592 | tf_op jit(solution)/shard_map/all_to_all | solution.py:42
  35.2 39.1 %collective-permute-start.26 = (bf16[128,896]{1,0:T(8,128)(2,1)}, bf16[128,896]{1,0:T(8,128)(2,1)}, u32[]{:S(2)}, u32[]{:S(2)}) collective-permute-start(bf16[128,896]{1,0:T(8,128)(2,1)} %bitcast.35), channel_id=1, source_target_pairs={{0,32},{16,48},{32,64},{48,80},{64,96},{80,112},{96,0},{112,16},{1... | collective-permute-start | bytes 688136 | tf_op jit(solution)/shard_map/ppermute | solution.py:23
  38.4 76.2 %collective-permute-start.27 = (bf16[128,896]{1,0:T(8,128)(2,1)}, bf16[128,896]{1,0:T(8,128)(2,1)}, u32[]{:S(2)}, u32[]{:S(2)}) collective-permute-start(bf16[128,896]{1,0:T(8,128)(2,1)} %bitcast.35), channel_id=1, source_target_pairs={{0,16},{16,32},{32,48},{48,64},{64,80},{80,96},{96,112},{112,0},{1... | collective-permute-start | bytes 688136 | tf_op jit(solution)/shard_map/ppermute | solution.py:23
  49.2 51.5 %all-to-all-start.1 = ((bf16[8,112,896]{2,1,0:T(8,128)(2,1)}), bf16[8,112,896]{2,1,0:T(8,128)(2,1)S(1)}, u32[]{:S(2)}, u32[]{:S(2)}) async-start(bf16[8,112,896]{2,1,0:T(8,128)(2,1)} %broadcast_in_dim.38), calls=%async_computation.1 | async-start | bytes 3211264 | tf_op jit(solution)/shard_map/all_to_all | solution.py:42
  70.9 14.6 %collective-permute-start = (bf16[128,256]{1,0:T(8,128)(2,1)S(1)}, bf16[128,256]{1,0:T(8,128)(2,1)S(1)}, u32[]{:S(2)}, u32[]{:S(2)}) collective-permute-start(bf16[128,256]{1,0:T(8,128)(2,1)S(1)} %get-tuple-element.133), channel_id=1, source_target_pairs={{0,16},{16,32},{32,48},{48,64},{64,80},{80,96},{96,112},{1,17},{17... | collective-permute-start | bytes 196616 | tf_op jit(solution)/shard_map/ppermute | solution.py:210
  75.9 11.6 %collective-permute-start.1 = (bf16[128,256]{1,0:T(8,128)(2,1)S(1)}, bf16[128,256]{1,0:T(8,128)(2,1)S(1)}, u32[]{:S(2)}, u32[]{:S(2)}) collective-permute-start(bf16[128,256]{1,0:T(8,128)(2,1)S(1)} %get-tuple-element.133), channel_id=1, source_target_pairs={{0,32},{16,48},{32,64},{48,80},{64,96},{80,112},{1,33},{17,49},{33... | collective-permute-start | bytes 196616 | tf_op jit(solution)/shard_map/ppermute | solution.py:210
  79.0 10.4 %collective-permute-start.2 = (bf16[128,256]{1,0:T(8,128)(2,1)S(1)}, bf16[128,256]{1,0:T(8,128)(2,1)S(1)}, u32[]{:S(2)}, u32[]{:S(2)}) collective-permute-start(bf16[128,256]{1,0:T(8,128)(2,1)S(1)} %get-tuple-element.133), channel_id=1, source_target_pairs={{0,48},{16,64},{32,80},{48,96},{64,112},{1,49},{17,65},{33,81},{49... | collective-permute-start | bytes 196616 | tf_op jit(solution)/shard_map/ppermute | solution.py:210
  82.7 8.9 %collective-permute-start.3 = (bf16[128,256]{1,0:T(8,128)(2,1)S(1)}, bf16[128,256]{1,0:T(8,128)(2,1)S(1)}, u32[]{:S(2)}, u32[]{:S(2)}) collective-permute-start(bf16[128,256]{1,0:T(8,128)(2,1)S(1)} %get-tuple-element.133), channel_id=1, source_target_pairs={{0,64},{16,80},{32,96},{48,112},{1,65},{17,81},{33,97},{49,113},{2... | collective-permute-start | bytes 196616 | tf_op jit(solution)/shard_map/ppermute | solution.py:210
  100.8 47.6 %all-to-all-start.2 = ((bf16[8,112,1280]{2,1,0:T(8,128)(2,1)}), bf16[8,112,1280]{2,1,0:T(8,128)(2,1)}, u32[]{:S(2)}, u32[]{:S(2)}) async-start(bf16[8,112,1280]{2,1,0:T(8,128)(2,1)} %copy.112), calls=%async_computation.2 | async-start | bytes 4587520 | tf_op jit(solution)/shard_map/all_to_all | solution.py:196
  111.1 19.6 %collective-permute-start.7 = (bf16[128,896]{1,0:T(8,128)(2,1)S(1)}, bf16[128,896]{1,0:T(8,128)(2,1)S(1)}, u32[]{:S(2)}, u32[]{:S(2)}) collective-permute-start(bf16[128,896]{1,0:T(8,128)(2,1)S(1)} %get-tuple-element.62), channel_id=1, source_target_pairs={{0,112},{16,0},{32,16},{48,32},{64,48},{80,64},{96,80},{112,96},{1... | collective-permute-start | bytes 688136 | tf_op jit(solution)/shard_map/ppermute | solution.py:23
  116.2 19.7 %collective-permute-start.8 = (bf16[128,896]{1,0:T(8,128)(2,1)S(1)}, bf16[128,896]{1,0:T(8,128)(2,1)S(1)}, u32[]{:S(2)}, u32[]{:S(2)}) collective-permute-start(bf16[128,896]{1,0:T(8,128)(2,1)S(1)} %get-tuple-element.62), channel_id=1, source_target_pairs={{0,96},{16,112},{32,0},{48,16},{64,32},{80,48},{96,64},{112,80},{1... | collective-permute-start | bytes 688136 | tf_op jit(solution)/shard_map/ppermute | solution.py:23
  116.8 25.1 %collective-permute-start.9 = (bf16[128,896]{1,0:T(8,128)(2,1)S(1)}, bf16[128,896]{1,0:T(8,128)(2,1)S(1)}, u32[]{:S(2)}, u32[]{:S(2)}) collective-permute-start(bf16[128,896]{1,0:T(8,128)(2,1)S(1)} %get-tuple-element.62), channel_id=1, source_target_pairs={{0,80},{16,96},{32,112},{48,0},{64,16},{80,32},{96,48},{112,64},{1... | collective-permute-start | bytes 688136 | tf_op jit(solution)/shard_map/ppermute | solution.py:23
  117.0 25.5 %collective-permute-start.10 = (bf16[128,896]{1,0:T(8,128)(2,1)S(1)}, bf16[128,896]{1,0:T(8,128)(2,1)S(1)}, u32[]{:S(2)}, u32[]{:S(2)}) collective-permute-start(bf16[128,896]{1,0:T(8,128)(2,1)S(1)} %get-tuple-element.62), channel_id=1, source_target_pairs={{0,64},{16,80},{32,96},{48,112},{64,0},{80,16},{96,32},{112,48},{1... | collective-permute-start | bytes 688136 | tf_op jit(solution)/shard_map/ppermute | solution.py:23
  119.4 23.8 %collective-permute-start.11 = (bf16[128,896]{1,0:T(8,128)(2,1)S(1)}, bf16[128,896]{1,0:T(8,128)(2,1)S(1)}, u32[]{:S(2)}, u32[]{:S(2)}) collective-permute-start(bf16[128,896]{1,0:T(8,128)(2,1)S(1)} %get-tuple-element.62), channel_id=1, source_target_pairs={{0,48},{16,64},{32,80},{48,96},{64,112},{80,0},{96,16},{112,32},{1... | collective-permute-start | bytes 688136 | tf_op jit(solution)/shard_map/ppermute | solution.py:23
  130.6 14.0 %collective-permute-start.12 = (bf16[128,896]{1,0:T(8,128)(2,1)S(1)}, bf16[128,896]{1,0:T(8,128)(2,1)S(1)}, u32[]{:S(2)}, u32[]{:S(2)}) collective-permute-start(bf16[128,896]{1,0:T(8,128)(2,1)S(1)} %get-tuple-element.62), channel_id=1, source_target_pairs={{0,32},{16,48},{32,64},{48,80},{64,96},{80,112},{96,0},{112,16},{1... | collective-permute-start | bytes 688136 | tf_op jit(solution)/shard_map/ppermute | solution.py:23
  135.9 11.8 %collective-permute-start.13 = (bf16[128,896]{1,0:T(8,128)(2,1)S(1)}, bf16[128,896]{1,0:T(8,128)(2,1)S(1)}, u32[]{:S(2)}, u32[]{:S(2)}) collective-permute-start(bf16[128,896]{1,0:T(8,128)(2,1)S(1)} %get-tuple-element.62), channel_id=1, source_target_pairs={{0,16},{16,32},{32,48},{48,64},{64,80},{80,96},{96,112},{112,0},{1... | collective-permute-start | bytes 688136 | tf_op jit(solution)/shard_map/ppermute | solution.py:23
  171.7 15.0 %collective-permute-start.34 = (bf16[128,896]{1,0:T(8,128)(2,1)S(1)}, bf16[128,896]{1,0:T(8,128)(2,1)S(1)}, u32[]{:S(2)}, u32[]{:S(2)}) collective-permute-start(bf16[128,896]{1,0:T(8,128)(2,1)S(1)} %get-tuple-element.76), channel_id=1, source_target_pairs={{0,112},{16,0},{32,16},{48,32},{64,48},{80,64},{96,80},{112,96},{1... | collective-permute-start | bytes 688136 | tf_op jit(solution)/shard_map/ppermute | solution.py:23
  178.5 10.3 %collective-permute-start.33 = (bf16[128,896]{1,0:T(8,128)(2,1)S(1)}, bf16[128,896]{1,0:T(8,128)(2,1)S(1)}, u32[]{:S(2)}, u32[]{:S(2)}) collective-permute-start(bf16[128,896]{1,0:T(8,128)(2,1)S(1)} %get-tuple-element.77), channel_id=1, source_target_pairs={{0,96},{16,112},{32,0},{48,16},{64,32},{80,48},{96,64},{112,80},{1... | collective-permute-start | bytes 688136 | tf_op jit(solution)/shard_map/ppermute | solution.py:23
  178.5 16.9 %collective-permute-start.32 = (bf16[128,896]{1,0:T(8,128)(2,1)S(1)}, bf16[128,896]{1,0:T(8,128)(2,1)S(1)}, u32[]{:S(2)}, u32[]{:S(2)}) collective-permute-start(bf16[128,896]{1,0:T(8,128)(2,1)S(1)} %get-tuple-element.78), channel_id=1, source_target_pairs={{0,80},{16,96},{32,112},{48,0},{64,16},{80,32},{96,48},{112,64},{1... | collective-permute-start | bytes 688136 | tf_op jit(solution)/shard_map/ppermute | solution.py:23
  179.7 19.0 %collective-permute-start.31 = (bf16[128,896]{1,0:T(8,128)(2,1)S(1)}, bf16[128,896]{1,0:T(8,128)(2,1)S(1)}, u32[]{:S(2)}, u32[]{:S(2)}) collective-permute-start(bf16[128,896]{1,0:T(8,128)(2,1)S(1)} %get-tuple-element.79), channel_id=1, source_target_pairs={{0,64},{16,80},{32,96},{48,112},{64,0},{80,16},{96,32},{112,48},{1... | collective-permute-start | bytes 688136 | tf_op jit(solution)/shard_map/ppermute | solution.py:23
  181.5 19.6 %collective-permute-start.30 = (bf16[128,896]{1,0:T(8,128)(2,1)S(1)}, bf16[128,896]{1,0:T(8,128)(2,1)S(1)}, u32[]{:S(2)}, u32[]{:S(2)}) collective-permute-start(bf16[128,896]{1,0:T(8,128)(2,1)S(1)} %get-tuple-element.80), channel_id=1, source_target_pairs={{0,48},{16,64},{32,80},{48,96},{64,112},{80,0},{96,16},{112,32},{1... | collective-permute-start | bytes 688136 | tf_op jit(solution)/shard_map/ppermute | solution.py:23
  186.8 16.7 %collective-permute-start.29 = (bf16[128,896]{1,0:T(8,128)(2,1)S(1)}, bf16[128,896]{1,0:T(8,128)(2,1)S(1)}, u32[]{:S(2)}, u32[]{:S(2)}) collective-permute-start(bf16[128,896]{1,0:T(8,128)(2,1)S(1)} %get-tuple-element.81), channel_id=1, source_target_pairs={{0,32},{16,48},{32,64},{48,80},{64,96},{80,112},{96,0},{112,16},{1... | collective-permute-start | bytes 688136 | tf_op jit(solution)/shard_map/ppermute | solution.py:23
  188.7 15.3 %collective-permute-start.28 = (bf16[128,896]{1,0:T(8,128)(2,1)S(1)}, bf16[128,896]{1,0:T(8,128)(2,1)S(1)}, u32[]{:S(2)}, u32[]{:S(2)}) collective-permute-start(bf16[128,896]{1,0:T(8,128)(2,1)S(1)} %get-tuple-element.75), channel_id=1, source_target_pairs={{0,16},{16,32},{32,48},{48,64},{64,80},{80,96},{96,112},{112,0},{1... | collective-permute-start | bytes 688136 | tf_op jit(solution)/shard_map/ppermute | solution.py:23
  195.4 9.6 %collective-permute-start.20 = (bf16[128,896]{1,0:T(8,128)(2,1)S(1)}, bf16[128,896]{1,0:T(8,128)(2,1)S(1)}, u32[]{:S(2)}, u32[]{:S(2)}) collective-permute-start(bf16[128,896]{1,0:T(8,128)(2,1)S(1)} %get-tuple-element.83), channel_id=1, source_target_pairs={{0,112},{16,0},{32,16},{48,32},{64,48},{80,64},{96,80},{112,96},{1... | collective-permute-start | bytes 688136 | tf_op jit(solution)/shard_map/ppermute | solution.py:23
  198.7 10.3 %collective-permute-start.19 = (bf16[128,896]{1,0:T(8,128)(2,1)S(1)}, bf16[128,896]{1,0:T(8,128)(2,1)S(1)}, u32[]{:S(2)}, u32[]{:S(2)}) collective-permute-start(bf16[128,896]{1,0:T(8,128)(2,1)S(1)} %get-tuple-element.84), channel_id=1, source_target_pairs={{0,96},{16,112},{32,0},{48,16},{64,32},{80,48},{96,64},{112,80},{1... | collective-permute-start | bytes 688136 | tf_op jit(solution)/shard_map/ppermute | solution.py:23
  201.2 12.5 %collective-permute-start.18 = (bf16[128,896]{1,0:T(8,128)(2,1)S(1)}, bf16[128,896]{1,0:T(8,128)(2,1)S(1)}, u32[]{:S(2)}, u32[]{:S(2)}) collective-permute-start(bf16[128,896]{1,0:T(8,128)(2,1)S(1)} %get-tuple-element.85), channel_id=1, source_target_pairs={{0,80},{16,96},{32,112},{48,0},{64,16},{80,32},{96,48},{112,64},{1... | collective-permute-start | bytes 688136 | tf_op jit(solution)/shard_map/ppermute | solution.py:23
  203.5 10.7 %collective-permute-start.17 = (bf16[128,896]{1,0:T(8,128)(2,1)S(1)}, bf16[128,896]{1,0:T(8,128)(2,1)S(1)}, u32[]{:S(2)}, u32[]{:S(2)}) collective-permute-start(bf16[128,896]{1,0:T(8,128)(2,1)S(1)} %get-tuple-element.86), channel_id=1, source_target_pairs={{0,64},{16,80},{32,96},{48,112},{64,0},{80,16},{96,32},{112,48},{1... | collective-permute-start | bytes 688136 | tf_op jit(solution)/shard_map/ppermute | solution.py:23
  204.1 10.5 %collective-permute-start.16 = (bf16[128,896]{1,0:T(8,128)(2,1)S(1)}, bf16[128,896]{1,0:T(8,128)(2,1)S(1)}, u32[]{:S(2)}, u32[]{:S(2)}) collective-permute-start(bf16[128,896]{1,0:T(8,128)(2,1)S(1)} %get-tuple-element.87), channel_id=1, source_target_pairs={{0,48},{16,64},{32,80},{48,96},{64,112},{80,0},{96,16},{112,32},{1... | collective-permute-start | bytes 688136 | tf_op jit(solution)/shard_map/ppermute | solution.py:23
  205.0 20.0 %collective-permute-start.15 = (bf16[128,896]{1,0:T(8,128)(2,1)S(1)}, bf16[128,896]{1,0:T(8,128)(2,1)S(1)}, u32[]{:S(2)}, u32[]{:S(2)}) collective-permute-start(bf16[128,896]{1,0:T(8,128)(2,1)S(1)} %get-tuple-element.88), channel_id=1, source_target_pairs={{0,32},{16,48},{32,64},{48,80},{64,96},{80,112},{96,0},{112,16},{1... | collective-permute-start | bytes 688136 | tf_op jit(solution)/shard_map/ppermute | solution.py:23
  209.0 16.1 %collective-permute-start.14 = (bf16[128,896]{1,0:T(8,128)(2,1)S(1)}, bf16[128,896]{1,0:T(8,128)(2,1)S(1)}, u32[]{:S(2)}, u32[]{:S(2)}) collective-permute-start(bf16[128,896]{1,0:T(8,128)(2,1)S(1)} %get-tuple-element.82), channel_id=1, source_target_pairs={{0,16},{16,32},{32,48},{48,64},{64,80},{80,96},{96,112},{112,0},{1... | collective-permute-start | bytes 688136 | tf_op jit(solution)/shard_map/ppermute | solution.py:23
  251.2 9.2 %collective-permute-start.41 = (bf16[128,256]{0,1:T(8,128)(2,1)S(1)}, bf16[128,256]{0,1:T(8,128)(2,1)S(1)}, u32[]{:S(2)}, u32[]{:S(2)}) collective-permute-start(bf16[128,256]{0,1:T(8,128)(2,1)S(1)} %get-tuple-element.106), channel_id=1, source_target_pairs={{112,0},{113,1},{114,2},{115,3},{116,4},{117,5},{118,6},{119,7},{1... | collective-permute-start | bytes 196616 | tf_op jit(solution)/shard_map/ppermute | solution.py:279
  252.7 9.0 %collective-permute-start.40 = (bf16[128,256]{0,1:T(8,128)(2,1)S(1)}, bf16[128,256]{0,1:T(8,128)(2,1)S(1)}, u32[]{:S(2)}, u32[]{:S(2)}) collective-permute-start(bf16[128,256]{0,1:T(8,128)(2,1)S(1)} %get-tuple-element.107), channel_id=1, source_target_pairs={{96,0},{112,16},{97,1},{113,17},{98,2},{114,18},{99,3},{115,19},{1... | collective-permute-start | bytes 196616 | tf_op jit(solution)/shard_map/ppermute | solution.py:279
  256.5 19.2 %collective-permute-start.39 = (bf16[128,256]{0,1:T(8,128)(2,1)S(1)}, bf16[128,256]{0,1:T(8,128)(2,1)S(1)}, u32[]{:S(2)}, u32[]{:S(2)}) collective-permute-start(bf16[128,256]{0,1:T(8,128)(2,1)S(1)} %get-tuple-element.108), channel_id=1, source_target_pairs={{80,0},{96,16},{112,32},{81,1},{97,17},{113,33},{82,2},{98,18},{11... | collective-permute-start | bytes 196616 | tf_op jit(solution)/shard_map/ppermute | solution.py:279
  257.8 21.6 %collective-permute-start.38 = (bf16[128,256]{0,1:T(8,128)(2,1)S(1)}, bf16[128,256]{0,1:T(8,128)(2,1)S(1)}, u32[]{:S(2)}, u32[]{:S(2)}) collective-permute-start(bf16[128,256]{0,1:T(8,128)(2,1)S(1)} %get-tuple-element.109), channel_id=1, source_target_pairs={{64,0},{80,16},{96,32},{112,48},{65,1},{81,17},{97,33},{113,49},{6... | collective-permute-start | bytes 196616 | tf_op jit(solution)/shard_map/ppermute | solution.py:279
  259.1 20.4 %collective-permute-start.37 = (bf16[128,256]{0,1:T(8,128)(2,1)S(1)}, bf16[128,256]{0,1:T(8,128)(2,1)S(1)}, u32[]{:S(2)}, u32[]{:S(2)}) collective-permute-start(bf16[128,256]{0,1:T(8,128)(2,1)S(1)} %get-tuple-element.110), channel_id=1, source_target_pairs={{48,0},{64,16},{80,32},{96,48},{112,64},{49,1},{65,17},{81,33},{97... | collective-permute-start | bytes 196616 | tf_op jit(solution)/shard_map/ppermute | solution.py:279
  260.4 19.1 %collective-permute-start.36 = (bf16[128,256]{0,1:T(8,128)(2,1)S(1)}, bf16[128,256]{0,1:T(8,128)(2,1)S(1)}, u32[]{:S(2)}, u32[]{:S(2)}) collective-permute-start(bf16[128,256]{0,1:T(8,128)(2,1)S(1)} %get-tuple-element.111), channel_id=1, source_target_pairs={{32,0},{48,16},{64,32},{80,48},{96,64},{112,80},{33,1},{49,17},{65... | collective-permute-start | bytes 196616 | tf_op jit(solution)/shard_map/ppermute | solution.py:279
  261.7 17.8 %collective-permute-start.35 = (bf16[128,256]{0,1:T(8,128)(2,1)S(1)}, bf16[128,256]{0,1:T(8,128)(2,1)S(1)}, u32[]{:S(2)}, u32[]{:S(2)}) collective-permute-start(bf16[128,256]{0,1:T(8,128)(2,1)S(1)} %get-tuple-element.105), channel_id=1, source_target_pairs={{16,0},{32,16},{48,32},{64,48},{80,64},{96,80},{112,96},{17,1},{33... | collective-permute-start | bytes 196616 | tf_op jit(solution)/shard_map/ppermute | solution.py:279
  275.7 48.6 %collective-permute-start.59 = (bf16[896,640]{1,0:T(8,128)(2,1)}, bf16[896,640]{1,0:T(8,128)(2,1)}, u32[]{:S(2)}, u32[]{:S(2)}) collective-permute-start(bf16[896,640]{1,0:T(8,128)(2,1)} %get-tuple-element.149), channel_id=1, source_target_pairs={{0,1},{1,0},{2,3},{3,2},{4,5},{5,4},{6,7},{7,6},{8,9},{9,8},{10,11... | collective-permute-start | bytes 3440648 | tf_op jit(solution)/shard_map/ppermute | solution.py:23
  279.4 17.8 %collective-permute-start.70 = (bf16[320,896]{1,0:T(8,128)(2,1)}, bf16[320,896]{1,0:T(8,128)(2,1)}, u32[]{:S(2)}, u32[]{:S(2)}) collective-permute-start(bf16[320,896]{1,0:T(8,128)(2,1)} %select_convert_fusion.2), channel_id=1, source_target_pairs={{0,1},{1,0},{2,3},{3,2},{4,5},{5,4},{6,7},{7,6},{8,9},{9,8},{10,11... | collective-permute-start | bytes 1720328 | tf_op jit(solution)/shard_map/ppermute | solution.py:23
  298.5 8.0 %collective-permute-start.73 = (bf16[2,40,896]{2,1,0:T(8,128)(2,1)S(1)}, bf16[2,40,896]{2,1,0:T(8,128)(2,1)S(1)}, u32[]{:S(2)}, u32[]{:S(2)}) collective-permute-start(bf16[2,40,896]{2,1,0:T(8,128)(2,1)S(1)} %get-tuple-element.95), channel_id=1, source_target_pairs={{0,4},{2,6},{4,0},{6,2},{1,5},{3,7},{5,1},{7,3},{8,12},{10,14},{12... | collective-permute-start | bytes 430088 | tf_op jit(solution)/shard_map/ppermute | solution.py:23
  312.5 59.2 %collective-permute-start.42 = (bf16[8,128,1024]{2,1,0:T(8,128)(2,1)S(1)}, bf16[8,128,1024]{2,1,0:T(8,128)(2,1)S(1)}, u32[]{:S(2)}, u32[]{:S(2)}) collective-permute-start(bf16[8,128,1024]{2,1,0:T(8,128)(2,1)S(1)} %select_convert_fusion), channel_id=1, source_target_pairs={{0,1},{1,0},{2,3},{3,2},{4,5},{5,4},{6,7},{7,6},{8,9},{9,8},{10,11... | collective-permute-start | bytes 6291464 | tf_op jit(solution)/shard_map/ppermute | solution.py:23
  320.3 9.0 %collective-permute-start.77 = (bf16[2,40,896]{2,1,0:T(8,128)(2,1)S(1)}, bf16[2,40,896]{2,1,0:T(8,128)(2,1)S(1)}, u32[]{:S(2)}, u32[]{:S(2)}) collective-permute-start(bf16[2,40,896]{2,1,0:T(8,128)(2,1)S(1)} %get-tuple-element.126), channel_id=1, source_target_pairs={{0,4},{2,6},{4,0},{6,2},{1,5},{3,7},{5,1},{7,3},{8,12},{10,14},{12... | collective-permute-start | bytes 430088 | tf_op jit(solution)/shard_map/ppermute | solution.py:23
  326.1 7.9 %collective-permute-start.62 = (bf16[2,112,640]{2,1,0:T(8,128)(2,1)S(1)}, bf16[2,112,640]{2,1,0:T(8,128)(2,1)S(1)}, u32[]{:S(2)}, u32[]{:S(2)}) collective-permute-start(bf16[2,112,640]{2,1,0:T(8,128)(2,1)S(1)} %get-tuple-element.92), channel_id=1, source_target_pairs={{0,4},{2,6},{4,0},{6,2},{1,5},{3,7},{5,1},{7,3},{8,12},{10,14},{12... | collective-permute-start | bytes 860168 | tf_op jit(solution)/shard_map/ppermute | solution.py:23
  326.7 14.3 %collective-permute-start.61 = (bf16[2,112,640]{2,1,0:T(8,128)(2,1)S(1)}, bf16[2,112,640]{2,1,0:T(8,128)(2,1)S(1)}, u32[]{:S(2)}, u32[]{:S(2)}) collective-permute-start(bf16[2,112,640]{2,1,0:T(8,128)(2,1)S(1)} %get-tuple-element.93), channel_id=1, source_target_pairs={{0,6},{2,0},{4,2},{6,4},{1,7},{3,1},{5,3},{7,5},{8,14},{10,8},{12,... | collective-permute-start | bytes 860168 | tf_op jit(solution)/shard_map/ppermute | solution.py:23
  329.3 12.0 %collective-permute-start.60 = (bf16[2,112,640]{2,1,0:T(8,128)(2,1)S(1)}, bf16[2,112,640]{2,1,0:T(8,128)(2,1)S(1)}, u32[]{:S(2)}, u32[]{:S(2)}) collective-permute-start(bf16[2,112,640]{2,1,0:T(8,128)(2,1)S(1)} %get-tuple-element.91), channel_id=1, source_target_pairs={{0,2},{2,4},{4,6},{6,0},{1,3},{3,5},{5,7},{7,1},{8,10},{10,12},{12... | collective-permute-start | bytes 860168 | tf_op jit(solution)/shard_map/ppermute | solution.py:23
  348.2 14.7 %collective-permute-start.65 = (bf16[112,640]{1,0:T(8,128)(2,1)S(1)}, bf16[112,640]{1,0:T(8,128)(2,1)S(1)}, u32[]{:S(2)}, u32[]{:S(2)}) collective-permute-start(bf16[112,640]{1,0:T(8,128)(2,1)S(1)} %collective-permute-done.64), channel_id=1, source_target_pairs={{0,8},{8,0},{1,9},{9,1},{2,10},{10,2},{3,11},{11,3},{4,12},{12,4},... | collective-permute-start | bytes 430088 | tf_op jit(solution)/shard_map/ppermute | solution.py:23
  356.1 22.6 %collective-permute-start.79 = (bf16[320,896]{1,0:T(8,128)(2,1)S(1)}, bf16[320,896]{1,0:T(8,128)(2,1)S(1)}, u32[]{:S(2)}, u32[]{:S(2)}) collective-permute-start(bf16[320,896]{1,0:T(8,128)(2,1)S(1)} %constant_dynamic-update-slice_fusion.32), channel_id=1, source_target_pairs={{0,1},{1,0},{2,3},{3,2},{4,5},{5,4},{6,7},{7,6},{8,9},{9,8},{10,11... | collective-permute-start | bytes 1720328 | tf_op jit(solution)/shard_map/ppermute | solution.py:23
  363.0 16.8 %collective-permute-start.68 = (bf16[2,112,640]{2,1,0:T(8,128)(2,1)S(1)}, bf16[2,112,640]{2,1,0:T(8,128)(2,1)S(1)}, u32[]{:S(2)}, u32[]{:S(2)}) collective-permute-start(bf16[2,112,640]{2,1,0:T(8,128)(2,1)S(1)} %get-tuple-element.119), channel_id=1, source_target_pairs={{0,2},{2,4},{4,6},{6,0},{1,3},{3,5},{5,7},{7,1},{8,10},{10,12},{12... | collective-permute-start | bytes 860168 | tf_op jit(solution)/shard_map/ppermute | solution.py:23
  365.4 18.0 %collective-permute-start.67 = (bf16[2,112,640]{2,1,0:T(8,128)(2,1)S(1)}, bf16[2,112,640]{2,1,0:T(8,128)(2,1)S(1)}, u32[]{:S(2)}, u32[]{:S(2)}) collective-permute-start(bf16[2,112,640]{2,1,0:T(8,128)(2,1)S(1)} %get-tuple-element.119), channel_id=1, source_target_pairs={{0,4},{2,6},{4,0},{6,2},{1,5},{3,7},{5,1},{7,3},{8,12},{10,14},{12... | collective-permute-start | bytes 860168 | tf_op jit(solution)/shard_map/ppermute | solution.py:23
  371.1 17.6 %collective-permute-start.66 = (bf16[2,112,640]{2,1,0:T(8,128)(2,1)S(1)}, bf16[2,112,640]{2,1,0:T(8,128)(2,1)S(1)}, u32[]{:S(2)}, u32[]{:S(2)}) collective-permute-start(bf16[2,112,640]{2,1,0:T(8,128)(2,1)S(1)} %get-tuple-element.119), channel_id=1, source_target_pairs={{0,6},{2,0},{4,2},{6,4},{1,7},{3,1},{5,3},{7,5},{8,14},{10,8},{12,... | collective-permute-start | bytes 860168 | tf_op jit(solution)/shard_map/ppermute | solution.py:23
  373.2 17.3 %collective-permute-start.49 = (bf16[128,1024]{1,0:T(8,128)(2,1)S(1)}, bf16[128,1024]{1,0:T(8,128)(2,1)S(1)}, u32[]{:S(2)}, u32[]{:S(2)}) collective-permute-start(bf16[128,1024]{1,0:T(8,128)(2,1)S(1)} %get-tuple-element.69), channel_id=1, source_target_pairs={{0,112},{16,0},{32,16},{48,32},{64,48},{80,64},{96,80},{112,96},{1... | collective-permute-start | bytes 786440 | tf_op jit(solution)/shard_map/ppermute | solution.py:23
  378.7 13.7 %collective-permute-start.48 = (bf16[128,1024]{1,0:T(8,128)(2,1)S(1)}, bf16[128,1024]{1,0:T(8,128)(2,1)S(1)}, u32[]{:S(2)}, u32[]{:S(2)}) collective-permute-start(bf16[128,1024]{1,0:T(8,128)(2,1)S(1)} %get-tuple-element.70), channel_id=1, source_target_pairs={{0,96},{16,112},{32,0},{48,16},{64,32},{80,48},{96,64},{112,80},{1... | collective-permute-start | bytes 786440 | tf_op jit(solution)/shard_map/ppermute | solution.py:23
  379.8 23.8 %collective-permute-start.47 = (bf16[128,1024]{1,0:T(8,128)(2,1)S(1)}, bf16[128,1024]{1,0:T(8,128)(2,1)S(1)}, u32[]{:S(2)}, u32[]{:S(2)}) collective-permute-start(bf16[128,1024]{1,0:T(8,128)(2,1)S(1)} %get-tuple-element.71), channel_id=1, source_target_pairs={{0,80},{16,96},{32,112},{48,0},{64,16},{80,32},{96,48},{112,64},{1... | collective-permute-start | bytes 786440 | tf_op jit(solution)/shard_map/ppermute | solution.py:23
  383.4 20.2 %collective-permute-start.46 = (bf16[128,1024]{1,0:T(8,128)(2,1)S(1)}, bf16[128,1024]{1,0:T(8,128)(2,1)S(1)}, u32[]{:S(2)}, u32[]{:S(2)}) collective-permute-start(bf16[128,1024]{1,0:T(8,128)(2,1)S(1)} %get-tuple-element.72), channel_id=1, source_target_pairs={{0,64},{16,80},{32,96},{48,112},{64,0},{80,16},{96,32},{112,48},{1... | collective-permute-start | bytes 786440 | tf_op jit(solution)/shard_map/ppermute | solution.py:23
  388.7 14.9 %collective-permute-start.45 = (bf16[128,1024]{1,0:T(8,128)(2,1)S(1)}, bf16[128,1024]{1,0:T(8,128)(2,1)S(1)}, u32[]{:S(2)}, u32[]{:S(2)}) collective-permute-start(bf16[128,1024]{1,0:T(8,128)(2,1)S(1)} %get-tuple-element.73), channel_id=1, source_target_pairs={{0,48},{16,64},{32,80},{48,96},{64,112},{80,0},{96,16},{112,32},{1... | collective-permute-start | bytes 786440 | tf_op jit(solution)/shard_map/ppermute | solution.py:23
  390.4 15.2 %collective-permute-start.44 = (bf16[128,1024]{1,0:T(8,128)(2,1)S(1)}, bf16[128,1024]{1,0:T(8,128)(2,1)S(1)}, u32[]{:S(2)}, u32[]{:S(2)}) collective-permute-start(bf16[128,1024]{1,0:T(8,128)(2,1)S(1)} %get-tuple-element.74), channel_id=1, source_target_pairs={{0,32},{16,48},{32,64},{48,80},{64,96},{80,112},{96,0},{112,16},{1... | collective-permute-start | bytes 786440 | tf_op jit(solution)/shard_map/ppermute | solution.py:23
  392.4 18.2 %collective-permute-start.43 = (bf16[128,1024]{1,0:T(8,128)(2,1)S(1)}, bf16[128,1024]{1,0:T(8,128)(2,1)S(1)}, u32[]{:S(2)}, u32[]{:S(2)}) collective-permute-start(bf16[128,1024]{1,0:T(8,128)(2,1)S(1)} %get-tuple-element.68), channel_id=1, source_target_pairs={{0,16},{16,32},{32,48},{48,64},{64,80},{80,96},{96,112},{112,0},{1... | collective-permute-start | bytes 786440 | tf_op jit(solution)/shard_map/ppermute | solution.py:23
  432.0 9.8 %collective-permute-start.58 = (bf16[128,1024]{0,1:T(8,128)(2,1)S(1)}, bf16[128,1024]{0,1:T(8,128)(2,1)S(1)}, u32[]{:S(2)}, u32[]{:S(2)}) collective-permute-start(bf16[128,1024]{0,1:T(8,128)(2,1)S(1)} %constant_dynamic-update-slice_fusion.24), channel_id=1, source_target_pairs={{0,1},{1,0},{2,3},{3,2},{4,5},{5,4},{6,7},{7,6},{8,9},{9,8},{10,11... | collective-permute-start | bytes 786440 | tf_op jit(solution)/shard_map/ppermute | solution.py:23
  440.7 7.7 %collective-permute-start.69 = (bf16[8,112,640]{2,1,0:T(8,128)(2,1)S(1)}, bf16[8,112,640]{2,1,0:T(8,128)(2,1)}, u32[]{:S(2)}, u32[]{:S(2)}) collective-permute-start(bf16[8,112,640]{2,1,0:T(8,128)(2,1)S(1)} %fusion.72), channel_id=1, source_target_pairs={{0,1},{1,0},{2,3},{3,2},{4,5},{5,4},{6,7},{7,6},{8,9},{9,8},{10,11... | collective-permute-start | bytes 3440648 | tf_op jit(solution)/shard_map/ppermute | solution.py:23
  (60 other events, 562.8 us)

commit v2 on v1

v2 whole, which is shorter than its diff:
```python
import jax
import jax.numpy as jnp
from jax import lax
from jax.experimental import pallas as pl
from jax.experimental.pallas import tpu as pltpu
from jax.sharding import Mesh
from jax.sharding import PartitionSpec as P

KV_HEADS = 2
HEAD_DIM = 64
EPS = 1e-06
THETA = 1000000.0
MASKED_SCORE = -1e30
GROUP = ("y", "xl")
SPREAD = ("z", "xh")
REPLICA = ("xh", "z", "c")
SIZES = (4, 2, 2, 4, 2)
AXES = ("y", "xl", "xh", "z", "c")
N = 8
PAD = 640
HALF = 64
BF = jnp.bfloat16
F32 = jnp.float32


def shift(array, axis, by, size):
    return lax.ppermute(array, axis, [(i, (i + by) % size) for i in range(size)])


def exchange(blocks, axis):
    return lax.all_to_all(blocks, axis, 0, 0, tiled=True)


def to_all(array, axis):
    return exchange(jnp.broadcast_to(array, (N, *array.shape)), axis)


def sum_at(blocks, axis):
    return jnp.sum(exchange(blocks, axis).astype(F32), axis=0)


def at(blocks, index):
    return lax.dynamic_index_in_dim(blocks, index, 0, keepdims=False)


def turn_half(values_in):
    half_size = values_in.shape[-1] // 2
    return jnp.concatenate([-values_in[..., half_size:], values_in[..., :half_size]], axis=-1)


def rotate(values_in, cosine_table, sine_table):
    return values_in * cosine_table + turn_half(values_in) * sine_table


def rotate_back(gradient, cosine_table, sine_table):
    return gradient * cosine_table - turn_half(gradient * sine_table)


def norm_forward(stream, gain):
    scale = lax.rsqrt(jnp.mean(stream * stream, axis=-1, keepdims=True) + EPS)
    return stream * scale * gain, scale


def norm_backward(stream, scale, gain, gradient):
    normalized = stream * scale
    scaled = gradient * gain
    gain_grad = jnp.sum(gradient * normalized, axis=0)
    grad = scale * (scaled - normalized * jnp.mean(scaled * normalized, axis=-1, keepdims=True))
    return grad, gain_grad


def mm(a, b):
    return jnp.dot(a, b, preferred_element_type=F32)


def mm_t(a, b):
    return lax.dot_general(a, b, (((1,), (1,)), ((), ())), preferred_element_type=F32)


def outer(a, b):
    return lax.dot_general(a, b, (((0,), (0,)), ((), ())), preferred_element_type=F32)


def core_sum(first, second, c):
    low = c == 0
    keep = jnp.where(low, first, second)
    send = jnp.where(low, second, first).astype(BF)
    return (keep + shift(send, "c", 1, 2).astype(F32)).astype(BF)


def core_pair(own, c):
    other = shift(own, "c", 1, 2)
    low = c == 0
    return jnp.where(low, own, other), jnp.where(low, other, own)


def pack_units(w_ref, packed_ref):
    units = w_ref.shape[1] // N
    packed_ref[...] = jnp.zeros_like(packed_ref)
    for j in range(N):
        packed_ref[j, :, :units] = w_ref[:, j * units : (j + 1) * units]


def unpack_units(core_ref, own_ref, other_ref, gate_ref, up_ref):
    units = gate_ref.shape[1] // N

    def write(source, target):
        for j in range(N):
            target[:, j * units : (j + 1) * units] = source[j, :, :units].astype(F32)

    @pl.when(core_ref[0] == 0)
    def _():
        write(own_ref, gate_ref)
        write(other_ref, up_ref)

    @pl.when(core_ref[0] != 0)
    def _():
        write(other_ref, gate_ref)
        write(own_ref, up_ref)


VMEM = pl.BlockSpec(memory_space=pltpu.VMEM)
SMEM = pl.BlockSpec(memory_space=pltpu.SMEM)


def call(kernel, outs, *args, specs=None, mib=32):
    return pl.pallas_call(
        kernel,
        out_shape=outs,
        in_specs=specs or [VMEM] * len(args),
        out_specs=jax.tree.map(lambda _: VMEM, outs),
        compiler_params=pltpu.CompilerParams(vmem_limit_bytes=mib * 2**20),
    )(*args)


def swap_pairs():
    pairs = []
    for y in range(4):
        for xl in range(2):
            for xh in range(2):
                for z in range(4):
                    for c in range(2):
                        source = (((y * 2 + xl) * 2 + xh) * 4 + z) * 2 + c
                        target = (((z * 2 + xh) * 2 + xl) * 4 + y) * 2 + c
                        pairs.append((source, target))
    return pairs


def local(
    hidden_in,
    segment_ids,
    attn_gain,
    w_query,
    b_query,
    w_key,
    b_key,
    w_value,
    b_value,
    w_out,
    ffn_gain,
    w_gate,
    w_up,
    w_down,
    cotangent,
):
    g = lax.axis_index(GROUP)
    c = lax.axis_index("c")
    rows, width = hidden_in.shape[1:]
    part = w_query.shape[1]
    units = w_down.shape[1]
    kv = w_key.shape[2]
    heads = width // HEAD_DIM
    ratio = heads // KV_HEADS

    segments = segment_ids[0]
    length = segments.shape[0]
    own_segments = lax.dynamic_slice_in_dim(segments, g * rows, rows, 0)
    query_index = g * rows + jnp.arange(rows, dtype=jnp.int32)
    earlier = jnp.sum((segments[None, :] < own_segments[:, None]).astype(jnp.int32), axis=-1)
    positions = query_index - earlier
    key_index = jnp.arange(length, dtype=jnp.int32)
    allowed = (key_index[None, :] <= query_index[:, None]) & (
        segments[None, :] == own_segments[:, None]
    )
    half = HEAD_DIM // 2
    frequency = THETA ** (-(2.0 * jnp.arange(half, dtype=F32)) / HEAD_DIM)
    angles = positions.astype(F32)[:, None] * frequency
    cosine = jnp.concatenate([jnp.cos(angles)] * 2, axis=-1)[:, None, :]
    sine = jnp.concatenate([jnp.sin(angles)] * 2, axis=-1)[:, None, :]

    small = jnp.concatenate([attn_gain[0], b_query[0], b_key[0], b_value[0], ffn_gain[0]])
    small = jnp.pad(small[None], ((0, 15), (0, width + 2 * kv - small.shape[0])))
    packed = jnp.concatenate(
        [jnp.concatenate([w_query[0], w_key[0], w_value[0]], axis=1), small], axis=0
    )
    halves = packed.reshape(2, HALF, width + 2 * kv)
    fetched = jnp.concatenate(core_pair(to_all(at(halves, c), GROUP), c), axis=1)
    w_qkv = fetched[:, :part].reshape(width, width + 2 * kv)
    vec = fetched[:, part].astype(F32)
    k16 = kv // N
    first_gain = vec[:, :part].reshape(-1)
    bias = jnp.concatenate(
        [
            vec[:, part : 2 * part].reshape(-1),
            vec[:, 2 * part : 2 * part + k16].reshape(-1),
            vec[:, 2 * part + k16 : 2 * part + 2 * k16].reshape(-1),
        ]
    )
    second_gain = vec[:, 2 * part + 2 * k16 : 3 * part + 2 * k16].reshape(-1)
    out_weight = lax.all_gather(w_out[0], GROUP, axis=0, tiled=True)
    group_down = lax.all_gather(cotangent[0], GROUP, axis=0, tiled=True)
    mine = jnp.where(c == 0, w_gate[0], w_up[0])
    mine = call(pack_units, jax.ShapeDtypeStruct((N, part, PAD), BF), mine)
    pair = core_pair(exchange(mine, GROUP), c)
    w_gu = jnp.concatenate([half_side.reshape(width, PAD) for half_side in pair], axis=1)
    w_dn = jnp.pad(w_down[0], ((0, PAD - units), (0, 0)))

    stream = hidden_in[0].astype(F32)
    normed, first_scale = norm_forward(stream, first_gain)
    normed = normed.astype(BF)
    raw = mm(normed, w_qkv) + bias
    turned = rotate(raw[:, : width + kv].reshape(rows, -1, HEAD_DIM), cosine, sine)
    turned = turned.reshape(rows, -1).astype(BF)
    queries = turned[:, :width].reshape(rows, KV_HEADS, ratio, HEAD_DIM)
    own_kv = jnp.concatenate([turned[:, width:], raw[:, width + kv :].astype(BF)], axis=1)
    all_kv = to_all(own_kv, GROUP).reshape(length, 2 * kv)
    keys = all_kv[:, :kv].reshape(length, KV_HEADS, HEAD_DIM)
    values = all_kv[:, kv:].reshape(length, KV_HEADS, HEAD_DIM)
    scores = jnp.einsum("qcgd,kcd->cgqk", queries, keys, preferred_element_type=F32)
    scores = jnp.where(allowed[None, None], scores * HEAD_DIM ** (-0.5), MASKED_SCORE)
    maximum = jnp.max(scores, axis=-1, keepdims=True)
    weights = jnp.exp(scores - maximum)
    totals = jnp.sum(weights, axis=-1, keepdims=True)
    probs = (weights / totals).astype(BF)
    mixed = jnp.einsum("cgqk,kcd->qcgd", probs, values, preferred_element_type=F32)
    attended = mixed.reshape(rows, -1).astype(BF)
    logsum = maximum + jnp.log(totals)
    middle = stream + mm(attended, out_weight)

    second_normed, second_scale = norm_forward(middle, second_gain)
    group_second = to_all(second_normed.astype(BF), GROUP).reshape(length, width)
    both = mm(group_second, w_gu)
    gate, up = both[:, :PAD], both[:, PAD:]
    sigmoid = jax.nn.sigmoid(gate)
    hidden = (gate * sigmoid * up).astype(BF)
    grad_hidden = mm_t(group_down, w_dn)
    grad_gate = (grad_hidden * up * sigmoid * (1.0 + gate * (1.0 - sigmoid))).astype(BF)
    grad_up = (grad_hidden * gate * sigmoid).astype(BF)
    grad_both = jnp.concatenate([grad_gate, grad_up], axis=1)
    second_terms = mm_t(grad_both, w_gu).astype(BF)
    grad_second = sum_at(second_terms.reshape(N, rows, width), GROUP)
    down_terms = mm(hidden, w_dn).astype(BF)
    grad_second, down_terms = lax.optimization_barrier((grad_second, down_terms))
    layer_out = middle + sum_at(down_terms.reshape(N, rows, width), GROUP)
    hidden_out = layer_out.astype(BF)[None]

    shares = core_sum(outer(group_second, grad_gate), outer(group_second, grad_up), c)
    share = sum_at(shares.reshape(N, part, PAD), SPREAD).astype(BF)
    share = lax.ppermute(share, AXES, swap_pairs())
    columns = to_all(share, SPREAD)
    other = shift(columns, "c", 1, 2)
    grads = (jax.ShapeDtypeStruct((part, N * units), F32),) * 2
    unpacked = call(unpack_units, grads, c.reshape(1), columns, other, specs=[SMEM, VMEM, VMEM])
    grad_w_gate, grad_w_up = unpacked[0][None], unpacked[1][None]
    down_share = outer(hidden, group_down)
    down_rows = PAD // 2
    down_share = core_sum(down_share[:down_rows], down_share[down_rows:], c)

    stream_grad = cotangent[0].astype(F32)
    term, gain_second = norm_backward(middle, second_scale, second_gain, grad_second)
    grad_middle = stream_grad + term
    attn_grad = grad_middle.astype(BF)
    grad_attended = mm_t(attn_grad, out_weight).astype(BF)
    small = jnp.pad(gain_second.reshape(N, 1, part), ((0, 0), (0, 15), (0, width - part)))
    grad_out = outer(attended, attn_grad).reshape(N, part, width)
    grad_out = jnp.concatenate([grad_out, small], axis=1)
    out_share = sum_at(core_sum(grad_out[:, :HALF], grad_out[:, HALF:], c), GROUP).astype(BF)
    share = jnp.concatenate([down_share, out_share]).reshape(N, -1, width)
    share = to_all(sum_at(share, SPREAD).astype(BF), SPREAD).reshape(-1, width)
    low, high = core_pair(share, c)
    grad_w_down = jnp.concatenate([low[:down_rows], high[:down_rows]])[None, :units].astype(F32)
    grad_out = jnp.concatenate([low[down_rows:], high[down_rows:]]).astype(F32)
    grad_split = grad_attended.reshape(queries.shape)
    probs = jnp.exp(scores - logsum)
    grad_probs = jnp.einsum("qcgd,kcd->cgqk", grad_split, values, preferred_element_type=F32)
    inner = jnp.sum(probs * grad_probs, axis=-1, keepdims=True)
    grad_scores = (probs * (grad_probs - inner) * HEAD_DIM ** (-0.5)).astype(BF)
    grad_queries = jnp.einsum("cgqk,kcd->qcgd", grad_scores, keys, preferred_element_type=F32)
    grad_keys = jnp.einsum("cgqk,qcgd->kcd", grad_scores, queries, preferred_element_type=F32)
    grad_values = jnp.einsum(
        "cgqk,qcgd->kcd", probs.astype(BF), grad_split, preferred_element_type=F32
    )
    grad_kv = jnp.concatenate([grad_keys.reshape(length, kv), grad_values.reshape(length, kv)], 1)
    own = sum_at(grad_kv.astype(BF).reshape(N, rows, 2 * kv), GROUP)
    grad_qk = jnp.concatenate([grad_queries.reshape(rows, width), own[:, :kv]], axis=1)
    grad_qk = rotate_back(grad_qk.reshape(rows, -1, HEAD_DIM), cosine, sine).reshape(rows, -1)
    grad_qkv = jnp.concatenate([grad_qk, own[:, kv:]], axis=1).astype(BF)
    grad_first = mm_t(grad_qkv, w_qkv)
    term, gain_first = norm_backward(stream, first_scale, first_gain, grad_first)
    grad_in = (grad_middle + term)[None]

    outer_qkv = outer(normed, grad_qkv)
    bias_grad = jnp.sum(grad_qkv.astype(F32), axis=0)
    row = jnp.concatenate(
        [
            bias_grad[:width].reshape(N, part),
            bias_grad[width : width + kv].reshape(N, k16),
            bias_grad[width + kv :].reshape(N, k16),
            gain_first.reshape(N, part),
        ],
        axis=1,
    )
    row = jnp.pad(row[:, None], ((0, 0), (0, 15), (0, width + 2 * kv - row.shape[1])))
    share = jnp.concatenate([outer_qkv.reshape(N, part, -1), row], axis=1)
    share = sum_at(core_sum(share[:, :HALF], share[:, HALF:], c), GROUP).astype(BF)
    share = sum_at(share.reshape(N, HALF // N, -1), SPREAD).astype(BF)
    share = to_all(share, SPREAD).reshape(HALF, -1)
    whole = jnp.concatenate(core_pair(share, c)).astype(F32)
    last = whole[part]
    return (
        hidden_out,
        grad_in,
        last[None, part + 2 * k16 : 2 * part + 2 * k16],
        whole[None, :part, :width],
        last[None, :part],
        whole[None, :part, width : width + kv],
        last[None, part : part + k16],
        whole[None, :part, width + kv :],
        last[None, part + k16 : part + 2 * k16],
        grad_out[None, :part],
        grad_out[part, :part][None],
        grad_w_gate,
        grad_w_up,
        grad_w_down,
    )


def solution(mesh):
    split = Mesh(mesh.devices.reshape(SIZES), AXES)
    tokens = P(REPLICA, GROUP, None)
    vector = P(None, GROUP)
    matrix = P(None, GROUP, None)
    weights = (vector, matrix, vector, matrix, vector, matrix, vector, matrix, vector)
    return jax.shard_map(
        local,
        mesh=split,
        in_specs=(tokens, P(REPLICA, None)) + weights + (matrix,) * 3 + (tokens,),
        out_specs=(tokens, tokens) + weights + (matrix,) * 3,
        check_vma=False,
    )
```

time: 469 us -> 478 us (1.019)
  the two profiles are of different devices: /device:TPU:1 before, /device:TPU:3 now
where the time goes in v2:
time: 478 us; the launch traced here: 468 us
  waiting for transfers between devices  169 us (35%)
  starting transfers between devices  109 us (23%)
  matrix products  79 us (17%)
  other arithmetic  53.7 us (11%)
  local copies, waits for them, and re-layouts  38 us (8%)
  between operations  15.3 us (3%)
    all_to_all x15, waiting for transfers between devices, exchange(): return lax.all_to_all(blocks, axis, 0, 0, tiled=True)  162 us
    all_to_all x15, starting transfers between devices, exchange(): return lax.all_to_all(blocks, axis, 0, 0, tiled=True)  79.5 us
    ppermute x9, starting transfers between devices, shift(): lax.ppermute(array, axis, [(i, (i + by) % size) for i in range(size)])  28 us
    dot_general x4, matrix products, mm_t(): lax.dot_general(a, b, (((1,), (1,)), ((), ())), preferred_element_type=F32)  16.3 us
    dot_general x5, matrix products, outer(): lax.dot_general(a, b, (((0,), (0,)), ((), ())), preferred_element_type=F32)  13.6 us
    dot_general x4, matrix products, mm(): return jnp.dot(a, b, preferred_element_type=F32)  13.6 us
    dot_general x1, matrix products, local(): jnp.einsum('cgqk,kcd->qcgd', grad_scores, keys, preferred_element_type=F32)  13.2 us
    dot_general x1, matrix products, local(): jnp.einsum('cgqk,qcgd->kcd', grad_scores, queries, preferred_element_type...  13.2 us
  transfers between devices with their start and end apart: 27, of which 17 were waited for; matrix products, arithmetic and copies ran while one was open for 31% of the time, Pallas kernels for 1%

profile of v2, /device:TPU:3, one launch (start us, length us, event | category | flops | bytes accessed | tf_op | source)
XLA Modules:
  0.0 468.5 jit_solution(7849730289699638545)
XLA Ops:
  7.9 3.4 concatenate.76
  13.6 5.5 %all-to-all-start = ((bf16[8,64,1152]{2,1,0:T(8,128)(2,1)}), bf16[8,64,1152]{2,1,0:T(8,128)(2,1)S(1)}, u32[]{:S(2)}, u32[]{:S(2)}) async-start(bf16[8,64,1152]{2,1,0:T(8,128)(2,1)} %broadcast_in_dim.45), calls=%async_computation | async-start | bytes 2359296 | tf_op jit(solution)/shard_map/all_to_all | solution.py:31
  19.8 22.6 %all-to-all-done = bf16[8,64,1152]{2,1,0:T(8,128)(2,1)S(1)} async-done(((bf16[8,64,1152]{2,1,0:T(8,128)(2,1)}), bf16[8,64,1152]{2,1,0:T(8,128)(2,1)S(1)}, u32[]{:S(2)}, u32[]{:S(2)}) %all-to-all-start) | async-done | bytes 1179680 | tf_op jit(solution)/shard_map/all_to_all | solution.py:31
  42.4 3.8 collective-permute-start
  52.4 2.0 copy.107
  56.9 7.0 %all-to-all-start.1 = ((bf16[8,128,256]{1,2,0:T(8,128)(2,1)}), bf16[8,128,256]{1,2,0:T(8,128)(2,1)S(1)}, u32[]{:S(2)}, u32[]{:S(2)}) async-start(bf16[8,128,256]{1,2,0:T(8,128)(2,1)} %broadcast_in_dim.84), calls=%async_computation.1 | async-start | bytes 1048576 | tf_op jit(solution)/shard_map/all_to_all | solution.py:31
  67.7 5.0 %all-to-all-done.1 = bf16[8,128,256]{1,2,0:T(8,128)(2,1)S(1)} async-done(((bf16[8,128,256]{1,2,0:T(8,128)(2,1)}), bf16[8,128,256]{1,2,0:T(8,128)(2,1)S(1)}, u32[]{:S(2)}, u32[]{:S(2)}) %all-to-all-start.1) | async-done | bytes 524320 | tf_op jit(solution)/shard_map/all_to_all | solution.py:31
  72.7 4.2 all-to-all-start.3
  80.3 1.9 copy-done
  83.6 2.0 multiply_reduce_fusion.2
  85.8 16.5 %all-to-all-done.3 = bf16[8,112,640]{2,1,0:T(8,128)(2,1)S(1)} async-done(((bf16[8,112,640]{2,1,0:T(8,128)(2,1)}), bf16[8,112,640]{2,1,0:T(8,128)(2,1)S(1)}, u32[]{:S(2)}, u32[]{:S(2)}) %all-to-all-start.3) | async-done | bytes 1146912 | tf_op jit(solution)/shard_map/all_to_all | solution.py:31
  104.0 6.7 %all-to-all-start.2 = ((bf16[8,128,896]{2,1,0:T(8,128)(2,1)}), bf16[8,128,896]{2,1,0:T(8,128)(2,1)S(1)}, u32[]{:S(2)}, u32[]{:S(2)}) async-start(bf16[8,128,896]{2,1,0:T(8,128)(2,1)} %broadcast_in_dim.87), calls=%async_computation.2 | async-start | bytes 3670016 | tf_op jit(solution)/shard_map/all_to_all | solution.py:31
  110.7 3.0 collective-permute-start.1
  113.7 2.6 collective-permute-done.1
  116.3 2.9 broadcast_select_fusion.3
  119.2 25.1 %all-to-all-done.2 = bf16[8,128,896]{2,1,0:T(8,128)(2,1)S(1)} async-done(((bf16[8,128,896]{2,1,0:T(8,128)(2,1)}), bf16[8,128,896]{2,1,0:T(8,128)(2,1)S(1)}, u32[]{:S(2)}, u32[]{:S(2)}) %all-to-all-start.2) | async-done | bytes 1835040 | tf_op jit(solution)/shard_map/all_to_all | solution.py:31
  144.3 6.3 %fusion.33 = f32[1024,1280]{0,1:T(8,128)} fusion(bf16[1024,896]{1,0:T(8,128)(2,1)S(1)} %bitcast.239, bf16[896,640]{1,0:T(8,128)(2,1)} %bitcast.255, bf16[896,640]{1,0:T(8,128)(2,1)} %bitcast.253), kind=kOutput, calls=%fused_computation.58 | convolution fusion | flops 2353397760 | bytes 9371648 | tf_op jit(solution)/shard_map/dot_general | solution.py:73
  150.6 7.1 %fusion.16 = (bf16[1024,640]{0,1:T(8,128)(2,1)S(1)}, bf16[1024,640]{0,1:T(8,128)(2,1)S(1)}, bf16[1024,640]{0,1:T(8,128)(2,1)}) fusion(f32[1024,1280]{0,1:T(8,128)} %fusion.33, bf16[1,1024,896]{2,1,0:T(8,128)(2,1)} %all-gather.7.cloned.1.call-done, bf16[608,896]{1,0:T(8,128)(2,1)} %bitcast.286), kind=kOutput, calls=%fused_computation.25 | convolution fusion | flops 1184890880 | bytes 12099584 | tf_op jit(solution)/shard_map/dot_general | solution.py:77
  157.7 4.1 fusion.26
  161.8 6.8 %all-to-all-start.4 = ((bf16[8,128,896]{2,1,0:T(8,128)(2,1)}), bf16[8,128,896]{2,1,0:T(8,128)(2,1)}, u32[]{:S(2)}, u32[]{:S(2)}) async-start(bf16[8,128,896]{2,1,0:T(8,128)(2,1)} %bitcast.252), calls=%async_computation.4 | async-start | bytes 3670016 | tf_op jit(solution)/shard_map/all_to_all | solution.py:31
  168.6 4.6 convolution_convert_fusion
  173.2 17.3 %all-to-all-done.4 = bf16[8,128,896]{2,1,0:T(8,128)(2,1)} async-done(((bf16[8,128,896]{2,1,0:T(8,128)(2,1)}), bf16[8,128,896]{2,1,0:T(8,128)(2,1)}, u32[]{:S(2)}, u32[]{:S(2)}) %all-to-all-start.4) | async-done | bytes 1835040 | tf_op jit(solution)/shard_map/all_to_all | solution.py:31
  192.4 5.2 %all-to-all-start.5 = ((bf16[8,128,896]{2,1,0:T(8,128)(2,1)}), bf16[8,128,896]{2,1,0:T(8,128)(2,1)}, u32[]{:S(2)}, u32[]{:S(2)}) async-start(bf16[8,128,896]{2,1,0:T(8,128)(2,1)} %bitcast.251), calls=%async_computation.5 | async-start | bytes 3670016 | tf_op jit(solution)/shard_map/all_to_all | solution.py:31
  197.6 3.1 fusion.101
  200.6 3.4 select_convert_fusion.1
  204.1 2.8 collective-permute-start.7
  207.2 11.0 %all-to-all-done.5 = bf16[8,128,896]{2,1,0:T(8,128)(2,1)} async-done(((bf16[8,128,896]{2,1,0:T(8,128)(2,1)}), bf16[8,128,896]{2,1,0:T(8,128)(2,1)}, u32[]{:S(2)}, u32[]{:S(2)}) %all-to-all-start.5) | async-done | bytes 1835040 | tf_op jit(solution)/shard_map/all_to_all | solution.py:31
  218.2 1.9 convert_reduce_fusion
  220.1 2.1 convert_add_fusion
  223.0 2.7 fusion.45
  227.5 5.3 %fusion.100 = f32[2,1024,128,7]{2,1,3,0:T(8,128)} fusion(bf16[1024,2,64,1]{0,2,3,1:T(8,128)(2,1)} %bitcast.260, bf16[128,2,7,64]{0,3,2,1:T(8,128)(2,1)} %bitcast.249), kind=kOutput, calls=%fused_computation.183 | convolution fusion | flops 234881024 | bytes 7831552 | tf_op jit(solution)/shard_map/qcgd,kcd->cgqk/dot_general | solution.py:285
  235.5 13.2 %fusion.44 = bf16[2,64,1024]{2,1,0:T(8,128)(2,1)} fusion(bf16[128,2,7,64]{0,3,2,1:T(8,128)(2,1)} %bitcast.264, f32[2,1024,128,7]{2,1,3,0:T(8,128)} %fusion.100, f32[2,7,128,1024]{2,3,1,0:T(8,128)} %copy-done, f32[2,7,128]{2,1,0:T(8,128)S(1)} %log_add_fusion), kind=kOutput, calls=%fused_computation.63 | convolution fusion | flops 247859968 | bytes 15178752 | tf_op jit(solution)/shard_map/cgqk,qcgd->kcd/dot_general | solution.py:289
  251.5 6.3 %all-to-all-start.6 = ((bf16[8,128,256]{1,2,0:T(8,128)(2,1)}), bf16[8,128,256]{1,2,0:T(8,128)(2,1)}, u32[]{:S(2)}, u32[]{:S(2)}) async-start(bf16[8,128,256]{1,2,0:T(8,128)(2,1)} %pad_maximum_fusion.8), calls=%async_computation.6 | async-start | bytes 1048576 | tf_op jit(solution)/shard_map/all_to_all | solution.py:31
  258.9 2.8 collective-permute-start.5
  261.7 13.2 %fusion.21 = f32[2,64,7,128]{3,1,2,0:T(8,128)} fusion(bf16[1024,2,64,1]{0,2,3,1:T(8,128)(2,1)} %bitcast.258, f32[2,1024,128,7]{2,1,3,0:T(8,128)} %fusion.100, f32[2,7,128,1024]{2,3,1,0:T(8,128)} %copy-done, f32[2,7,128]{2,1,0:T(8,128)S(1)} %log_add_fusion), kind=kOutput, calls=%fused_computation.33 | convolution fusion | flops 247728896 | bytes 15408128 | tf_op jit(solution)/shard_map/cgqk,kcd->qcgd/dot_general | solution.py:288
  274.9 2.0 copy.125
  279.7 1.9 pad_maximum_fusion.9
  281.6 2.1 copy.127
  285.6 2.0 copy.128
  289.1 2.4 fusion.84
  301.4 2.6 add_convert_fusion.1
  304.0 5.8 %all-to-all-start.13 = ((bf16[8,112,640]{2,1,0:T(8,128)(2,1)}), bf16[8,112,640]{2,1,0:T(8,128)(2,1)}, u32[]{:S(2)}, u32[]{:S(2)}) async-start(bf16[8,112,640]{2,1,0:T(8,128)(2,1)} %bitcast.242), calls=%async_computation.13 | async-start | bytes 2293760 | tf_op jit(solution)/shard_map/all_to_all | solution.py:31
  309.8 2.4 add_convert_fusion.2
  312.1 15.8 %all-to-all-done.13 = bf16[8,112,640]{2,1,0:T(8,128)(2,1)} async-done(((bf16[8,112,640]{2,1,0:T(8,128)(2,1)}), bf16[8,112,640]{2,1,0:T(8,128)(2,1)}, u32[]{:S(2)}, u32[]{:S(2)}) %all-to-all-start.13) | async-done | bytes 1146912 | tf_op jit(solution)/shard_map/all_to_all | solution.py:31
  328.0 5.2 %all-to-all-start.10 = ((bf16[8,64,896]{2,1,0:T(8,128)(2,1)}), bf16[8,64,896]{2,1,0:T(8,128)(2,1)S(1)}, u32[]{:S(2)}, u32[]{:S(2)}) async-start(bf16[8,64,896]{2,1,0:T(8,128)(2,1)} %add_convert_fusion.2), calls=%async_computation.10 | async-start | bytes 1835008 | tf_op jit(solution)/shard_map/all_to_all | solution.py:31
  333.2 3.9 add_convert_fusion
  337.1 7.8 %all-to-all-done.10 = bf16[8,64,896]{2,1,0:T(8,128)(2,1)S(1)} async-done(((bf16[8,64,896]{2,1,0:T(8,128)(2,1)}), bf16[8,64,896]{2,1,0:T(8,128)(2,1)S(1)}, u32[]{:S(2)}, u32[]{:S(2)}) %all-to-all-start.10) | async-done | bytes 917536 | tf_op jit(solution)/shard_map/all_to_all | solution.py:31
  344.8 4.9 %all-to-all-start.7 = ((bf16[8,64,1152]{2,1,0:T(8,128)(2,1)}), bf16[8,64,1152]{2,1,0:T(8,128)(2,1)S(1)}, u32[]{:S(2)}, u32[]{:S(2)}) async-start(bf16[8,64,1152]{2,1,0:T(8,128)(2,1)} %add_convert_fusion), calls=%async_computation.7 | async-start | bytes 2359296 | tf_op jit(solution)/shard_map/all_to_all | solution.py:31
  351.2 1.9 collective-permute-start.8
  353.1 4.8 %fusion.22 = f32[640,896]{1,0:T(8,128)} fusion(bf16[1024,640]{0,1:T(8,128)(2,1)} %get-tuple-element.28, bf16[1,1024,896]{2,1,0:T(8,128)(2,1)} %all-gather.7.cloned.1.call-done), kind=kOutput, calls=%fused_computation.46 | convolution fusion | flops 1174405120 | bytes 5439488 | tf_op jit(solution)/shard_map/dot_general | solution.py:81
  357.9 12.7 %all-to-all-done.7 = bf16[8,64,1152]{2,1,0:T(8,128)(2,1)S(1)} async-done(((bf16[8,64,1152]{2,1,0:T(8,128)(2,1)}), bf16[8,64,1152]{2,1,0:T(8,128)(2,1)S(1)}, u32[]{:S(2)}, u32[]{:S(2)}) %all-to-all-start.7) | async-done | bytes 1179680 | tf_op jit(solution)/shard_map/all_to_all | solution.py:31
  371.7 5.1 %all-to-all-start.14 = ((bf16[8,112,640]{2,1,0:T(8,128)(2,1)}), bf16[8,112,640]{2,1,0:T(8,128)(2,1)S(1)}, u32[]{:S(2)}, u32[]{:S(2)}) async-start(bf16[8,112,640]{2,1,0:T(8,128)(2,1)} %broadcast_in_dim.97), calls=%async_computation.14 | async-start | bytes 2293760 | tf_op jit(solution)/shard_map/all_to_all | solution.py:31
  385.5 7.9 %all-to-all-done.14.own_ref = bf16[8,112,640]{2,1,0:T(8,128)(2,1)S(1)} async-done(((bf16[8,112,640]{2,1,0:T(8,128)(2,1)}), bf16[8,112,640]{2,1,0:T(8,128)(2,1)S(1)}, u32[]{:S(2)}, u32[]{:S(2)}) %all-to-all-start.14) | async-done | bytes 1146912 | tf_op jit(solution)/shard_map/all_to_all | solution.py:31
  393.3 4.3 all-to-all-start.8
  398.6 6.2 %all-to-all-done.8 = bf16[8,8,1152]{2,1,0:T(8,128)(2,1)S(1)} async-done(((bf16[8,8,1152]{2,1,0:T(8,128)(2,1)}), bf16[8,8,1152]{2,1,0:T(8,128)(2,1)S(1)}, u32[]{:S(2)}, u32[]{:S(2)}) %all-to-all-start.8) | async-done | bytes 147488 | tf_op jit(solution)/shard_map/all_to_all | solution.py:31
  405.5 4.3 all-to-all-start.11
  409.8 2.8 collective-permute-start.9
  413.6 6.7 %all-to-all-done.11 = bf16[8,48,896]{2,1,0:T(8,128)(2,1)} async-done(((bf16[8,48,896]{2,1,0:T(8,128)(2,1)}), bf16[8,48,896]{2,1,0:T(8,128)(2,1)}, u32[]{:S(2)}, u32[]{:S(2)}) %all-to-all-start.11) | async-done | bytes 688160 | tf_op jit(solution)/shard_map/all_to_all | solution.py:31
  420.9 4.0 all-to-all-start.9
  426.1 5.9 %all-to-all-done.9 = bf16[8,8,1152]{2,1,0:T(8,128)(2,1)} async-done(((bf16[8,8,1152]{2,1,0:T(8,128)(2,1)}), bf16[8,8,1152]{2,1,0:T(8,128)(2,1)}, u32[]{:S(2)}, u32[]{:S(2)}) %all-to-all-start.9) | async-done | bytes 147488 | tf_op jit(solution)/shard_map/all_to_all | solution.py:31
  433.0 4.2 all-to-all-start.12
  437.2 5.2 %collective-permute-start.3 = (bf16[64,1152]{1,0:T(8,128)(2,1)}, bf16[64,1152]{1,0:T(8,128)(2,1)}, u32[]{:S(2)}, u32[]{:S(2)}) collective-permute-start(bf16[64,1152]{1,0:T(8,128)(2,1)} %bitcast.62), channel_id=1, source_target_pairs={{0,1},{1,0},{2,3},{3,2},{4,5},{5,4},{6,7},{7,6},{8,9},{9,8},{10,11... | collective-permute-start | bytes 442376 | tf_op jit(solution)/shard_map/ppermute | solution.py:27
  443.3 2.6 shard_map.255
  447.2 6.2 %collective-permute-start.6 = (bf16[384,896]{1,0:T(8,128)(2,1)}, bf16[384,896]{1,0:T(8,128)(2,1)S(1)}, u32[]{:S(2)}, u32[]{:S(2)}) collective-permute-start(bf16[384,896]{1,0:T(8,128)(2,1)} %bitcast.71), channel_id=1, source_target_pairs={{0,1},{1,0},{2,3},{3,2},{4,5},{5,4},{6,7},{7,6},{8,9},{9,8},{10,11... | collective-permute-start | bytes 2064392 | tf_op jit(solution)/shard_map/ppermute | solution.py:27
  (204 shorter events, 76.2 us)
Async XLA Ops:
  7.2 76.4 %all-gather.5.cloned.1.call-start = ((), (), s32[]{:S(2)}) async-start(), calls=%async_computation.15 | async-start | bytes 1806336 | tf_op jit(solution)/shard_map/all_gather | solution.py:210
  12.3 33.8 %copy-start.30 = (s32[1,1024]{1,0:T(1,128)S(1)}, s32[1,1024]{1,0:T(1,128)}, u32[]{:S(2)}) copy-start(s32[1,1024]{1,0:T(1,128)} %param.16) | copy-start | bytes 12292
  13.5 33.3 %copy-start.10 = (bf16[1,128,896]{2,1,0:T(8,128)(2,1)S(1)}, bf16[1,128,896]{2,1,0:T(8,128)(2,1)}, u32[]{:S(2)}) copy-start(bf16[1,128,896]{2,1,0:T(8,128)(2,1)} %param.15) | copy-start | bytes 688132
  13.6 28.8 %all-to-all-start = ((bf16[8,64,1152]{2,1,0:T(8,128)(2,1)}), bf16[8,64,1152]{2,1,0:T(8,128)(2,1)S(1)}, u32[]{:S(2)}, u32[]{:S(2)}) async-start(bf16[8,64,1152]{2,1,0:T(8,128)(2,1)} %broadcast_in_dim.45), calls=%async_computation | async-start | bytes 2359296 | tf_op jit(solution)/shard_map/all_to_all | solution.py:31
  19.1 131.6 %all-gather.7.cloned.1.call-start = ((), (), s32[]{:S(2)}) async-start(), calls=%async_computation.16 | async-start | bytes 2064384 | tf_op jit(solution)/shard_map/all_gather | solution.py:211
  42.4 6.4 %collective-permute-start = (bf16[8,64,1152]{2,1,0:T(8,128)(2,1)S(1)}, bf16[8,64,1152]{2,1,0:T(8,128)(2,1)}, u32[]{:S(2)}, u32[]{:S(2)}) collective-permute-start(bf16[8,64,1152]{2,1,0:T(8,128)(2,1)S(1)} %all-to-all-done), channel_id=1, source_target_pairs={{0,1},{1,0},{2,3},{3,2},{4,5},{5,4},{6,7},{7,6},{8,9},{9,8},{10,11... | collective-permute-start | bytes 3538952 | tf_op jit(solution)/shard_map/ppermute | solution.py:27
  46.8 9.0 %copy-start.11 = (f32[128,1024]{1,0:T(8,128)}, f32[128,1024]{1,0:T(8,128)S(1)}, u32[]{:S(2)}) copy-start(f32[128,1024]{1,0:T(8,128)S(1)} %copy.106) | copy-start | bytes 1572868
  46.9 8.7 %copy-start.29 = (f32[128,64]{0,1:T(8,128)}, f32[128,64]{0,1:T(8,128)S(1)}, u32[]{:S(2)}) copy-start(f32[128,64]{0,1:T(8,128)S(1)} %pad_maximum_fusion.16) | copy-start | bytes 98308
  50.6 3.8 copy-start.2
  56.9 15.8 %all-to-all-start.1 = ((bf16[8,128,256]{1,2,0:T(8,128)(2,1)}), bf16[8,128,256]{1,2,0:T(8,128)(2,1)S(1)}, u32[]{:S(2)}, u32[]{:S(2)}) async-start(bf16[8,128,256]{1,2,0:T(8,128)(2,1)} %broadcast_in_dim.84), calls=%async_computation.1 | async-start | bytes 1048576 | tf_op jit(solution)/shard_map/all_to_all | solution.py:31
  72.7 29.6 %all-to-all-start.3 = ((bf16[8,112,640]{2,1,0:T(8,128)(2,1)}), bf16[8,112,640]{2,1,0:T(8,128)(2,1)S(1)}, u32[]{:S(2)}, u32[]{:S(2)}) async-start(bf16[8,112,640]{2,1,0:T(8,128)(2,1)} %shard_map.254), calls=%async_computation.3 | async-start | bytes 2293760 | tf_op jit(solution)/shard_map/all_to_all | solution.py:31
  77.1 0.9 copy-start.25
  77.3 2.0 copy-start.23
  77.5 2.8 copy-start.24
  79.3 2.9 copy-start
  83.6 20.4 %copy-start.26 = (bf16[2,64,7,128]{3,1,2,0:T(8,128)(2,1)}, bf16[2,64,7,128]{3,1,2,0:T(8,128)(2,1)S(1)}, u32[]{:S(2)}) copy-start(bf16[2,64,7,128]{3,1,2,0:T(8,128)(2,1)S(1)} %fusion.48) | copy-start | bytes 688132
  85.7 121.2 %copy-start.6 = (f32[128,896]{1,0:T(8,128)}, f32[128,896]{1,0:T(8,128)S(1)}, u32[]{:S(2)}) copy-start(f32[128,896]{1,0:T(8,128)S(1)} %get-tuple-element.64) | copy-start | bytes 1376260
  102.3 1.6 copy-start.12
  104.0 40.3 %all-to-all-start.2 = ((bf16[8,128,896]{2,1,0:T(8,128)(2,1)}), bf16[8,128,896]{2,1,0:T(8,128)(2,1)S(1)}, u32[]{:S(2)}, u32[]{:S(2)}) async-start(bf16[8,128,896]{2,1,0:T(8,128)(2,1)} %broadcast_in_dim.87), calls=%async_computation.2 | async-start | bytes 3670016 | tf_op jit(solution)/shard_map/all_to_all | solution.py:31
  110.7 5.6 %collective-permute-start.1 = (bf16[8,112,640]{2,1,0:T(8,128)(2,1)}, bf16[8,112,640]{2,1,0:T(8,128)(2,1)S(1)}, u32[]{:S(2)}, u32[]{:S(2)}) collective-permute-start(bf16[8,112,640]{2,1,0:T(8,128)(2,1)} %copy-done.12), channel_id=1, source_target_pairs={{0,1},{1,0},{2,3},{3,2},{4,5},{5,4},{6,7},{7,6},{8,9},{9,8},{10,11... | collective-permute-start | bytes 3440648 | tf_op jit(solution)/shard_map/ppermute | solution.py:27
  150.6 7.1 %copy-start.21 = (bf16[8,112,640]{2,1,0:T(8,128)(2,1)S(1)}, bf16[8,112,640]{2,1,0:T(8,128)(2,1)}, u32[]{:S(2)}) copy-start(bf16[8,112,640]{2,1,0:T(8,128)(2,1)} %get-tuple-element.31) | copy-start | bytes 3440644
  150.6 7.1 %copy-start.22 = (bf16[8,112,640]{2,1,0:T(8,128)(2,1)S(1)}, bf16[8,112,640]{2,1,0:T(8,128)(2,1)}, u32[]{:S(2)}) copy-start(bf16[8,112,640]{2,1,0:T(8,128)(2,1)} %get-tuple-element.32) | copy-start | bytes 3440644
  157.7 4.1 copy-start.19
  157.7 4.1 copy-start.31
  161.8 28.7 %all-to-all-start.4 = ((bf16[8,128,896]{2,1,0:T(8,128)(2,1)}), bf16[8,128,896]{2,1,0:T(8,128)(2,1)}, u32[]{:S(2)}, u32[]{:S(2)}) async-start(bf16[8,128,896]{2,1,0:T(8,128)(2,1)} %bitcast.252), calls=%async_computation.4 | async-start | bytes 3670016 | tf_op jit(solution)/shard_map/all_to_all | solution.py:31
  192.4 14.5 %copy-start.16 = (f32[128,896]{1,0:T(8,128)}, f32[128,896]{1,0:T(8,128)S(1)}, u32[]{:S(2)}) copy-start(f32[128,896]{1,0:T(8,128)S(1)} %convert_reduce_fusion.1) | copy-start | bytes 1376260
  192.4 25.8 %all-to-all-start.5 = ((bf16[8,128,896]{2,1,0:T(8,128)(2,1)}), bf16[8,128,896]{2,1,0:T(8,128)(2,1)}, u32[]{:S(2)}, u32[]{:S(2)}) async-start(bf16[8,128,896]{2,1,0:T(8,128)(2,1)} %bitcast.251), calls=%async_computation.5 | async-start | bytes 3670016 | tf_op jit(solution)/shard_map/all_to_all | solution.py:31
  197.6 3.1 copy-start.20
  200.6 3.5 copy-start.3
  204.1 95.8 %collective-permute-start.7 = (bf16[896,640]{1,0:T(8,128)(2,1)}, bf16[896,640]{1,0:T(8,128)(2,1)}, u32[]{:S(2)}, u32[]{:S(2)}) collective-permute-start(bf16[896,640]{1,0:T(8,128)(2,1)} %get-tuple-element.65), channel_id=1, source_target_pairs={{0,1},{1,0},{2,3},{3,2},{4,5},{5,4},{6,7},{7,6},{8,9},{9,8},{10,11... | collective-permute-start | bytes 3440648 | tf_op jit(solution)/shard_map/ppermute | solution.py:27
  218.2 14.6 %slice-start = ((s8[7340032]{0:T(1024)(128)(4,1)}), s8[3145728]{0:T(1024)(128)(4,1)S(1)}, s32[]{:S(2)}) async-start(s8[7340032]{0:T(1024)(128)(4,1)} %bitcast.235), calls=%async_computation.17 | async-start | bytes 6291456
  222.3 0.8 copy-start.7
  227.5 5.3 %slice-start.1 = ((s8[7340032]{0:T(1024)(128)(4,1)}), s8[4194304]{0:T(1024)(128)(4,1)S(1)}, s32[]{:S(2)}) async-start(s8[7340032]{0:T(1024)(128)(4,1)} %bitcast.235), calls=%async_computation.18 | async-start | bytes 8388608
  227.5 5.3 %copy-start.18 = (bf16[128,896]{0,1:T(8,128)(2,1)S(1)}, bf16[128,896]{0,1:T(8,128)(2,1)}, u32[]{:S(2)}) copy-start(bf16[128,896]{0,1:T(8,128)(2,1)} %copy.117) | copy-start | bytes 688132
  232.9 2.1 copy-start.8
  232.9 2.1 copy-start.27
  251.5 25.4 %all-to-all-start.6 = ((bf16[8,128,256]{1,2,0:T(8,128)(2,1)}), bf16[8,128,256]{1,2,0:T(8,128)(2,1)}, u32[]{:S(2)}, u32[]{:S(2)}) async-start(bf16[8,128,256]{1,2,0:T(8,128)(2,1)} %pad_maximum_fusion.8), calls=%async_computation.6 | async-start | bytes 1048576 | tf_op jit(solution)/shard_map/all_to_all | solution.py:31
  258.9 50.9 %collective-permute-start.5 = (bf16[8,64,896]{2,1,0:T(8,128)(2,1)}, bf16[8,64,896]{2,1,0:T(8,128)(2,1)}, u32[]{:S(2)}, u32[]{:S(2)}) collective-permute-start(bf16[8,64,896]{2,1,0:T(8,128)(2,1)} %select_convert_fusion.2), channel_id=1, source_target_pairs={{0,1},{1,0},{2,3},{3,2},{4,5},{5,4},{6,7},{7,6},{8,9},{9,8},{10,11... | collective-permute-start | bytes 2752520 | tf_op jit(solution)/shard_map/ppermute | solution.py:27
  289.1 2.4 copy-start.13
  291.5 0.8 copy-start.14
  297.1 2.7 copy-start.1
  297.2 3.4 copy-start.4
  297.2 4.2 copy-start.5
  299.8 33.3 %collective-permute-start.2 = (bf16[8,64,1152]{2,1,0:T(8,128)(2,1)}, bf16[8,64,1152]{2,1,0:T(8,128)(2,1)}, u32[]{:S(2)}, u32[]{:S(2)}) collective-permute-start(bf16[8,64,1152]{2,1,0:T(8,128)(2,1)} %select_convert_fusion), channel_id=1, source_target_pairs={{0,1},{1,0},{2,3},{3,2},{4,5},{5,4},{6,7},{7,6},{8,9},{9,8},{10,11... | collective-permute-start | bytes 3538952 | tf_op jit(solution)/shard_map/ppermute | solution.py:27
  304.0 24.0 %all-to-all-start.13 = ((bf16[8,112,640]{2,1,0:T(8,128)(2,1)}), bf16[8,112,640]{2,1,0:T(8,128)(2,1)}, u32[]{:S(2)}, u32[]{:S(2)}) async-start(bf16[8,112,640]{2,1,0:T(8,128)(2,1)} %bitcast.242), calls=%async_computation.13 | async-start | bytes 2293760 | tf_op jit(solution)/shard_map/all_to_all | solution.py:31
  328.0 16.8 %all-to-all-start.10 = ((bf16[8,64,896]{2,1,0:T(8,128)(2,1)}), bf16[8,64,896]{2,1,0:T(8,128)(2,1)S(1)}, u32[]{:S(2)}, u32[]{:S(2)}) async-start(bf16[8,64,896]{2,1,0:T(8,128)(2,1)} %add_convert_fusion.2), calls=%async_computation.10 | async-start | bytes 1835008 | tf_op jit(solution)/shard_map/all_to_all | solution.py:31
  344.8 13.1 %copy-start.17 = (bf16[8,64,896]{2,1,0:T(8,128)(2,1)}, bf16[8,64,896]{2,1,0:T(8,128)(2,1)S(1)}, u32[]{:S(2)}) copy-start(bf16[8,64,896]{2,1,0:T(8,128)(2,1)S(1)} %all-to-all-done.10) | copy-start | bytes 2752516
  344.8 25.7 %all-to-all-start.7 = ((bf16[8,64,1152]{2,1,0:T(8,128)(2,1)}), bf16[8,64,1152]{2,1,0:T(8,128)(2,1)S(1)}, u32[]{:S(2)}, u32[]{:S(2)}) async-start(bf16[8,64,1152]{2,1,0:T(8,128)(2,1)} %add_convert_fusion), calls=%async_computation.7 | async-start | bytes 2359296 | tf_op jit(solution)/shard_map/all_to_all | solution.py:31
  351.2 6.8 %collective-permute-start.8 = (bf16[112,640]{1,0:T(8,128)(2,1)S(1)}, bf16[112,640]{1,0:T(8,128)(2,1)S(1)}, u32[]{:S(2)}, u32[]{:S(2)}) collective-permute-start(bf16[112,640]{1,0:T(8,128)(2,1)S(1)} %reduce_sum.194), channel_id=1, source_target_pairs={{0,0},{1,1},{2,32},{3,33},{4,64},{5,65},{6,96},{7,97},{8,16},{9,17... | collective-permute-start | bytes 430088 | tf_op jit(solution)/shard_map/ppermute | solution.py:259
  371.7 21.7 %all-to-all-start.14 = ((bf16[8,112,640]{2,1,0:T(8,128)(2,1)}), bf16[8,112,640]{2,1,0:T(8,128)(2,1)S(1)}, u32[]{:S(2)}, u32[]{:S(2)}) async-start(bf16[8,112,640]{2,1,0:T(8,128)(2,1)} %broadcast_in_dim.97), calls=%async_computation.14 | async-start | bytes 2293760 | tf_op jit(solution)/shard_map/all_to_all | solution.py:31
  378.5 3.1 collective-permute-start.4
  393.3 11.5 %all-to-all-start.8 = ((bf16[8,8,1152]{2,1,0:T(8,128)(2,1)}), bf16[8,8,1152]{2,1,0:T(8,128)(2,1)S(1)}, u32[]{:S(2)}, u32[]{:S(2)}) async-start(bf16[8,8,1152]{2,1,0:T(8,128)(2,1)} %bitcast.61), calls=%async_computation.8 | async-start | bytes 294912 | tf_op jit(solution)/shard_map/all_to_all | solution.py:31
  404.8 0.7 copy-start.28
  405.5 36.9 %copy-start.9 = (f32[128,896]{1,0:T(8,128)S(1)}, f32[128,896]{1,0:T(8,128)}, u32[]{:S(2)}) copy-start(f32[128,896]{1,0:T(8,128)} %copy-done.7) | copy-start | bytes 1376260
  405.5 36.9 %copy-start.15 = (f32[128,896]{1,0:T(8,128)S(1)}, f32[128,896]{1,0:T(8,128)}, u32[]{:S(2)}) copy-start(f32[128,896]{1,0:T(8,128)} %copy-done.14) | copy-start | bytes 1376260
  405.5 14.8 %all-to-all-start.11 = ((bf16[8,48,896]{2,1,0:T(8,128)(2,1)}), bf16[8,48,896]{2,1,0:T(8,128)(2,1)}, u32[]{:S(2)}, u32[]{:S(2)}) async-start(bf16[8,48,896]{2,1,0:T(8,128)(2,1)} %bitcast.70), calls=%async_computation.11 | async-start | bytes 1376256 | tf_op jit(solution)/shard_map/all_to_all | solution.py:31
  409.8 33.5 %collective-permute-start.9 = (bf16[8,112,640]{2,1,0:T(8,128)(2,1)S(1)}, bf16[8,112,640]{2,1,0:T(8,128)(2,1)S(1)}, u32[]{:S(2)}, u32[]{:S(2)}) collective-permute-start(bf16[8,112,640]{2,1,0:T(8,128)(2,1)S(1)} %all-to-all-done.14.own_ref), channel_id=1, source_target_pairs={{0,1},{1,0},{2,3},{3,2},{4,5},{5,4},{6,7},{7,6},{8,9},{9,8},{10,11... | collective-permute-start | bytes 3440648 | tf_op jit(solution)/shard_map/ppermute | solution.py:27
  420.9 11.1 %all-to-all-start.9 = ((bf16[8,8,1152]{2,1,0:T(8,128)(2,1)}), bf16[8,8,1152]{2,1,0:T(8,128)(2,1)}, u32[]{:S(2)}, u32[]{:S(2)}) async-start(bf16[8,8,1152]{2,1,0:T(8,128)(2,1)} %broadcast_in_dim.91), calls=%async_computation.9 | async-start | bytes 294912 | tf_op jit(solution)/shard_map/all_to_all | solution.py:31
  433.0 14.2 %all-to-all-start.12 = ((bf16[8,48,896]{2,1,0:T(8,128)(2,1)}), bf16[8,48,896]{2,1,0:T(8,128)(2,1)}, u32[]{:S(2)}, u32[]{:S(2)}) async-start(bf16[8,48,896]{2,1,0:T(8,128)(2,1)} %broadcast_in_dim.95), calls=%async_computation.12 | async-start | bytes 1376256 | tf_op jit(solution)/shard_map/all_to_all | solution.py:31
  437.2 16.2 %collective-permute-start.3 = (bf16[64,1152]{1,0:T(8,128)(2,1)}, bf16[64,1152]{1,0:T(8,128)(2,1)}, u32[]{:S(2)}, u32[]{:S(2)}) collective-permute-start(bf16[64,1152]{1,0:T(8,128)(2,1)} %bitcast.62), channel_id=1, source_target_pairs={{0,1},{1,0},{2,3},{3,2},{4,5},{5,4},{6,7},{7,6},{8,9},{9,8},{10,11... | collective-permute-start | bytes 442376 | tf_op jit(solution)/shard_map/ppermute | solution.py:27
  447.2 9.8 %collective-permute-start.6 = (bf16[384,896]{1,0:T(8,128)(2,1)}, bf16[384,896]{1,0:T(8,128)(2,1)S(1)}, u32[]{:S(2)}, u32[]{:S(2)}) collective-permute-start(bf16[384,896]{1,0:T(8,128)(2,1)} %bitcast.71), channel_id=1, source_target_pairs={{0,1},{1,0},{2,3},{3,2},{4,5},{5,4},{6,7},{7,6},{8,9},{9,8},{10,11... | collective-permute-start | bytes 2064392 | tf_op jit(solution)/shard_map/ppermute | solution.py:27
Sparse Core Ops, SparseCore 0:
  9.7 55.2 all-gather.4
  66.6 70.6 all-gather.6

commit v3 on v2

v3 whole, which is shorter than its diff:
```python
import jax
import jax.numpy as jnp
from jax import lax
from jax.experimental import pallas as pl
from jax.experimental.pallas import tpu as pltpu
from jax.sharding import Mesh
from jax.sharding import PartitionSpec as P

KV_HEADS = 2
HEAD_DIM = 64
EPS = 1e-06
THETA = 1000000.0
MASKED_SCORE = -1e30
GROUP = ("y", "xl")
SPREAD = ("z", "xh")
REPLICA = ("xh", "z", "c")
SIZES = (4, 2, 2, 4, 2)
AXES = ("y", "xl", "xh", "z", "c")
N = 8
PAD = 640
HALF = 64
BF = jnp.bfloat16
F32 = jnp.float32


def shift(array, axis, by, size):
    return lax.ppermute(array, axis, [(i, (i + by) % size) for i in range(size)])


def exchange(blocks, axis):
    return lax.all_to_all(blocks, axis, 0, 0, tiled=True)


def to_all(array, axis):
    return exchange(jnp.broadcast_to(array, (N, *array.shape)), axis)


def sum_at(blocks, axis):
    return jnp.sum(exchange(blocks, axis).astype(F32), axis=0)


def at(blocks, index):
    return lax.dynamic_index_in_dim(blocks, index, 0, keepdims=False)


def norm_forward(stream, gain):
    scale = lax.rsqrt(jnp.mean(stream * stream, axis=-1, keepdims=True) + EPS)
    return stream * scale * gain, scale


def norm_backward(stream, scale, gain, gradient):
    normalized = stream * scale
    scaled = gradient * gain
    gain_grad = jnp.sum(gradient * normalized, axis=0)
    grad = scale * (scaled - normalized * jnp.mean(scaled * normalized, axis=-1, keepdims=True))
    return grad, gain_grad


def mm(a, b):
    return jnp.dot(a, b, preferred_element_type=F32)


def mm_t(a, b):
    return lax.dot_general(a, b, (((1,), (1,)), ((), ())), preferred_element_type=F32)


def outer(a, b):
    return lax.dot_general(a, b, (((0,), (0,)), ((), ())), preferred_element_type=F32)


def core_sum(first, second, c):
    low = c == 0
    keep = jnp.where(low, first, second)
    send = jnp.where(low, second, first).astype(BF)
    return (keep + shift(send, "c", 1, 2).astype(F32)).astype(BF)


def core_pair(own, c):
    other = shift(own, "c", 1, 2)
    low = c == 0
    return jnp.where(low, own, other), jnp.where(low, other, own)


def pack_units(w_ref, packed_ref):
    units = w_ref.shape[1] // N
    packed_ref[...] = jnp.zeros_like(packed_ref)
    for j in range(N):
        packed_ref[j, :, :units] = w_ref[:, j * units : (j + 1) * units]


def unpack_units(blocks_ref, gate_ref, up_ref):
    units = gate_ref.shape[1] // N
    for i, target in enumerate((gate_ref, up_ref)):
        for j in range(N):
            target[:, j * units : (j + 1) * units] = blocks_ref[j, i, :, :units].astype(F32)


VMEM = pl.BlockSpec(memory_space=pltpu.VMEM)
SMEM = pl.BlockSpec(memory_space=pltpu.SMEM)


def call(kernel, outs, *args, scalars=0, scratch=(), flops=0, mib=48):
    cost = pl.CostEstimate(flops=flops, bytes_accessed=2**20, transcendentals=0)
    return pl.pallas_call(
        kernel,
        out_shape=outs,
        in_specs=[SMEM] * scalars + [VMEM] * (len(args) - scalars),
        out_specs=jax.tree.map(lambda _: VMEM, outs),
        scratch_shapes=[pltpu.VMEM(shape, dtype) for shape, dtype in scratch],
        compiler_params=pltpu.CompilerParams(vmem_limit_bytes=mib * 2**20),
        cost_estimate=cost,
    )(*args)


def pack_weights(core_ref, q_ref, k_ref, v_ref, row_ref, out_ref):
    part = q_ref.shape[0]
    width, kv = q_ref.shape[1], k_ref.shape[1]
    spans = ((0, q_ref), (width, k_ref), (width + kv, v_ref))

    @pl.when(core_ref[0] == 0)
    def _():
        for j in range(N):
            for start, ref in spans:
                out_ref[j, :, start : start + ref.shape[1]] = ref[:HALF]

    @pl.when(core_ref[0] != 0)
    def _():
        for j in range(N):
            for start, ref in spans:
                out_ref[j, : part - HALF, start : start + ref.shape[1]] = ref[HALF:]
            out_ref[j, part - HALF :] = row_ref[...]


def dot(a, b, da, db):
    return lax.dot_general(a, b, (((da,), (db,)), ((), ())), preferred_element_type=F32)


def turned_rows(block, cos, sin, back):
    half = HEAD_DIM // 2
    top, low = block[:half], block[half:]
    if back:
        return [top * cos + low * sin, low * cos - top * sin]
    return [top * cos - low * sin, low * cos + top * sin]


def project_tokens(core_ref, x_ref, own_ref, other_ref, cos_ref, sin_ref, w_ref, rows_ref, q_ref, kv_ref, n_ref, scale_ref):
    part = w_ref.shape[0] // N
    width = x_ref.shape[1]
    lanes = w_ref.shape[1]
    kv = (lanes - width) // 2

    def assemble(low, high):
        small = jnp.zeros((16, lanes), F32)
        for j in range(N):
            w_ref[part * j : part * j + HALF] = low[j]
            w_ref[part * j + HALF : part * (j + 1)] = high[j, : part - HALF]
            small = small + high[j, part - HALF :].astype(F32)
        rows_ref[...] = small

    @pl.when(core_ref[0] == 0)
    def _():
        assemble(own_ref, other_ref)

    @pl.when(core_ref[0] != 0)
    def _():
        assemble(other_ref, own_ref)

    x = x_ref[...].astype(F32)
    scale = lax.rsqrt(jnp.mean(x * x, axis=-1, keepdims=True) + EPS)
    scale_ref[...] = scale
    normed = (x * scale * rows_ref[0:1, :width]).astype(BF)
    n_ref[...] = normed
    raw = dot(normed, w_ref[...], 1, 0) + rows_ref[1:2, :]
    kv_ref[:, kv:] = raw[:, width + kv :].astype(BF)
    turned = raw[:, : width + kv].T
    cos, sin = cos_ref[...], sin_ref[...]
    for h in range(width // HEAD_DIM):
        block = turned[h * HEAD_DIM : (h + 1) * HEAD_DIM]
        q_ref[h * HEAD_DIM : (h + 1) * HEAD_DIM] = jnp.concatenate(
            turned_rows(block, cos, sin, False)
        ).astype(BF)
    keys = []
    for h in range(width // HEAD_DIM, (width + kv) // HEAD_DIM):
        keys += turned_rows(turned[h * HEAD_DIM : (h + 1) * HEAD_DIM], cos, sin, False)
    kv_ref[:, :kv] = jnp.concatenate(keys).T.astype(BF)


CHUNK = 256


def heads_side_by_side(ref, first, ratio):
    return jnp.concatenate(
        [ref[(first + i) * HEAD_DIM : (first + i + 1) * HEAD_DIM] for i in range(ratio)], axis=1
    )


def mask_bias(start, group, key_ref, own_ref, rows, ratio):
    key = start + lax.broadcasted_iota(jnp.int32, (CHUNK, rows), 0)
    query = group * rows + lax.broadcasted_iota(jnp.int32, (CHUNK, rows), 1)
    allowed = (key <= query) & (key_ref[start : start + CHUNK] == own_ref[...])
    bias = jnp.where(allowed, 0.0, MASKED_SCORE)
    return jnp.concatenate([bias] * ratio, axis=1)


def attend_kernel(group_ref, q_ref, kv_ref, key_ref, own_ref, out_ref, log_ref, score_ref):
    rows = q_ref.shape[1]
    length = kv_ref.shape[0]
    kv = kv_ref.shape[1] // 2
    ratio = q_ref.shape[0] // kv
    starts = range(0, length, CHUNK)
    for head in range(KV_HEADS):
        queries = heads_side_by_side(q_ref, head * ratio, ratio) * BF(HEAD_DIM**-0.5)
        span = slice(head * HEAD_DIM, (head + 1) * HEAD_DIM)
        top = jnp.full((1, ratio * rows), MASKED_SCORE, F32)
        for start in starts:
            scores = dot(kv_ref[start : start + CHUNK, span], queries, 1, 0)
            scores = scores + mask_bias(start, group_ref[0], key_ref, own_ref, rows, ratio)
            score_ref[start : start + CHUNK] = scores
            top = jnp.maximum(top, jnp.max(scores, axis=0, keepdims=True))
        total = jnp.zeros_like(top)
        mixed = jnp.zeros((HEAD_DIM, ratio * rows), F32)
        for start in starts:
            weights = jnp.exp(score_ref[start : start + CHUNK] - top)
            total = total + jnp.sum(weights, axis=0, keepdims=True)
            values = kv_ref[start : start + CHUNK, kv:][:, span]
            mixed = mixed + dot(values, weights.astype(BF), 0, 0)
        log_ref[head : head + 1] = top + jnp.log(total)
        mixed = (mixed / total).astype(BF)
        for i in range(ratio):
            at_head = (head * ratio + i) * HEAD_DIM
            out_ref[at_head : at_head + HEAD_DIM] = mixed[:, i * rows : (i + 1) * rows]


def attend_back_kernel(group_ref, q_ref, kv_ref, key_ref, own_ref, grad_ref, log_ref, cos_ref, sin_ref, gq_ref, gkv_ref, prob_ref, diff_ref):
    rows = q_ref.shape[1]
    length = kv_ref.shape[0]
    kv = kv_ref.shape[1] // 2
    ratio = q_ref.shape[0] // kv
    starts = range(0, length, CHUNK)
    cos, sin = cos_ref[...], sin_ref[...]
    grads_k, grads_v = [[], []], [[], []]
    for head in range(KV_HEADS):
        queries = heads_side_by_side(q_ref, head * ratio, ratio) * BF(HEAD_DIM**-0.5)
        grads = heads_side_by_side(grad_ref, head * ratio, ratio)
        span = slice(head * HEAD_DIM, (head + 1) * HEAD_DIM)
        log = log_ref[head : head + 1]
        inner = jnp.zeros((1, ratio * rows), F32)
        for start in starts:
            scores = dot(kv_ref[start : start + CHUNK, span], queries, 1, 0)
            scores = scores + mask_bias(start, group_ref[0], key_ref, own_ref, rows, ratio)
            probs = jnp.exp(scores - log)
            prob_ref[start : start + CHUNK] = probs
            diff = dot(kv_ref[start : start + CHUNK, kv:][:, span], grads, 1, 0)
            diff_ref[start : start + CHUNK] = diff
            inner = inner + jnp.sum(probs * diff, axis=0, keepdims=True)
        grad_q = jnp.zeros((HEAD_DIM, ratio * rows), F32)
        for start in starts:
            probs = prob_ref[start : start + CHUNK]
            grad_s = (probs * (diff_ref[start : start + CHUNK] - inner)).astype(BF)
            grads_k[head].append(dot(grad_s, queries, 1, 1))
            grads_v[head].append(dot(probs.astype(BF), grads, 1, 1))
            grad_q = grad_q + dot(kv_ref[start : start + CHUNK, span], grad_s, 0, 0)
        grad_q = grad_q * HEAD_DIM**-0.5
        blocks = []
        for i in range(ratio):
            blocks += turned_rows(grad_q[:, i * rows : (i + 1) * rows], cos, sin, True)
        lanes = ratio * HEAD_DIM
        gq_ref[:, head * lanes : (head + 1) * lanes] = jnp.concatenate(blocks).T.astype(BF)
    for i, start in enumerate(starts):
        parts = [grads_k[0][i], grads_k[1][i], grads_v[0][i], grads_v[1][i]]
        gkv_ref[start : start + CHUNK] = jnp.concatenate(parts, axis=1).astype(BF)


def tail_kernel(core_ref, arrived_ref, gq_ref, w_ref, x_ref, scale_ref, rows_ref, n_ref, mid_ref, cos_ref, sin_ref, in_ref, keep_ref, send_ref, g_ref, share_ref):
    rows, width = x_ref.shape
    lanes = w_ref.shape[1]
    kv = (lanes - width) // 2
    part = width // N
    total = arrived_ref[0].astype(F32)
    for j in range(1, N):
        total = total + arrived_ref[j].astype(F32)
    turned = total[:, :kv].T
    keys = []
    for h in range(KV_HEADS):
        block = turned[h * HEAD_DIM : (h + 1) * HEAD_DIM]
        keys += turned_rows(block, cos_ref[...], sin_ref[...], True)
    g_ref[:, :width] = gq_ref[...]
    g_ref[:, width : width + kv] = jnp.concatenate(keys).T.astype(BF)
    g_ref[:, width + kv :] = total[:, kv:].astype(BF)
    grads = g_ref[...]
    first = dot(grads, w_ref[...], 1, 1)
    scale = scale_ref[...]
    normalized = x_ref[...].astype(F32) * scale
    scaled = first * rows_ref[0:1, :width]
    mean = jnp.mean(scaled * normalized, axis=-1, keepdims=True)
    in_ref[...] = mid_ref[...] + scale * (scaled - normalized * mean)
    gain = jnp.sum(first * normalized, axis=0, keepdims=True)
    share_ref[...] = dot(n_ref[...], grads, 0, 0)
    bias = jnp.sum(grads.astype(F32), axis=0, keepdims=True)
    gain = jnp.concatenate([gain, jnp.zeros((1, lanes - width), F32)], axis=1)
    small = jnp.concatenate([bias, gain, jnp.zeros((14, lanes), F32)])

    def write(low, high):
        for j in range(N):
            low[j] = share_ref[part * j : part * j + HALF].astype(low.dtype)
            high[j, : part - HALF] = share_ref[part * j + HALF : part * (j + 1)].astype(high.dtype)
            high[j, part - HALF :] = small.astype(high.dtype)

    @pl.when(core_ref[0] == 0)
    def _():
        write(keep_ref, send_ref)

    @pl.when(core_ref[0] != 0)
    def _():
        write(send_ref, keep_ref)


def swap_pairs():
    pairs = []
    for group in range(N):
        for spread in range(N):
            for c in range(2):
                pairs.append(((group * N + spread) * 2 + c, (spread * N + group) * 2 + c))
    return pairs


def shape(dtype, *dims):
    return jax.ShapeDtypeStruct(dims, dtype)


def local(
    hidden_in,
    segment_ids,
    attn_gain,
    w_query,
    b_query,
    w_key,
    b_key,
    w_value,
    b_value,
    w_out,
    ffn_gain,
    w_gate,
    w_up,
    w_down,
    cotangent,
):
    g = lax.axis_index(GROUP)
    c = lax.axis_index("c")
    rows, width = hidden_in.shape[1:]
    part = w_query.shape[1]
    units = w_down.shape[1]
    kv = w_key.shape[2]
    heads = width // HEAD_DIM

    lanes = width + 2 * kv
    k16 = kv // N
    core, group = c.reshape(1), g.reshape(1)

    def spread_out(vector):
        place = jnp.arange(N * vector.shape[0]) // vector.shape[0] == g
        return jnp.where(place, jnp.tile(vector, N), BF(0))

    bias = [spread_out(b[0]) for b in (b_query, b_key, b_value)]
    blank = jnp.zeros((2 * kv,), BF)
    small = jnp.stack(
        [
            jnp.concatenate([spread_out(attn_gain[0]), blank]),
            jnp.concatenate(bias),
            jnp.concatenate([spread_out(ffn_gain[0]), blank]),
        ]
    )
    small = jnp.pad(small, ((0, 13), (0, 0)))
    halves = call(
        pack_weights, shape(BF, N, HALF, lanes), core, w_query[0], w_key[0], w_value[0], small, scalars=1
    )
    own_half = exchange(halves, GROUP)
    own_half, w_gate, w_up, w_out, cotangent = lax.optimization_barrier(
        (own_half, w_gate, w_up, w_out, cotangent)
    )
    other_half = shift(own_half, "c", 1, 2)

    segments = segment_ids[0]
    length = segments.shape[0]
    own_segments = lax.dynamic_slice_in_dim(segments, g * rows, rows, 0)
    query_index = g * rows + jnp.arange(rows, dtype=jnp.int32)
    earlier = jnp.sum((segments[None, :] < own_segments[:, None]).astype(jnp.int32), axis=-1)
    positions = query_index - earlier
    half = HEAD_DIM // 2
    frequency = THETA ** (-(2.0 * jnp.arange(half, dtype=F32)) / HEAD_DIM)
    angles = positions.astype(F32)[None, :] * frequency[:, None]
    cosine, sine = jnp.cos(angles), jnp.sin(angles)
    key_segments, own_segments = segments[:, None], own_segments[None]

    w_qkv, gains, queries, own_kv, normed, first_scale = call(
        project_tokens,
        (
            shape(BF, width, lanes),
            shape(F32, 16, lanes),
            shape(BF, width, rows),
            shape(BF, rows, 2 * kv),
            shape(BF, rows, width),
            shape(F32, rows, 1),
        ),
        core,
        hidden_in[0],
        own_half,
        other_half,
        cosine,
        sine,
        scalars=1,
    )
    second_gain = gains[2, :width]
    all_kv = to_all(own_kv, GROUP).reshape(length, 2 * kv)

    mine = jnp.where(c == 0, w_gate[0], w_up[0])
    mine = call(pack_units, shape(BF, N, part, PAD), mine)
    out_weight = lax.all_gather(w_out[0], GROUP, axis=0, tiled=True)
    all_kv, mine, cotangent = lax.optimization_barrier((all_kv, mine, cotangent))
    group_down = lax.all_gather(cotangent[0], GROUP, axis=0, tiled=True)
    pair = core_pair(exchange(mine, GROUP), c)
    w_gu = jnp.concatenate([half_side.reshape(width, PAD) for half_side in pair], axis=1)
    w_dn = jnp.pad(w_down[0], ((0, PAD - units), (0, 0)))

    wide = heads // KV_HEADS * rows
    attended, logsum = call(
        attend_kernel,
        (shape(BF, width, rows), shape(F32, KV_HEADS, wide)),
        group,
        queries,
        all_kv,
        key_segments,
        own_segments,
        scalars=1,
        scratch=[((length, wide), F32)],
    )
    stream = hidden_in[0].astype(F32)
    middle = stream + outer(attended, out_weight)

    second_normed, second_scale = norm_forward(middle, second_gain)
    group_second = to_all(second_normed.astype(BF), GROUP).reshape(length, width)
    both = mm(group_second, w_gu)
    gate, up = both[:, :PAD], both[:, PAD:]
    sigmoid = jax.nn.sigmoid(gate)
    hidden = (gate * sigmoid * up).astype(BF)
    grad_hidden = mm_t(group_down, w_dn)
    grad_gate = (grad_hidden * up * sigmoid * (1.0 + gate * (1.0 - sigmoid))).astype(BF)
    grad_up = (grad_hidden * gate * sigmoid).astype(BF)
    grad_both = jnp.concatenate([grad_gate, grad_up], axis=1)
    second_terms = mm_t(grad_both, w_gu).astype(BF)
    grad_second = sum_at(second_terms.reshape(N, rows, width), GROUP)
    down_terms = mm(hidden, w_dn).astype(BF)
    grad_second, down_terms = lax.optimization_barrier((grad_second, down_terms))
    layer_out = middle + sum_at(down_terms.reshape(N, rows, width), GROUP)
    hidden_out = layer_out.astype(BF)[None]

    shares = [outer(group_second, grad).astype(BF) for grad in (grad_gate, grad_up)]
    shares = jnp.stack([share.reshape(N, part, PAD) for share in shares], axis=1)
    shares = shares.reshape(2 * N * part, PAD)
    share = lax.psum_scatter(shares, REPLICA, scatter_dimension=0, tiled=True)
    share = lax.ppermute(share, AXES, swap_pairs())
    columns = lax.all_gather(share, REPLICA, axis=0, tiled=True).reshape(N, 2, part, PAD)
    grads = (shape(F32, part, N * units),) * 2
    grad_w_gate, grad_w_up = [grad[None] for grad in call(unpack_units, grads, columns)]
    down_share = outer(hidden, group_down)
    down_rows = PAD // 2
    down_share = core_sum(down_share[:down_rows], down_share[down_rows:], c)

    stream_grad = cotangent[0].astype(F32)
    term, gain_second = norm_backward(middle, second_scale, second_gain, grad_second)
    grad_middle = stream_grad + term
    attn_grad = grad_middle.astype(BF)
    grad_attended = mm_t(out_weight, attn_grad).astype(BF)
    small = jnp.pad(gain_second.reshape(N, 1, part), ((0, 0), (0, 15), (0, width - part)))
    grad_out = mm(attended, attn_grad).reshape(N, part, width)
    grad_out = jnp.concatenate([grad_out, small], axis=1)
    out_share = sum_at(core_sum(grad_out[:, :HALF], grad_out[:, HALF:], c), GROUP).astype(BF)
    share = jnp.concatenate([down_share, out_share]).reshape(N, -1, width)
    share = to_all(sum_at(share, SPREAD).astype(BF), SPREAD).reshape(-1, width)
    low, high = core_pair(share, c)
    grad_w_down = jnp.concatenate([low[:down_rows], high[:down_rows]])[None, :units].astype(F32)
    grad_out = jnp.concatenate([low[down_rows:], high[down_rows:]]).astype(F32)
    grad_q, grad_kv = call(
        attend_back_kernel,
        (shape(BF, rows, width), shape(BF, length, 2 * kv)),
        group,
        queries,
        all_kv,
        key_segments,
        own_segments,
        grad_attended,
        logsum,
        cosine,
        sine,
        scalars=1,
        scratch=[((length, wide), F32)] * 2,
    )
    arrived = exchange(grad_kv.reshape(N, rows, 2 * kv), GROUP)

    grad_in, keep, send = call(
        tail_kernel,
        (shape(F32, rows, width), shape(F32, N, HALF, lanes), shape(BF, N, HALF, lanes)),
        core,
        arrived,
        grad_q,
        w_qkv,
        hidden_in[0],
        first_scale,
        gains,
        normed,
        grad_middle,
        cosine,
        sine,
        scalars=1,
        scratch=[((rows, lanes), BF), ((width, lanes), F32)],
    )
    grad_in = grad_in[None]
    share = (keep + shift(send, "c", 1, 2).astype(F32)).astype(BF)
    share = sum_at(share, GROUP).astype(BF)
    share = sum_at(share.reshape(N, HALF // N, -1), SPREAD).astype(BF)
    share = to_all(share, SPREAD).reshape(HALF, -1)
    whole = jnp.concatenate(core_pair(share, c)).astype(F32)
    bias, gain = whole[part], whole[part + 1]

    def own_part(vector, start, size):
        return lax.dynamic_slice_in_dim(vector, start + g * size, size, 0)[None]

    return (
        hidden_out,
        grad_in,
        own_part(gain, 0, part),
        whole[None, :part, :width],
        own_part(bias, 0, part),
        whole[None, :part, width : width + kv],
        own_part(bias, width, k16),
        whole[None, :part, width + kv :],
        own_part(bias, width + kv, k16),
        grad_out[None, :part],
        grad_out[part, :part][None],
        grad_w_gate,
        grad_w_up,
        grad_w_down,
    )


def solution(mesh):
    split = Mesh(mesh.devices.reshape(SIZES), AXES)
    tokens = P(REPLICA, GROUP, None)
    vector = P(None, GROUP)
    matrix = P(None, GROUP, None)
    weights = (vector, matrix, vector, matrix, vector, matrix, vector, matrix, vector)
    return jax.shard_map(
        local,
        mesh=split,
        in_specs=(tokens, P(REPLICA, None)) + weights + (matrix,) * 3 + (tokens,),
        out_specs=(tokens, tokens) + weights + (matrix,) * 3,
        check_vma=False,
    )
```

time: 478 us -> 401 us (0.84)
  the two profiles are of different devices: /device:TPU:3 before, /device:TPU:1 now
where the time goes in v3:
time: 401 us; the launch traced here: 399 us
  waiting for transfers between devices  172 us (43%)
  starting transfers between devices  88.2 us (22%)
  matrix products  36.7 us (9%)
  other arithmetic  27 us (7%)
  blocking collectives  22.3 us (6%)
  local copies, waits for them, and re-layouts  21 us (5%)
  Pallas kernels  18.2 us (5%)
  between operations  14.3 us (4%)
    all_to_all x12, waiting for transfers between devices, exchange(): return lax.all_to_all(blocks, axis, 0, 0, tiled=True)  128 us
    all_to_all x12, starting transfers between devices, exchange(): return lax.all_to_all(blocks, axis, 0, 0, tiled=True)  58.1 us
    all_gather x1, waiting for transfers between devices, local(): out_weight = lax.all_gather(w_out[0], GROUP, axis=0, tiled=True)  27.7 us
    ppermute x7, starting transfers between devices, shift(): lax.ppermute(array, axis, [(i, (i + by) % size) for i in range(size)])  26.9 us
    all_to_all x1, blocking collectives, exchange(): return lax.all_to_all(blocks, axis, 0, 0, tiled=True)  22.3 us
    pallas_call x7, Pallas kernels, call(): pl.pallas_call(kernel, out_shape=outs, in_specs=[SMEM] * scalars + [VMEM]...  18.2 us
    dot_general x3, matrix products, mm(): return jnp.dot(a, b, preferred_element_type=F32)  12.6 us
    dot_general x4, matrix products, outer(): lax.dot_general(a, b, (((0,), (0,)), ((), ())), preferred_element_type=F32)  12.3 us
  transfers between devices with their start and end apart: 24, of which 15 were waited for; matrix products, arithmetic and copies ran while one was open for 15% of the time, Pallas kernels for 4%

profile of v3, /device:TPU:1, one launch (start us, length us, event | category | flops | bytes accessed | tf_op | source)
XLA Modules:
  0.0 399.4 jit_solution(18205644803097450771)
XLA Ops:
  13.7 22.3 %all_to_all.65.own_ref = bf16[8,64,1152]{2,1,0:T(8,128)(2,1)S(1)} all-to-all(bf16[8,64,1152]{2,1,0:T(8,128)(2,1)S(1)} %shard_map.254), channel_id=1, replica_groups=mesh['y'=4,'xl'=2,'xh'=2,'z'=4,'c'=2] {'y','xl'}, dimensions={0} | all-to-all | bytes 2359296 | tf_op jit(solution)/shard_map/all_to_all | solution.py:31
  36.0 1.8 collective-permute-start
  38.2 2.1 collective-permute-done.other_ref
  41.2 1.3 copy-done.2
  43.3 3.5 all-to-all-start.1
  46.9 1.4 select_bitcast_fusion.w_ref
  48.3 1.3 shard_map.256
  49.6 13.0 %all-to-all-done.1 = bf16[8,128,256]{2,1,0:T(8,128)(2,1)S(1)} async-done(((bf16[8,128,256]{2,1,0:T(8,128)(2,1)}), bf16[8,128,256]{2,1,0:T(8,128)(2,1)S(1)}, u32[]{:S(2)}, u32[]{:S(2)}) %all-to-all-start.1) | async-done | bytes 524320 | tf_op jit(solution)/shard_map/all_to_all | solution.py:31
  62.6 4.3 %all-to-all-start.3 = ((bf16[8,112,640]{2,1,0:T(8,128)(2,1)}), bf16[8,112,640]{2,1,0:T(8,128)(2,1)}, u32[]{:S(2)}, u32[]{:S(2)}) async-start(bf16[8,112,640]{2,1,0:T(8,128)(2,1)} %shard_map.256), calls=%async_computation.3 | async-start | bytes 2293760 | tf_op jit(solution)/shard_map/all_to_all | solution.py:31
  67.2 3.2 shard_map.257
  70.4 27.7 %all-gather.8.cloned.1.call-done = bf16[1,896,896]{2,1,0:T(8,128)(2,1)} async-done(((bf16[1,112,896]{2,1,0:T(8,128)(2,1)}), bf16[1,896,896]{2,1,0:T(8,128)(2,1)}) %all-gather.8.cloned.1.call-update) | async-done | bytes 1605648 | tf_op jit(solution)/shard_map/all_gather | solution.py:418
  98.0 2.0 multiply_reduce_fusion.2
  100.2 1.5 broadcast_in_dim.62
  101.6 4.3 %all-to-all-start.2 = ((bf16[8,128,896]{2,1,0:T(8,128)(2,1)}), bf16[8,128,896]{2,1,0:T(8,128)(2,1)}, u32[]{:S(2)}, u32[]{:S(2)}) async-start(bf16[8,128,896]{2,1,0:T(8,128)(2,1)} %broadcast_in_dim.62), calls=%async_computation.2 | async-start | bytes 3670016 | tf_op jit(solution)/shard_map/all_to_all | solution.py:31
  106.0 1.3 collective-permute-start.1
  107.3 2.6 collective-permute-done.1
  109.9 2.9 broadcast_select_fusion.1
  112.8 33.2 %all-to-all-done.2 = bf16[8,128,896]{2,1,0:T(8,128)(2,1)} async-done(((bf16[8,128,896]{2,1,0:T(8,128)(2,1)}), bf16[8,128,896]{2,1,0:T(8,128)(2,1)}, u32[]{:S(2)}, u32[]{:S(2)}) %all-to-all-start.2) | async-done | bytes 1835040 | tf_op jit(solution)/shard_map/all_to_all | solution.py:31
  146.1 7.4 %fusion.15 = f32[1024,1280]{0,1:T(8,128)} fusion(bf16[1024,896]{1,0:T(8,128)(2,1)} %bitcast.19, bf16[896,640]{1,0:T(8,128)(2,1)} %bitcast.103, bf16[896,640]{1,0:T(8,128)(2,1)} %bitcast.101), kind=kOutput, calls=%fused_computation.30 | convolution fusion | flops 2353397760 | bytes 9371648 | tf_op jit(solution)/shard_map/dot_general | solution.py:60
  153.5 11.4 %all-gather.10.cloned.1.call-done = bf16[1,1024,896]{2,1,0:T(8,128)(2,1)} async-done(((bf16[1,128,896]{2,1,0:T(8,128)(2,1)}), bf16[1,1024,896]{2,1,0:T(8,128)(2,1)}) %all-gather.10.cloned.1.call-update) | async-done | bytes 1835024 | tf_op jit(solution)/shard_map/all_gather | solution.py:420
  164.9 7.1 %multiply_convert_fusion.2 = (bf16[1024,640]{0,1:T(8,128)(2,1)S(1)}, bf16[1024,640]{0,1:T(8,128)(2,1)S(1)}, bf16[1024,640]{0,1:T(8,128)(2,1)}) fusion(f32[1024,1280]{0,1:T(8,128)} %fusion.15, bf16[608,896]{1,0:T(8,128)(2,1)} %bitcast.117, bf16[1,1024,896]{2,1,0:T(8,128)(2,1)} %all-gather.10.cloned.1.call-done), kind=kOutput, calls=%fused_computation.8 | convolution fusion | flops 1184890880 | bytes 12099584 | tf_op jit(solution)/shard_map/dot_general | solution.py:64
  172.0 4.1 %fusion.8 = bf16[1024,896]{1,0:T(8,128)(2,1)} fusion(bf16[1024,640]{0,1:T(8,128)(2,1)S(1)} %get-tuple-element.67, bf16[1024,640]{0,1:T(8,128)(2,1)S(1)} %get-tuple-element.66, bf16[896,640]{1,0:T(8,128)(2,1)S(1)} %bitcast.104, bf16[896,640]{1,0:T(8,128)(2,1)S(1)} %bitcast.102), kind=kOutput, calls=%fused_computation.22 | convolution fusion | flops 2359558144 | bytes 6750208 | tf_op jit(solution)/shard_map/dot_general | solution.py:64
  176.2 4.3 %all-to-all-start.4 = ((bf16[8,128,896]{2,1,0:T(8,128)(2,1)}), bf16[8,128,896]{2,1,0:T(8,128)(2,1)}, u32[]{:S(2)}, u32[]{:S(2)}) async-start(bf16[8,128,896]{2,1,0:T(8,128)(2,1)} %bitcast.100), calls=%async_computation.4 | async-start | bytes 3670016 | tf_op jit(solution)/shard_map/all_to_all | solution.py:31
  180.5 4.6 %convolution_convert_fusion = bf16[1024,896]{1,0:T(8,128)(2,1)} fusion(bf16[1024,640]{0,1:T(8,128)(2,1)} %get-tuple-element.68, bf16[608,896]{1,0:T(8,128)(2,1)} %bitcast.118), kind=kOutput, calls=%fused_computation.23 | convolution fusion | flops 1175322624 | bytes 4235264 | tf_op jit(solution)/shard_map/dot_general | solution.py:60
  185.1 19.2 %all-to-all-done.4 = bf16[8,128,896]{2,1,0:T(8,128)(2,1)} async-done(((bf16[8,128,896]{2,1,0:T(8,128)(2,1)}), bf16[8,128,896]{2,1,0:T(8,128)(2,1)}, u32[]{:S(2)}, u32[]{:S(2)}) %all-to-all-start.4) | async-done | bytes 1835040 | tf_op jit(solution)/shard_map/all_to_all | solution.py:31
  204.3 1.8 convert_reduce_fusion.1
  206.1 4.3 %all-to-all-start.5 = ((bf16[8,128,896]{2,1,0:T(8,128)(2,1)}), bf16[8,128,896]{2,1,0:T(8,128)(2,1)}, u32[]{:S(2)}, u32[]{:S(2)}) async-start(bf16[8,128,896]{2,1,0:T(8,128)(2,1)} %bitcast.99), calls=%async_computation.5 | async-start | bytes 3670016 | tf_op jit(solution)/shard_map/all_to_all | solution.py:31
  210.8 3.6 convolution_convert_fusion.2
  214.4 3.2 convolution_convert_fusion.1
  217.8 1.6 copy.41
  219.8 13.6 %all-to-all-done.5 = bf16[8,128,896]{2,1,0:T(8,128)(2,1)} async-done(((bf16[8,128,896]{2,1,0:T(8,128)(2,1)}), bf16[8,128,896]{2,1,0:T(8,128)(2,1)}, u32[]{:S(2)}, u32[]{:S(2)}) %all-to-all-start.5) | async-done | bytes 1835040 | tf_op jit(solution)/shard_map/all_to_all | solution.py:31
  233.4 2.0 convert_reduce_fusion
  235.4 1.9 convert_add_fusion
  237.9 6.6 %shard_map.258 = (bf16[128,896]{1,0:T(8,128)(2,1)S(1)}, bf16[1024,256]{1,0:T(8,128)(2,1)}) custom-call(s32[1]{0:T(128)} %bitcast.1.group_ref, bf16[896,128]{1,0:T(8,128)(2,1)S(1)} %get-tuple-element.40.q_ref, bf16[1024,256]{1,0:T(8,128)(2,1)S(1)} %bitcast.88, s32[1024,1]{1,0:T(8,128)S(1)} %copy.37.key_ref, ...), custom_call_target="tpu_custom_call" | custom-call | bytes 1048576 | tf_op jit(solution)/shard_map/pallas_call | solution.py:104
  244.5 4.0 all-to-all-start.6
  249.0 1.3 select_convert_fusion
  250.9 1.7 collective-permute-start.5
  252.7 4.2 %all-to-all-done.6.arrived_ref = bf16[8,128,256]{2,1,0:T(8,128)(2,1)S(1)} async-done(((bf16[8,128,256]{2,1,0:T(8,128)(2,1)}), bf16[8,128,256]{2,1,0:T(8,128)(2,1)S(1)}, u32[]{:S(2)}, u32[]{:S(2)}) %all-to-all-start.6) | async-done | bytes 524320 | tf_op jit(solution)/shard_map/all_to_all | solution.py:31
  256.9 1.6 copy-done.3
  258.5 3.6 shard_map.259
  262.1 5.0 %collective-permute-start.2 = (bf16[8,64,1152]{2,1,0:T(8,128)(2,1)}, bf16[8,64,1152]{2,1,0:T(8,128)(2,1)}, u32[]{:S(2)}, u32[]{:S(2)}) collective-permute-start(bf16[8,64,1152]{2,1,0:T(8,128)(2,1)} %get-tuple-element.61), channel_id=1, source_target_pairs={{0,1},{1,0},{2,3},{3,2},{4,5},{5,4},{6,7},{7,6},{8,9},{9,8},{10,11... | collective-permute-start | bytes 3538952 | tf_op jit(solution)/shard_map/ppermute | solution.py:27
  267.1 2.3 add_convert_fusion.1
  269.5 3.6 all-to-all-start.10
  273.0 3.6 fusion.4
  276.6 2.6 add_convert_fusion
  279.2 9.7 %all-to-all-done.10 = bf16[8,64,896]{2,1,0:T(8,128)(2,1)S(1)} async-done(((bf16[8,64,896]{2,1,0:T(8,128)(2,1)}), bf16[8,64,896]{2,1,0:T(8,128)(2,1)S(1)}, u32[]{:S(2)}, u32[]{:S(2)}) %all-to-all-start.10) | async-done | bytes 917536 | tf_op jit(solution)/shard_map/all_to_all | solution.py:31
  289.9 3.6 all-to-all-start.7
  295.3 2.8 collective-permute-start.7
  298.1 2.0 add_convert_fusion.2
  300.1 1.4 reduce_sum.110
  301.5 8.3 %all-to-all-done.7 = bf16[8,64,1152]{2,1,0:T(8,128)(2,1)S(1)} async-done(((bf16[8,64,1152]{2,1,0:T(8,128)(2,1)}), bf16[8,64,1152]{2,1,0:T(8,128)(2,1)S(1)}, u32[]{:S(2)}, u32[]{:S(2)}) %all-to-all-start.7) | async-done | bytes 1179680 | tf_op jit(solution)/shard_map/all_to_all | solution.py:31
  310.6 15.8 %all-to-all-start.8 = ((bf16[8,8,1152]{2,1,0:T(8,128)(2,1)}), bf16[8,8,1152]{2,1,0:T(8,128)(2,1)S(1)}, u32[]{:S(2)}, u32[]{:S(2)}) async-start(bf16[8,8,1152]{2,1,0:T(8,128)(2,1)} %bitcast.28), calls=%async_computation.8 | async-start | bytes 294912 | tf_op jit(solution)/shard_map/all_to_all | solution.py:31
  327.4 6.3 %all-to-all-done.8 = bf16[8,8,1152]{2,1,0:T(8,128)(2,1)S(1)} async-done(((bf16[8,8,1152]{2,1,0:T(8,128)(2,1)}), bf16[8,8,1152]{2,1,0:T(8,128)(2,1)S(1)}, u32[]{:S(2)}, u32[]{:S(2)}) %all-to-all-start.8) | async-done | bytes 147488 | tf_op jit(solution)/shard_map/all_to_all | solution.py:31
  333.7 3.5 all-to-all-start.11
  337.3 9.8 %all-to-all-done.11 = bf16[8,48,896]{2,1,0:T(8,128)(2,1)S(1)} async-done(((bf16[8,48,896]{2,1,0:T(8,128)(2,1)}), bf16[8,48,896]{2,1,0:T(8,128)(2,1)S(1)}, u32[]{:S(2)}, u32[]{:S(2)}) %all-to-all-start.11) | async-done | bytes 688160 | tf_op jit(solution)/shard_map/all_to_all | solution.py:31
  347.8 3.4 all-to-all-start.9
  351.3 8.1 %all-to-all-done.9 = bf16[8,8,1152]{2,1,0:T(8,128)(2,1)S(1)} async-done(((bf16[8,8,1152]{2,1,0:T(8,128)(2,1)}), bf16[8,8,1152]{2,1,0:T(8,128)(2,1)S(1)}, u32[]{:S(2)}, u32[]{:S(2)}) %all-to-all-start.9) | async-done | bytes 147488 | tf_op jit(solution)/shard_map/all_to_all | solution.py:31
  360.2 3.5 all-to-all-start.12
  363.8 7.5 %collective-permute-start.3 = (bf16[64,1152]{1,0:T(8,128)(2,1)S(1)}, bf16[64,1152]{1,0:T(8,128)(2,1)S(1)}, u32[]{:S(2)}, u32[]{:S(2)}) collective-permute-start(bf16[64,1152]{1,0:T(8,128)(2,1)S(1)} %bitcast.107), channel_id=1, source_target_pairs={{0,1},{1,0},{2,3},{3,2},{4,5},{5,4},{6,7},{7,6},{8,9},{9,8},{10,11... | collective-permute-start | bytes 442376 | tf_op jit(solution)/shard_map/ppermute | solution.py:27
  371.3 2.3 all-to-all-done.12
  373.6 8.6 %collective-permute-start.6 = (bf16[384,896]{1,0:T(8,128)(2,1)S(1)}, bf16[384,896]{1,0:T(8,128)(2,1)S(1)}, u32[]{:S(2)}, u32[]{:S(2)}) collective-permute-start(bf16[384,896]{1,0:T(8,128)(2,1)S(1)} %bitcast.98), channel_id=1, source_target_pairs={{0,1},{1,0},{2,3},{3,2},{4,5},{5,4},{6,7},{7,6},{8,9},{9,8},{10,11... | collective-permute-start | bytes 2064392 | tf_op jit(solution)/shard_map/ppermute | solution.py:27
  386.4 1.5 fusion.23
  388.7 1.6 copy-done
  390.3 2.5 shard_map.260
  (117 shorter events, 22.7 us)
Async XLA Ops:
  7.2 90.9 %all-gather.8.cloned.1.call-start = ((), (), s32[]{:S(2)}) async-start(), calls=%async_computation.16 | async-start | bytes 1806336 | tf_op jit(solution)/shard_map/all_gather | solution.py:418
  11.1 0.9 copy-start.4
  12.1 0.7 copy-start.5
  12.8 0.7 copy-start.6
  13.6 24.3 %copy-start.16 = (s32[1,1024]{1,0:T(1,128)S(1)}, s32[1,1024]{1,0:T(1,128)}, u32[]{:S(2)}) copy-start(s32[1,1024]{1,0:T(1,128)} %param.16) | copy-start | bytes 12292
  13.6 26.8 %copy-start.1 = (bf16[1,128,896]{2,1,0:T(8,128)(2,1)S(1)}, bf16[1,128,896]{2,1,0:T(8,128)(2,1)}, u32[]{:S(2)}) copy-start(bf16[1,128,896]{2,1,0:T(8,128)(2,1)} %param.15) | copy-start | bytes 688132
  36.0 4.3 %collective-permute-start = (bf16[8,64,1152]{2,1,0:T(8,128)(2,1)S(1)}, bf16[8,64,1152]{2,1,0:T(8,128)(2,1)S(1)}, u32[]{:S(2)}, u32[]{:S(2)}) collective-permute-start(bf16[8,64,1152]{2,1,0:T(8,128)(2,1)S(1)} %all_to_all.65.own_ref), channel_id=1, source_target_pairs={{0,1},{1,0},{2,3},{3,2},{4,5},{5,4},{6,7},{7,6},{8,9},{9,8},{10,11... | collective-permute-start | bytes 3538952 | tf_op jit(solution)/shard_map/ppermute | solution.py:27
  41.2 1.3 copy-start.2
  42.5 4.4 %copy-start.15 = (bf16[1,112,4864]{2,1,0:T(8,128)(2,1)S(1)}, bf16[1,112,4864]{2,1,0:T(8,128)(2,1)}, u32[]{:S(2)}) copy-start(bf16[1,112,4864]{2,1,0:T(8,128)(2,1)} %param.26) | copy-start | bytes 3268612
  43.3 19.3 %all-to-all-start.1 = ((bf16[8,128,256]{2,1,0:T(8,128)(2,1)}), bf16[8,128,256]{2,1,0:T(8,128)(2,1)S(1)}, u32[]{:S(2)}, u32[]{:S(2)}) async-start(bf16[8,128,256]{2,1,0:T(8,128)(2,1)} %broadcast_in_dim.61), calls=%async_computation.1 | async-start | bytes 1048576 | tf_op jit(solution)/shard_map/all_to_all | solution.py:31
  46.8 118.1 %all-gather.10.cloned.1.call-start = ((), (), s32[]{:S(2)}) async-start(), calls=%async_computation.17 | async-start | bytes 2064384 | tf_op jit(solution)/shard_map/all_gather | solution.py:420
  62.6 37.5 %all-to-all-start.3 = ((bf16[8,112,640]{2,1,0:T(8,128)(2,1)}), bf16[8,112,640]{2,1,0:T(8,128)(2,1)}, u32[]{:S(2)}, u32[]{:S(2)}) async-start(bf16[8,112,640]{2,1,0:T(8,128)(2,1)} %shard_map.256), calls=%async_computation.3 | async-start | bytes 2293760 | tf_op jit(solution)/shard_map/all_to_all | solution.py:31
  101.6 44.4 %all-to-all-start.2 = ((bf16[8,128,896]{2,1,0:T(8,128)(2,1)}), bf16[8,128,896]{2,1,0:T(8,128)(2,1)}, u32[]{:S(2)}, u32[]{:S(2)}) async-start(bf16[8,128,896]{2,1,0:T(8,128)(2,1)} %broadcast_in_dim.62), calls=%async_computation.2 | async-start | bytes 3670016 | tf_op jit(solution)/shard_map/all_to_all | solution.py:31
  106.0 4.0 collective-permute-start.1
  164.9 7.1 %copy-start.13 = (bf16[8,112,640]{2,1,0:T(8,128)(2,1)S(1)}, bf16[8,112,640]{2,1,0:T(8,128)(2,1)}, u32[]{:S(2)}) copy-start(bf16[8,112,640]{2,1,0:T(8,128)(2,1)} %get-tuple-element.69) | copy-start | bytes 3440644
  164.9 7.1 %copy-start.14 = (bf16[8,112,640]{2,1,0:T(8,128)(2,1)S(1)}, bf16[8,112,640]{2,1,0:T(8,128)(2,1)}, u32[]{:S(2)}) copy-start(bf16[8,112,640]{2,1,0:T(8,128)(2,1)} %get-tuple-element.70) | copy-start | bytes 3440644
  172.0 4.1 %copy-start.17 = (bf16[1024,640]{0,1:T(8,128)(2,1)}, bf16[1024,640]{0,1:T(8,128)(2,1)S(1)}, u32[]{:S(2)}) copy-start(bf16[1024,640]{0,1:T(8,128)(2,1)S(1)} %get-tuple-element.67) | copy-start | bytes 3932164
  172.0 4.1 %copy-start.19 = (bf16[1024,640]{0,1:T(8,128)(2,1)}, bf16[1024,640]{0,1:T(8,128)(2,1)S(1)}, u32[]{:S(2)}) copy-start(bf16[1024,640]{0,1:T(8,128)(2,1)S(1)} %get-tuple-element.66) | copy-start | bytes 3932164
  176.2 28.2 %all-to-all-start.4 = ((bf16[8,128,896]{2,1,0:T(8,128)(2,1)}), bf16[8,128,896]{2,1,0:T(8,128)(2,1)}, u32[]{:S(2)}, u32[]{:S(2)}) async-start(bf16[8,128,896]{2,1,0:T(8,128)(2,1)} %bitcast.100), calls=%async_computation.4 | async-start | bytes 3670016 | tf_op jit(solution)/shard_map/all_to_all | solution.py:31
  206.1 27.3 %all-to-all-start.5 = ((bf16[8,128,896]{2,1,0:T(8,128)(2,1)}), bf16[8,128,896]{2,1,0:T(8,128)(2,1)}, u32[]{:S(2)}, u32[]{:S(2)}) async-start(bf16[8,128,896]{2,1,0:T(8,128)(2,1)} %bitcast.99), calls=%async_computation.5 | async-start | bytes 3670016 | tf_op jit(solution)/shard_map/all_to_all | solution.py:31
  210.5 84.8 %reduce-scatter.2.cloned.1.call-start = ((), (), s32[]{:S(2)}) async-start(), calls=%async_computation.14 | async-start | bytes 2437120 | tf_op jit(solution)/shard_map/reduce_scatter | solution.py:460
  210.7 3.6 copy-start.18
  233.4 3.9 copy-start.9
  244.5 12.4 %all-to-all-start.6 = ((bf16[8,128,256]{2,1,0:T(8,128)(2,1)}), bf16[8,128,256]{2,1,0:T(8,128)(2,1)S(1)}, u32[]{:S(2)}, u32[]{:S(2)}) async-start(bf16[8,128,256]{2,1,0:T(8,128)(2,1)} %bitcast.26), calls=%async_computation.6 | async-start | bytes 1048576 | tf_op jit(solution)/shard_map/all_to_all | solution.py:31
  249.0 1.9 copy-start.7
  250.9 16.2 %collective-permute-start.5 = (bf16[8,64,896]{2,1,0:T(8,128)(2,1)}, bf16[8,64,896]{2,1,0:T(8,128)(2,1)}, u32[]{:S(2)}, u32[]{:S(2)}) collective-permute-start(bf16[8,64,896]{2,1,0:T(8,128)(2,1)} %select_convert_fusion), channel_id=1, source_target_pairs={{0,1},{1,0},{2,3},{3,2},{4,5},{5,4},{6,7},{7,6},{8,9},{9,8},{10,11... | collective-permute-start | bytes 2752520 | tf_op jit(solution)/shard_map/ppermute | solution.py:27
  256.9 1.6 copy-start.3
  258.5 8.6 %copy-start.8 = (f32[896,896]{1,0:T(8,128)S(1)}, f32[896,896]{1,0:T(8,128)}, u32[]{:S(2)}) copy-start(f32[896,896]{1,0:T(8,128)} %copy-done.7) | copy-start | bytes 9633796
  262.1 14.5 %collective-permute-start.2 = (bf16[8,64,1152]{2,1,0:T(8,128)(2,1)}, bf16[8,64,1152]{2,1,0:T(8,128)(2,1)}, u32[]{:S(2)}, u32[]{:S(2)}) collective-permute-start(bf16[8,64,1152]{2,1,0:T(8,128)(2,1)} %get-tuple-element.61), channel_id=1, source_target_pairs={{0,1},{1,0},{2,3},{3,2},{4,5},{5,4},{6,7},{7,6},{8,9},{9,8},{10,11... | collective-permute-start | bytes 3538952 | tf_op jit(solution)/shard_map/ppermute | solution.py:27
  269.5 19.5 %all-to-all-start.10 = ((bf16[8,64,896]{2,1,0:T(8,128)(2,1)}), bf16[8,64,896]{2,1,0:T(8,128)(2,1)S(1)}, u32[]{:S(2)}, u32[]{:S(2)}) async-start(bf16[8,64,896]{2,1,0:T(8,128)(2,1)} %add_convert_fusion.1), calls=%async_computation.10 | async-start | bytes 1835008 | tf_op jit(solution)/shard_map/all_to_all | solution.py:31
  273.0 3.6 copy-start.11
  289.0 0.9 copy-start.10
  289.9 19.9 %all-to-all-start.7 = ((bf16[8,64,1152]{2,1,0:T(8,128)(2,1)}), bf16[8,64,1152]{2,1,0:T(8,128)(2,1)S(1)}, u32[]{:S(2)}, u32[]{:S(2)}) async-start(bf16[8,64,1152]{2,1,0:T(8,128)(2,1)} %add_convert_fusion), calls=%async_computation.7 | async-start | bytes 2359296 | tf_op jit(solution)/shard_map/all_to_all | solution.py:31
  293.5 95.2 %all-gather.6.cloned.1.call-start = ((), (), s32[]{:S(2)}) async-start(), calls=%async_computation.15 | async-start | bytes 2437120 | tf_op jit(solution)/shard_map/all_gather | solution.py:462
  294.4 3.7 collective-permute-start.4
  295.3 2.8 collective-permute-start.7
  300.1 26.3 %copy-start.12 = (bf16[320,896]{1,0:T(8,128)(2,1)S(1)}, bf16[320,896]{1,0:T(8,128)(2,1)}, u32[]{:S(2)}) copy-start(bf16[320,896]{1,0:T(8,128)(2,1)} %add_convert_fusion.2) | copy-start | bytes 1720324
  310.6 23.1 %all-to-all-start.8 = ((bf16[8,8,1152]{2,1,0:T(8,128)(2,1)}), bf16[8,8,1152]{2,1,0:T(8,128)(2,1)S(1)}, u32[]{:S(2)}, u32[]{:S(2)}) async-start(bf16[8,8,1152]{2,1,0:T(8,128)(2,1)} %bitcast.28), calls=%async_computation.8 | async-start | bytes 294912 | tf_op jit(solution)/shard_map/all_to_all | solution.py:31
  333.7 13.4 %all-to-all-start.11 = ((bf16[8,48,896]{2,1,0:T(8,128)(2,1)}), bf16[8,48,896]{2,1,0:T(8,128)(2,1)S(1)}, u32[]{:S(2)}, u32[]{:S(2)}) async-start(bf16[8,48,896]{2,1,0:T(8,128)(2,1)} %bitcast.34), calls=%async_computation.11 | async-start | bytes 1376256 | tf_op jit(solution)/shard_map/all_to_all | solution.py:31
  347.8 11.6 %all-to-all-start.9 = ((bf16[8,8,1152]{2,1,0:T(8,128)(2,1)}), bf16[8,8,1152]{2,1,0:T(8,128)(2,1)S(1)}, u32[]{:S(2)}, u32[]{:S(2)}) async-start(bf16[8,8,1152]{2,1,0:T(8,128)(2,1)} %broadcast_in_dim.65), calls=%async_computation.9 | async-start | bytes 294912 | tf_op jit(solution)/shard_map/all_to_all | solution.py:31
  360.2 13.4 %all-to-all-start.12 = ((bf16[8,48,896]{2,1,0:T(8,128)(2,1)}), bf16[8,48,896]{2,1,0:T(8,128)(2,1)S(1)}, u32[]{:S(2)}, u32[]{:S(2)}) async-start(bf16[8,48,896]{2,1,0:T(8,128)(2,1)} %broadcast_in_dim.69), calls=%async_computation.12 | async-start | bytes 1376256 | tf_op jit(solution)/shard_map/all_to_all | solution.py:31
  363.8 18.5 %collective-permute-start.3 = (bf16[64,1152]{1,0:T(8,128)(2,1)S(1)}, bf16[64,1152]{1,0:T(8,128)(2,1)S(1)}, u32[]{:S(2)}, u32[]{:S(2)}) collective-permute-start(bf16[64,1152]{1,0:T(8,128)(2,1)S(1)} %bitcast.107), channel_id=1, source_target_pairs={{0,1},{1,0},{2,3},{3,2},{4,5},{5,4},{6,7},{7,6},{8,9},{9,8},{10,11... | collective-permute-start | bytes 442376 | tf_op jit(solution)/shard_map/ppermute | solution.py:27
  373.6 11.9 %collective-permute-start.6 = (bf16[384,896]{1,0:T(8,128)(2,1)S(1)}, bf16[384,896]{1,0:T(8,128)(2,1)S(1)}, u32[]{:S(2)}, u32[]{:S(2)}) collective-permute-start(bf16[384,896]{1,0:T(8,128)(2,1)S(1)} %bitcast.98), channel_id=1, source_target_pairs={{0,1},{1,0},{2,3},{3,2},{4,5},{5,4},{6,7},{7,6},{8,9},{9,8},{10,11... | collective-permute-start | bytes 2064392 | tf_op jit(solution)/shard_map/ppermute | solution.py:27
  388.7 1.6 copy-start
Sparse Core Ops, SparseCore 0:
  36.2 61.8 all-gather.7
  99.7 65.2 all-gather.9
  219.5 74.8 reduce-scatter.1
  298.2 71.9 all-gather.5
